TPU v7x, 128 devices: a whole 4x4x4 slice. The times are simulated.
128 devices in a mesh: prefix: 16 (over z, x_hi, core), resp: 8 (over y, x_lo).
Axes of the slice: x: 4 (x_hi: 2, x_lo: 2; x = x_hi * 2 + x_lo), y: 4, z: 4, core: 2. Of those that a mesh axis runs over, the one named last changes fastest.
Arguments:
- resp_query: bfloat16 [16, 1024, 5120], P('prefix', 'resp'), may hold values from -120 to 120
- resp_keys: bfloat16 [16, 1024, 1024], P('prefix', 'resp'), may hold values from -5 to 5
- resp_values: bfloat16 [16, 1024, 1024], P('prefix', 'resp'), may hold values from -5 to 5
- resp_out: bfloat16 [16, 1024, 5120], P('prefix', 'resp'), may hold values from -6 to 6
- resp_grad: bfloat16 [16, 1024, 5120], P('prefix', 'resp'), may hold values from -24 to 24
- prompt_keys: bfloat16 [1024, 1024], P('prefix'), may hold values from -4 to 4
- prompt_values: bfloat16 [1024, 1024], P('prefix'), may hold values from -5 to 5
- resp_lengths: int32 [16], P('prefix'), may hold values from 1 to 1024, 10240 in all
Outputs:
- grad_query: bfloat16 [16, 1024, 5120], P('prefix', 'resp')
- grad_resp_keys: bfloat16 [16, 1024, 1024], P('prefix', 'resp')
- grad_resp_values: bfloat16 [16, 1024, 1024], P('prefix', 'resp')
- grad_prompt_keys: bfloat16 [1024, 1024], P(('prefix', 'resp'))
- grad_prompt_values: bfloat16 [1024, 1024], P(('prefix', 'resp'))
Inputs may be any that keep to these rules, and one draw needn't show every extreme that they name: `resp_lengths`: one response fills all 1024 slots.
All inputs are finite; a program needn't handle non-finite values. No bound on the sum of `resp_lengths` on one device may be relied on, other than what follows from the above.
Results may differ from a plain program's by a relative error of at most 0.019.
Values may be sent and summed in bfloat16 or wider, within the bound.
No kernel may reach another device: no remote copies, remote signals or barrier semaphores. Data moves between devices by JAX's collectives and lax.ppermute only.
A program may use at most 192 MiB of HBM per device.

v0:
```python
import jax
import jax.numpy as jnp
from jax import lax
from jax.sharding import PartitionSpec as P

HEADS = 40
KV_HEADS = 8
HEAD_DIM = 128
KB = 512


def head_scores(query_heads, key_block, score_scale):
    kv_heads = query_heads.shape[1]
    key_heads = key_block.reshape(key_block.shape[0], kv_heads, -1)
    return (
        jnp.einsum("bkgd,nkd->bkgn", query_heads, key_heads, preferred_element_type=jnp.float32)
        * score_scale
    )


def causal_limit(scores, slot_index, first_key):
    key_slot = first_key + jnp.arange(scores.shape[-1], dtype=jnp.int32)
    allowed = key_slot[None, :] <= slot_index[:, None]
    return jnp.where(allowed[:, None, None, :], scores, -jnp.inf)


def gather_stats(running, query_heads, key_blocks, slot_index, causal, reach, score_scale):
    block_rows = key_blocks.shape[1]

    def advance(carried, inputs):
        block_index, key_block = inputs

        def compute(current):
            running_max, running_sum = current
            scores = head_scores(query_heads, key_block, score_scale)
            if causal:
                scores = causal_limit(scores, slot_index, block_index * block_rows)
            new_max = jnp.maximum(running_max, jnp.max(scores, axis=-1))
            running_sum = running_sum * jnp.exp(running_max - new_max) + jnp.sum(
                jnp.exp(scores - new_max[..., None]), axis=-1
            )
            return (new_max, running_sum)

        return (
            lax.cond(block_index * block_rows <= reach, compute, lambda current: current, carried),
            None,
        )

    indices = jnp.arange(key_blocks.shape[0], dtype=jnp.int32)
    running, unused = lax.scan(advance, running, (indices, key_blocks))
    return running


def gather_grads(
    query_grad,
    query_heads,
    grad_heads,
    grad_dot,
    log_total,
    live_weight,
    key_blocks,
    value_blocks,
    slot_index,
    causal,
    reach,
    score_scale,
):
    block_rows = key_blocks.shape[1]
    kv_width = key_blocks.shape[2]
    kv_heads = query_heads.shape[1]

    def advance(carried, inputs):
        block_index, key_block, value_block = inputs

        def compute(current):
            scores = head_scores(query_heads, key_block, score_scale)
            if causal:
                scores = causal_limit(scores, slot_index, block_index * block_rows)
            weights = jnp.exp(scores - log_total[..., None]) * live_weight[:, None, None, None]
            weights_low = weights.astype(jnp.bfloat16)
            value_heads = value_block.reshape(block_rows, kv_heads, -1)
            weight_grad = jnp.einsum(
                "bkgd,nkd->bkgn", grad_heads, value_heads, preferred_element_type=jnp.float32
            )
            score_grad = (score_scale * weights * (weight_grad - grad_dot[..., None])).astype(
                jnp.bfloat16
            )
            key_heads = key_block.reshape(block_rows, kv_heads, -1)
            current = current + jnp.einsum(
                "bkgn,nkd->bkgd", score_grad, key_heads, preferred_element_type=jnp.float32
            )
            key_grad = jnp.einsum(
                "bkgn,bkgd->nkd", score_grad, query_heads, preferred_element_type=jnp.float32
            ).reshape(block_rows, kv_width)
            value_grad = jnp.einsum(
                "bkgn,bkgd->nkd", weights_low, grad_heads, preferred_element_type=jnp.float32
            ).reshape(block_rows, kv_width)
            return (current, (key_grad, value_grad))

        def skipped(current):
            blank = jnp.zeros((block_rows, kv_width), jnp.float32)
            return (current, (blank, blank))

        return lax.cond(block_index * block_rows <= reach, compute, skipped, carried)

    indices = jnp.arange(key_blocks.shape[0], dtype=jnp.int32)
    query_grad, grads_out = lax.scan(advance, query_grad, (indices, key_blocks, value_blocks))
    return (query_grad, grads_out[0].reshape(-1, kv_width), grads_out[1].reshape(-1, kv_width))


def reduce_prompt(key_grad, value_grad):
    return (
        lax.psum_scatter(key_grad, ("prefix", "resp"), scatter_dimension=0, tiled=True),
        lax.psum_scatter(value_grad, ("prefix", "resp"), scatter_dimension=0, tiled=True),
    )


def local(
    resp_query,
    resp_keys,
    resp_values,
    resp_out,
    resp_grad,
    prompt_keys,
    prompt_values,
    resp_lengths,
):
    row_count = resp_query.shape[1]
    kv_width = resp_keys.shape[2]
    group_size = HEADS // KV_HEADS
    score_scale = HEAD_DIM ** (-0.5)
    query_heads = resp_query.reshape(row_count, KV_HEADS, group_size, HEAD_DIM)
    grad_heads = resp_grad.reshape(row_count, KV_HEADS, group_size, HEAD_DIM)
    out_heads = resp_out.reshape(row_count, KV_HEADS, group_size, HEAD_DIM)
    grad_dot = jnp.einsum(
        "bkgd,bkgd->bkg", grad_heads, out_heads, preferred_element_type=jnp.float32
    )
    first_slot = lax.axis_index("resp") * row_count
    slot_index = first_slot + jnp.arange(row_count, dtype=jnp.int32)
    length = resp_lengths[0]
    live_weight = (slot_index < length).astype(jnp.float32)
    has_work = first_slot < length
    prompt_reach = jnp.where(has_work, jnp.int32(2**30), jnp.int32(-1))
    causal_reach = jnp.where(
        has_work, jnp.minimum(first_slot + row_count, length) - 1, jnp.int32(-1)
    )
    prompt_rows, prompt_vals = (
        lax.all_gather(prompt_keys, "prefix", axis=0, tiled=True),
        lax.all_gather(prompt_values, "prefix", axis=0, tiled=True),
    )
    own_keys, own_values = (
        lax.all_gather(resp_keys, "resp", axis=1, tiled=True),
        lax.all_gather(resp_values, "resp", axis=1, tiled=True),
    )
    prompt_key_blocks = prompt_rows.reshape(-1, KB, kv_width)
    prompt_value_blocks = prompt_vals.reshape(-1, KB, kv_width)
    resp_key_blocks = own_keys.reshape(-1, KB, kv_width)
    resp_value_blocks = own_values.reshape(-1, KB, kv_width)
    start_max = jnp.full((row_count, KV_HEADS, group_size), -jnp.inf, jnp.float32)
    start_sum = jnp.zeros((row_count, KV_HEADS, group_size), jnp.float32)
    running = gather_stats(
        (start_max, start_sum),
        query_heads,
        prompt_key_blocks,
        slot_index,
        False,
        prompt_reach,
        score_scale,
    )
    running = gather_stats(
        running, query_heads, resp_key_blocks, slot_index, True, causal_reach, score_scale
    )
    log_total = running[0] + jnp.log(running[1])
    blank_grad = jnp.zeros((row_count, KV_HEADS, group_size, HEAD_DIM), jnp.float32)
    query_grad = blank_grad
    query_grad, key_grad, value_grad = gather_grads(
        query_grad,
        query_heads,
        grad_heads,
        grad_dot,
        log_total,
        live_weight,
        prompt_key_blocks,
        prompt_value_blocks,
        slot_index,
        False,
        prompt_reach,
        score_scale,
    )
    query_grad, prompt_summed = (query_grad, reduce_prompt(key_grad, value_grad))
    response_query_grad = query_grad
    response_query_grad, key_grad, value_grad = gather_grads(
        response_query_grad,
        query_heads,
        grad_heads,
        grad_dot,
        log_total,
        live_weight,
        resp_key_blocks,
        resp_value_blocks,
        slot_index,
        True,
        causal_reach,
        score_scale,
    )
    grad_query = response_query_grad.reshape(1, row_count, HEADS * HEAD_DIM).astype(jnp.bfloat16)
    grad_resp_keys = (
        lax.psum_scatter(key_grad, "resp", scatter_dimension=0, tiled=True)
        .reshape(1, row_count, kv_width)
        .astype(jnp.bfloat16)
    )
    grad_resp_values = (
        lax.psum_scatter(value_grad, "resp", scatter_dimension=0, tiled=True)
        .reshape(1, row_count, kv_width)
        .astype(jnp.bfloat16)
    )
    return (
        grad_query,
        grad_resp_keys,
        grad_resp_values,
        prompt_summed[0].astype(jnp.bfloat16),
        prompt_summed[1].astype(jnp.bfloat16),
    )


def solution(mesh):
    return jax.shard_map(
        local,
        mesh=mesh,
        in_specs=(
            P("prefix", "resp", None),
            P("prefix", "resp", None),
            P("prefix", "resp", None),
            P("prefix", "resp", None),
            P("prefix", "resp", None),
            P("prefix", None),
            P("prefix", None),
            P("prefix"),
        ),
        out_specs=(
            P("prefix", "resp", None),
            P("prefix", "resp", None),
            P("prefix", "resp", None),
            P(("prefix", "resp"), None),
            P(("prefix", "resp"), None),
        ),
        check_vma=False,
    )
```

profile of v0, /device:TPU:0, one launch (start us, length us, event | category | flops | bytes accessed | tf_op | source)
XLA Modules:
  0.0 1738.1 jit_solution(5352911762353296694)
XLA Ops:
  20.4 43.9 %all-gather.7.cloned.1.call-done = bf16[1,1024,1024]{2,1,0:T(8,128)(2,1)} async-done(((bf16[1,128,1024]{2,1,0:T(8,128)(2,1)}), bf16[1,1024,1024]{2,1,0:T(8,128)(2,1)}) %all-gather.7.cloned.1.call-update) | async-done | bytes 2097168 | tf_op jit(solution)/shard_map/all_gather | solution.py:152
  68.2 45.4 %all-gather.5.cloned.1.call-done = bf16[1024,1024]{1,0:T(8,128)(2,1)} async-done(((bf16[64,1024]{1,0:T(8,128)(2,1)}), bf16[1024,1024]{1,0:T(8,128)(2,1)}) %all-gather.5.cloned.1.call-update) | async-done | bytes 2097168 | tf_op jit(solution)/shard_map/all_gather | solution.py:148
  117.6 44.9 %all-gather.9.cloned.1.call-done = bf16[1024,1024]{1,0:T(8,128)(2,1)} async-done(((bf16[64,1024]{1,0:T(8,128)(2,1)}), bf16[1024,1024]{1,0:T(8,128)(2,1)}) %all-gather.9.cloned.1.call-update) | async-done | bytes 2097168 | tf_op jit(solution)/shard_map/all_gather | solution.py:149
  166.5 12.6 while.62
  167.9 4.9 conditional.12
  174.2 4.9 conditional.12
  179.1 9.3 while.63
  180.5 6.5 conditional.13
  195.5 55.3 %while.64 = (s32[]{:T(128)}, f32[128,8,5,128]{3,0,2,1:T(8,128)}, f32[2,512,1024]{2,1,0:T(8,128)}, f32[2,512,1024]{2,1,0:T(8,128)}, s32[2]{0:T(128)S(1)}, /*index...) while((s32[]{:T(128)}, f32[128,8,5,128]{3,0,2,1:T(8,128)}, ...), condition=%wide.region_15.16_spmd.clone, body=%wide.region_12.15_spmd.clone.sunk | while | flops 3384934912 | bytes 117504408 | solution.py:107
  197.5 16.1 conditional.14
  218.4 4.8 constant_dynamic-update-slice_fusion.6
  225.2 16.0 conditional.14
  246.0 4.8 constant_dynamic-update-slice_fusion.6
  250.9 4.2 copy.89
  260.3 50.5 %while.65 = (s32[]{:T(128)}, f32[128,8,5,128]{3,0,2,1:T(8,128)}, f32[2,512,1024]{2,1,0:T(8,128)}, f32[2,512,1024]{2,1,0:T(8,128)}, s32[2]{0:T(128)S(1)}, /*index...) while((s32[]{:T(128)}, f32[128,8,5,128]{3,0,2,1:T(8,128)}, ...), condition=%wide.region_19.20_spmd.clone.clone, body=%wide.region_16.19_spmd.clone.clone.sunk | while | flops 3390243840 | bytes 143920624 | solution.py:107
  262.2 25.5 %conditional.15 = (f32[128,8,5,128]{3,0,2,1:T(8,128)}, f32[1,512,1024]{1,2,0:T(8,128)}, f32[1,512,1024]{1,2,0:T(8,128)}) conditional(s32[]{:T(128)} %convert_element_type.110, f32[128,8,5,128]{3,0,2,1:T(8,128)} %get-tuple-element.1238, (s32[]{:T(128)}, s32[128]{0:T(128)S(1)}, bf16[2,512,1024]{1,2,0:T(8,128)(2,1)}, s32[]{:T(128)}, ...), branch_computations={%region_17.17_spmd, %region_18.18_spmd} | conditional | flops 3390243328 | bytes 127141576 | solution.py:104
  263.9 5.6 fusion.36
  270.3 7.0 fusion.23
  283.5 4.2 fusion.28
  306.6 4.1 constant_dynamic-update-slice_fusion.7
  315.8 585.4 %reduce-scatter.9.cloned.1.call-done = f32[8,1024]{1,0:T(8,128)} async-done(((f32[1024,1024]{1,0:T(8,128)}), f32[8,1024]{1,0:T(8,128)}) %reduce-scatter.9.cloned.1.call-update) | async-done | bytes 32784 | tf_op jit(solution)/shard_map/reduce_scatter | solution.py:113
  902.5 86.4 %reduce-scatter.7.cloned.1.call-done = f32[128,1024]{1,0:T(8,128)} async-done(((f32[1024,1024]{1,0:T(8,128)}), f32[128,1024]{1,0:T(8,128)}) %reduce-scatter.7.cloned.1.call-update) | async-done | bytes 524304 | tf_op jit(solution)/shard_map/reduce_scatter | solution.py:213
  990.7 92.0 %reduce-scatter.5.cloned.1.call-done = f32[128,1024]{1,0:T(8,128)} async-done(((f32[1024,1024]{1,0:T(8,128)}), f32[128,1024]{1,0:T(8,128)}) %reduce-scatter.5.cloned.1.call-update) | async-done | bytes 524304 | tf_op jit(solution)/shard_map/reduce_scatter | solution.py:208
  1084.5 645.5 %reduce-scatter.11.cloned.1.call-done = f32[8,1024]{1,0:T(8,128)} async-done(((f32[1024,1024]{1,0:T(8,128)}), f32[8,1024]{1,0:T(8,128)}) %reduce-scatter.11.cloned.1.call-update) | async-done | bytes 32784 | tf_op jit(solution)/shard_map/reduce_scatter | solution.py:114
  (139 shorter events, 140.8 us)
Async XLA Ops:
  7.2 57.1 %all-gather.7.cloned.1.call-start = ((), (), s32[]{:S(2)}) async-start(), calls=%async_computation.5 | async-start | bytes 2359296 | tf_op jit(solution)/shard_map/all_gather | solution.py:152
  7.9 105.7 %all-gather.5.cloned.1.call-start = ((), (), s32[]{:S(2)}) async-start(), calls=%async_computation.4 | async-start | bytes 2228224 | tf_op jit(solution)/shard_map/all_gather | solution.py:148
  8.6 153.9 %all-gather.9.cloned.1.call-start = ((), (), s32[]{:S(2)}) async-start(), calls=%async_computation.6 | async-start | bytes 2228224 | tf_op jit(solution)/shard_map/all_gather | solution.py:149
  9.4 241.5 %all-gather.11.cloned.1.call-start = ((), (), s32[]{:S(2)}) async-start(), calls=%async_computation.7 | async-start | bytes 2359296 | tf_op jit(solution)/shard_map/all_gather | solution.py:153
  10.0 891.2 %reduce-scatter.9.cloned.1.call-start = ((), (), s32[]{:S(2)}) async-start(), calls=%async_computation.10 | async-start | bytes 4227072 | tf_op jit(solution)/shard_map/reduce_scatter | solution.py:113
  199.2 1.6 copy-start.4
  200.8 3.8 copy-start
  207.5 1.8 copy-start.1
  207.5 2.3 copy-start.5
  226.9 1.6 copy-start.4
  228.5 3.8 copy-start
  235.2 1.8 copy-start.1
  235.2 2.3 copy-start.5
  250.9 738.0 %reduce-scatter.7.cloned.1.call-start = ((), (), s32[]{:S(2)}) async-start(), calls=%async_computation.9 | async-start | bytes 4718592 | tf_op jit(solution)/shard_map/reduce_scatter | solution.py:213
  270.2 7.1 copy-start.2
  277.3 6.0 slice-start
  277.3 6.0 slice-start.1
  280.2 3.1 copy-start.3
  280.2 3.1 slice-start.2
  280.2 3.3 copy-start.6
  310.7 772.0 %reduce-scatter.5.cloned.1.call-start = ((), (), s32[]{:S(2)}) async-start(), calls=%async_computation.8 | async-start | bytes 4718592 | tf_op jit(solution)/shard_map/reduce_scatter | solution.py:208
  311.5 1418.4 %reduce-scatter.11.cloned.1.call-start = ((), (), s32[]{:S(2)}) async-start(), calls=%async_computation.11 | async-start | bytes 4227072 | tf_op jit(solution)/shard_map/reduce_scatter | solution.py:114
Sparse Core Ops, SparseCore 0:
  9.6 54.5 all-gather.6
  66.7 46.8 all-gather.4
  116.1 46.3 all-gather.8
  164.0 50.8 all-gather.10
  251.0 650.0 reduce-scatter.8
  903.5 85.3 reduce-scatter.6
  991.4 91.2 reduce-scatter.4
  1085.2 644.7 reduce-scatter.10
where the time goes:
time: 1740 us
  waiting for transfers between devices  1550 us (89%)
  local copies, waits for them, and re-layouts  94.8 us (5%)
  matrix products  55.4 us (3%)
  other arithmetic  17.8 us (1%)
    reduce_scatter x1, waiting for transfers between devices, reduce_prompt(): lax.psum_scatter(value_grad, ('prefix', 'resp'), scatter_dimension=0, til...  645 us
    reduce_scatter x1, waiting for transfers between devices, reduce_prompt(): lax.psum_scatter(key_grad, ('prefix', 'resp'), scatter_dimension=0, tiled...  585 us
    reduce_scatter x1, waiting for transfers between devices, local(): lax.psum_scatter(key_grad, 'resp', scatter_dimension=0, tiled=True)  92 us
    reduce_scatter x1, waiting for transfers between devices, local(): lax.psum_scatter(value_grad, 'resp', scatter_dimension=0, tiled=True)  86.4 us
    all_gather x1, waiting for transfers between devices, local(): lax.all_gather(prompt_keys, 'prefix', axis=0, tiled=True)  45.4 us
    all_gather x1, waiting for transfers between devices, local(): lax.all_gather(prompt_values, 'prefix', axis=0, tiled=True)  44.9 us
    all_gather x1, waiting for transfers between devices, local(): lax.all_gather(resp_keys, 'resp', axis=1, tiled=True)  43.9 us
    dynamic_update_slice x12, local copies, waits for them, and re-layouts, gather_grads(): lax.scan(advance, query_grad, (indices, key_blocks, value_blocks))  37.1 us
  transfers between devices with their start and end apart: 8, of which 7 were waited for; matrix products, arithmetic and copies ran while one was open for 10% of the time, Pallas kernels for 0%

commit v1 on v0

v1 whole, which is shorter than its diff:
```python
import jax
import jax.numpy as jnp
from jax import lax
from jax.experimental import pallas as pl
from jax.experimental.pallas import tpu as pltpu
from jax.sharding import PartitionSpec as P

HEADS = 40
KV_HEADS = 8
GROUP = HEADS // KV_HEADS
HEAD_DIM = 128
SCALE = HEAD_DIM ** (-0.5)
EXP2_SCALE = SCALE * 1.4426950408889634
QW = GROUP * HEAD_DIM
KVD = 3 * HEAD_DIM
SEND_W = 2 * QW + KVD
BACK_W = QW + 2 * HEAD_DIM
TILE = 256
WIDE_TILE = 512
VMEM_LIMIT = 56 * 1024 * 1024

NT = (((1,), (1,)), ((), ()))
NN = (((1,), (0,)), ((), ()))


def dot(a, b, dims):
    return lax.dot_general(a, b, dims, preferred_element_type=jnp.float32)


def pack_kernel(q_ref, g_ref, o_ref, k_ref, v_ref, send_ref):
    send_ref[0, :, 0:HEAD_DIM] = k_ref[...]
    send_ref[0, :, HEAD_DIM : 2 * HEAD_DIM] = v_ref[...]
    for j in range(GROUP):
        cols = slice(j * HEAD_DIM, (j + 1) * HEAD_DIM)
        at = KVD + 2 * j * HEAD_DIM
        send_ref[0, :, at : at + HEAD_DIM] = q_ref[:, cols]
        send_ref[0, :, at + HEAD_DIM : at + 2 * HEAD_DIM] = g_ref[:, cols]
    product = g_ref[...].astype(jnp.float32) * o_ref[...].astype(jnp.float32)
    high = product.astype(jnp.bfloat16)
    low = (product - high.astype(jnp.float32)).astype(jnp.bfloat16)
    row = lax.broadcasted_iota(jnp.int32, (QW, HEAD_DIM), 0) // HEAD_DIM
    lane = lax.broadcasted_iota(jnp.int32, (QW, HEAD_DIM), 1)
    mine = (lane >= 3 * row) & (lane < 3 * row + 3)
    ones = jnp.where(mine, 1.0, 0.0).astype(jnp.bfloat16)
    left = dot(high, ones, NN) + dot(low, ones, NN)
    part = lax.broadcasted_iota(jnp.int32, left.shape, 1) % 3
    first = left.astype(jnp.bfloat16).astype(jnp.float32)
    second = (left - first).astype(jnp.bfloat16).astype(jnp.float32)
    third = left - first - second
    deltas = jnp.where(part == 0, first, jnp.where(part == 1, second, third))
    send_ref[0, :, 2 * HEAD_DIM : KVD] = deltas.astype(jnp.bfloat16)


def pack(q, g, o, k, v):
    rows = q.shape[0]
    wide = pl.BlockSpec((rows, QW), lambda h: (0, h))
    thin = pl.BlockSpec((rows, HEAD_DIM), lambda h: (0, h))
    return pl.pallas_call(
        pack_kernel,
        grid=(KV_HEADS,),
        in_specs=[wide, wide, wide, thin, thin],
        out_specs=pl.BlockSpec((1, rows, SEND_W), lambda h: (h, 0, 0)),
        out_shape=jax.ShapeDtypeStruct((KV_HEADS, rows, SEND_W), jnp.bfloat16),
        name="pack",
    )(q, g, o, k, v)


def unpack_kernel(back_ref, q_ref, k_ref, v_ref):
    q_ref[...] = back_ref[0, :, 0:QW]
    k_ref[...] = back_ref[0, :, QW : QW + HEAD_DIM]
    v_ref[...] = back_ref[0, :, QW + HEAD_DIM :]


def unpack(back):
    rows = back.shape[1]
    wide = pl.BlockSpec((rows, QW), lambda h: (0, h))
    thin = pl.BlockSpec((rows, HEAD_DIM), lambda h: (0, h))
    return pl.pallas_call(
        unpack_kernel,
        grid=(KV_HEADS,),
        in_specs=[pl.BlockSpec((1, rows, BACK_W), lambda h: (h, 0, 0))],
        out_specs=[wide, thin, thin],
        out_shape=[
            jax.ShapeDtypeStruct((rows, KV_HEADS * QW), jnp.bfloat16),
            jax.ShapeDtypeStruct((rows, KV_HEADS * HEAD_DIM), jnp.bfloat16),
            jax.ShapeDtypeStruct((rows, KV_HEADS * HEAD_DIM), jnp.bfloat16),
        ],
        name="unpack",
    )(back)


def attend_kernel(
    len_ref, x_ref, pkv_ref, back_ref, pg_ref, k_all, v_all, k_t, qs, gs, e_all, m_all, l_all, p_s, l_s, dq_t, dk, dv
):
    slots = x_ref.shape[0]
    prompt = pkv_ref.shape[0]
    wide = GROUP * TILE
    parts = prompt // WIDE_TILE
    length = len_ref[0]
    k_all[0:prompt] = pkv_ref[:, 0:HEAD_DIM]
    v_all[0:prompt] = pkv_ref[:, HEAD_DIM:]
    k_all[prompt:] = x_ref[:, 0:HEAD_DIM]
    v_all[prompt:] = x_ref[:, HEAD_DIM : 2 * HEAD_DIM]
    for t in range((prompt + slots) // TILE):
        rows = slice(t * TILE, (t + 1) * TILE)
        k_t[:, rows] = k_all[rows].astype(jnp.float32).T.astype(jnp.bfloat16)
    dk[...] = jnp.zeros_like(dk)
    dv[...] = jnp.zeros_like(dv)
    back_ref[...] = jnp.zeros_like(back_ref)

    seen = lax.broadcasted_iota(jnp.int32, (TILE, TILE), 0) <= lax.broadcasted_iota(
        jnp.int32, (TILE, TILE), 1
    )

    def heads(j):
        return slice(j * TILE, (j + 1) * TILE)

    def select(j, size):
        lane = lax.broadcasted_iota(jnp.int32, (size, HEAD_DIM), 1)
        return jnp.where((lane >= 3 * j) & (lane < 3 * j + 3), -1.0, 0.0).astype(jnp.bfloat16)

    def score_tile(rows, size, index, diagonal):
        for j in range(GROUP):
            s = dot(k_all[rows], qs[heads(j)], NT)
            if diagonal:
                s = jnp.where(seen, s, -jnp.inf)
            top = jnp.max(s, axis=0, keepdims=True)
            e = jnp.exp2((s - top) * EXP2_SCALE)
            m_all[pl.ds(index, 1), heads(j)] = top
            l_all[pl.ds(index, 1), heads(j)] = jnp.sum(e, axis=0, keepdims=True)
            e_all[rows, heads(j)] = e

    def grad_tile(rows, size, index, at):
        for j in range(GROUP):
            shifted = dot(
                jnp.concatenate([v_all[rows], select(j, size)], axis=1), gs[heads(j)], NT
            )
            p = e_all[rows, heads(j)] * m_all[pl.ds(index, 1), heads(j)]
            p_s[at : at + size, heads(j)] = p.astype(jnp.bfloat16)
            l_s[at : at + size, heads(j)] = (p * shifted).astype(jnp.bfloat16)

    def grad_sums(rows, size):
        dv[rows] += dot(p_s[0:size], gs[:, 0:HEAD_DIM], NN)
        dk[rows] += dot(l_s[0:size], qs[...], NN)
        return dot(k_t[:, rows], l_s[0:size], NN)

    def slot_block(i, carry):
        here = pl.ds(pl.multiple_of(i * TILE, TILE), TILE)
        for j in range(GROUP):
            at = KVD + 2 * j * HEAD_DIM
            qs[heads(j)] = x_ref[here, at : at + HEAD_DIM]
            gs[heads(j), 0:HEAD_DIM] = x_ref[here, at + HEAD_DIM : at + 2 * HEAD_DIM]
            gs[heads(j), HEAD_DIM:] = x_ref[here, 2 * HEAD_DIM : KVD]

        def own(t):
            return pl.ds(pl.multiple_of(prompt + t * TILE, TILE), TILE)

        for t in range(parts):
            score_tile(slice(t * WIDE_TILE, (t + 1) * WIDE_TILE), WIDE_TILE, t, False)
        score_tile(own(i), TILE, parts + i, True)

        def score_body(t, carry):
            score_tile(own(t), TILE, parts + t, False)
            return carry

        lax.fori_loop(0, i, score_body, 0)

        tile_index = lax.broadcasted_iota(jnp.int32, m_all.shape, 0)
        tops = jnp.where(tile_index <= parts + i, m_all[...], -jnp.inf)
        sums = jnp.where(tile_index <= parts + i, l_all[...], 0.0)
        weight = jnp.exp2((tops - jnp.max(tops, axis=0, keepdims=True)) * EXP2_SCALE)
        total = jnp.sum(weight * sums, axis=0, keepdims=True)
        slot = lax.broadcasted_iota(jnp.int32, (1, wide), 1) % TILE + i * TILE
        live = jnp.where(slot < length, 1.0, 0.0)
        m_all[...] = weight * (live / total)

        for t in range(parts):
            grad_tile(slice(t * WIDE_TILE, (t + 1) * WIDE_TILE), WIDE_TILE, t, t * WIDE_TILE)
        dq_t[...] = grad_sums(slice(0, prompt), prompt)

        def grad_body(t, carry):
            grad_tile(own(t), TILE, parts + t, 0)
            dq_t[...] += grad_sums(own(t), TILE)
            return carry

        lax.fori_loop(0, i + 1, grad_body, 0)
        for j in range(GROUP):
            back_ref[here, j * HEAD_DIM : (j + 1) * HEAD_DIM] = (
                (dq_t[:, heads(j)] * SCALE).T.astype(jnp.bfloat16)
            )
        return carry

    lax.fori_loop(0, lax.div(length + TILE - 1, TILE), slot_block, 0)
    back_ref[:, QW : QW + HEAD_DIM] = (dk[prompt:] * SCALE).astype(jnp.bfloat16)
    back_ref[:, QW + HEAD_DIM :] = dv[prompt:].astype(jnp.bfloat16)
    pg_ref[:, 0:HEAD_DIM] = (dk[0:prompt] * SCALE).astype(jnp.bfloat16)
    pg_ref[:, HEAD_DIM:] = dv[0:prompt].astype(jnp.bfloat16)


def attend(lengths, x, pkv):
    slots = x.shape[0]
    prompt = pkv.shape[0]
    keys = slots + prompt
    wide = GROUP * TILE
    vmem = pl.BlockSpec(memory_space=pltpu.VMEM)
    return pl.pallas_call(
        attend_kernel,
        in_specs=[pl.BlockSpec(memory_space=pltpu.SMEM), vmem, vmem],
        out_specs=[vmem, vmem],
        out_shape=[
            jax.ShapeDtypeStruct((slots, BACK_W), jnp.bfloat16),
            jax.ShapeDtypeStruct((prompt, 2 * HEAD_DIM), jnp.bfloat16),
        ],
        scratch_shapes=[
            pltpu.VMEM((keys, HEAD_DIM), jnp.bfloat16),
            pltpu.VMEM((keys, HEAD_DIM), jnp.bfloat16),
            pltpu.VMEM((HEAD_DIM, keys), jnp.bfloat16),
            pltpu.VMEM((wide, HEAD_DIM), jnp.bfloat16),
            pltpu.VMEM((wide, 2 * HEAD_DIM), jnp.bfloat16),
            pltpu.VMEM((keys, wide), jnp.float32),
            pltpu.VMEM((8, wide), jnp.float32),
            pltpu.VMEM((8, wide), jnp.float32),
            pltpu.VMEM((prompt, wide), jnp.bfloat16),
            pltpu.VMEM((prompt, wide), jnp.bfloat16),
            pltpu.VMEM((HEAD_DIM, wide), jnp.float32),
            pltpu.VMEM((keys, HEAD_DIM), jnp.float32),
            pltpu.VMEM((keys, HEAD_DIM), jnp.float32),
        ],
        compiler_params=pltpu.CompilerParams(vmem_limit_bytes=VMEM_LIMIT),
        name="attend",
    )(lengths, x, pkv)


def local(
    resp_query,
    resp_keys,
    resp_values,
    resp_out,
    resp_grad,
    prompt_keys,
    prompt_values,
    resp_lengths,
):
    head = lax.axis_index("resp")
    cut = lambda a: lax.dynamic_slice_in_dim(a, head * HEAD_DIM, HEAD_DIM, 1)
    pkv = jnp.concatenate([cut(prompt_keys), cut(prompt_values)], axis=1)
    responses = lax.axis_size("prefix")
    part, width = pkv.shape
    copies = jnp.broadcast_to(pkv[None], (responses, part, width))
    send = pack(resp_query[0], resp_grad[0], resp_out[0], resp_keys[0], resp_values[0])
    x = lax.all_to_all(send, "resp", 0, 0, tiled=True)
    rows = x.shape[1]
    pkv = lax.all_to_all(copies, "prefix", 0, 0, tiled=True).reshape(responses * part, width)
    back, pg = attend(resp_lengths, x.reshape(KV_HEADS * rows, SEND_W), pkv)
    pg = lax.all_to_all(pg.reshape(responses, part, width), "prefix", 0, 0, tiled=True)
    back = lax.all_to_all(back.reshape(KV_HEADS, rows, BACK_W), "resp", 0, 0, tiled=True)
    pg = jnp.sum(pg.astype(jnp.float32), axis=0).astype(jnp.bfloat16)
    own = part // KV_HEADS
    pg = lax.all_to_all(pg.reshape(KV_HEADS, own, width), "resp", 0, 0, tiled=True)
    pg = pg.reshape(KV_HEADS, own, 2, HEAD_DIM).transpose(2, 1, 0, 3).reshape(2, own, KV_HEADS * HEAD_DIM)
    grad_query, grad_keys, grad_values = unpack(back)
    return (grad_query[None], grad_keys[None], grad_values[None], pg[0], pg[1])


def solution(mesh):
    return jax.shard_map(
        local,
        mesh=mesh,
        in_specs=(
            P("prefix", "resp", None),
            P("prefix", "resp", None),
            P("prefix", "resp", None),
            P("prefix", "resp", None),
            P("prefix", "resp", None),
            P("prefix", None),
            P("prefix", None),
            P("prefix"),
        ),
        out_specs=(
            P("prefix", "resp", None),
            P("prefix", "resp", None),
            P("prefix", "resp", None),
            P(("prefix", "resp"), None),
            P(("prefix", "resp"), None),
        ),
        check_vma=False,
    )
```

time: 1740 us -> 164 us (0.09)
  waiting for transfers between devices: 1550 us -> 66.5 us
  local copies, waits for them, and re-layouts: 94.8 us -> 5.97 us
  matrix products: 55.4 us -> 0 us
  Pallas kernels: 0 us -> 38.9 us
  blocking collectives: 0 us -> 33.8 us
  other arithmetic: 17.8 us -> 0.08 us
    reduce_scatter x4 -> x0, waiting for transfers between devices: 1410 us -> none  [the longest x1 645 us: reduce_prompt(): lax.psum_scatter(value_grad, ('prefix', 'resp'), scatter_dimension=0, til...]
    all_gather x4 -> x0, waiting for transfers between devices: 134 us -> none  [the longest x1 45.4 us: local(): lax.all_gather(prompt_keys, 'prefix', axis=0, tiled=True)]
    all_to_all x0 -> x3, waiting for transfers between devices: none -> 66.5 us  [the longest x1 39.9 us: local(): x = lax.all_to_all(send, 'resp', 0, 0, tiled=True)]
    dot_general x18 -> x0, matrix products: 55.4 us -> none  [the longest x3 14.6 us: compute(): jnp.einsum('bkgd,nkd->bkgn', grad_heads, value_heads, preferred_element_t...]
    pallas_call x0 -> x3, Pallas kernels: none -> 38.9 us  [the longest x1 25.7 us: attend(): pl.pallas_call(attend_kernel, in_specs=[pl.BlockSpec(memory_space=pltpu.S...]
    dynamic_update_slice x12 -> x0, local copies, waits for them, and re-layouts: 37.1 us -> none  [gather_grads(): lax.scan(advance, query_grad, (indices, key_blocks, value_blocks))]
    all_to_all x0 -> x2, blocking collectives: none -> 33.8 us  [the longest x1 25 us: local(): lax.all_to_all(pg.reshape(responses, part, width), 'prefix', 0, 0, tiled=...]
    unnamed x8 -> x6, local copies, waits for them, and re-layouts: 24.2 us -> 3.76 us
  transfers between devices with their start and end apart: 8 -> 3, of which waited for: 7 -> 3; matrix products, arithmetic and copies ran while one was open for 10% -> 0% of each run, Pallas kernels for 0% -> 5%
where the time goes in v1:
time: 164 us; the launch traced here: 163 us
  waiting for transfers between devices  66.5 us (41%)
  Pallas kernels  38.9 us (24%)
  blocking collectives  33.8 us (21%)
  starting transfers between devices  16.1 us (10%)
  local copies, waits for them, and re-layouts  5.97 us (4%)
    all_to_all x1, waiting for transfers between devices, local(): x = lax.all_to_all(send, 'resp', 0, 0, tiled=True)  39.9 us
    pallas_call x1, Pallas kernels, attend(): pl.pallas_call(attend_kernel, in_specs=[pl.BlockSpec(memory_space=pltpu.S...  25.7 us
    all_to_all x1, blocking collectives, local(): lax.all_to_all(pg.reshape(responses, part, width), 'prefix', 0, 0, tiled=...  25 us
    all_to_all x1, waiting for transfers between devices, local(): lax.all_to_all(back.reshape(KV_HEADS, rows, BACK_W), 'resp', 0, 0, tiled=...  21.9 us
    all_to_all x1, blocking collectives, local(): lax.all_to_all(pg.reshape(KV_HEADS, own, width), 'resp', 0, 0, tiled=True)  8.81 us
    all_to_all x1, starting transfers between devices, local(): lax.all_to_all(copies, 'prefix', 0, 0, tiled=True)  7.96 us
    pallas_call x1, Pallas kernels, pack(): pl.pallas_call(pack_kernel, grid=(KV_HEADS,), in_specs=[wide, wide, wide,...  7.68 us
    pallas_call x1, Pallas kernels, unpack(): pl.pallas_call(unpack_kernel, grid=(KV_HEADS,), in_specs=[pl.BlockSpec((1...  5.56 us
  transfers between devices with their start and end apart: 3, of which 3 were waited for; matrix products, arithmetic and copies ran while one was open for 0% of the time, Pallas kernels for 5%

profile of v1, /device:TPU:0, one launch (start us, length us, event | category | flops | bytes accessed | tf_op | source)
XLA Modules:
  0.0 162.6 jit_solution(12813316848700641220)
XLA Ops:
  0.6 0.8 constant_dynamic-slice_fusion
  1.4 0.8 broadcast_in_dim.15
  2.2 8.0 %all-to-all-start.1 = ((bf16[16,64,256]{2,1,0:T(8,128)(2,1)}), bf16[16,64,256]{2,1,0:T(8,128)(2,1)S(1)}, u32[]{:S(2)}, u32[]{:S(2)}) async-start(bf16[16,64,256]{2,1,0:T(8,128)(2,1)} %broadcast_in_dim.15), calls=%async_computation.1 | async-start | bytes 1048576 | tf_op jit(solution)/shard_map/all_to_all | solution.py:253
  10.2 7.7 %pack.1 = bf16[8,128,1664]{2,1,0:T(8,128)(2,1)} custom-call(bf16[128,5120]{1,0:T(8,128)(2,1)} %bitcast.23, bf16[128,5120]{1,0:T(8,128)(2,1)} %bitcast.24, bf16[128,5120]{1,0:T(8,128)(2,1)} %bitcast.25, bf16[128,1024]{1,0:T(8,128)(2,1)} %bitcast.27, bf16[128,1024]{1,0:T(8,128)(2,1)} %bitcast.28), custom_call_target="tpu_custom_call" | custom-call | tf_op jit(solution)/shard_map/pack/pallas_call | solution.py:58
  17.9 4.7 %all-to-all-done.1 = bf16[16,64,256]{2,1,0:T(8,128)(2,1)S(1)} async-done(((bf16[16,64,256]{2,1,0:T(8,128)(2,1)}), bf16[16,64,256]{2,1,0:T(8,128)(2,1)S(1)}, u32[]{:S(2)}, u32[]{:S(2)}) %all-to-all-start.1) | async-done | bytes 524320 | tf_op jit(solution)/shard_map/all_to_all | solution.py:253
  22.6 0.0 copy-start.2
  22.6 0.8 copy-done.2
  23.4 4.5 %all-to-all-start = ((bf16[8,128,1664]{2,1,0:T(8,128)(2,1)}), bf16[8,128,1664]{2,1,0:T(8,128)(2,1)S(1)}, u32[]{:S(2)}, u32[]{:S(2)}) async-start(bf16[8,128,1664]{2,1,0:T(8,128)(2,1)} %pack.1), calls=%async_computation | async-start | bytes 6815744 | tf_op jit(solution)/shard_map/all_to_all | solution.py:251
  28.5 39.9 %all-to-all-done = bf16[8,128,1664]{2,1,0:T(8,128)(2,1)S(1)} async-done(((bf16[8,128,1664]{2,1,0:T(8,128)(2,1)}), bf16[8,128,1664]{2,1,0:T(8,128)(2,1)S(1)}, u32[]{:S(2)}, u32[]{:S(2)}) %all-to-all-start) | async-done | bytes 3407904 | tf_op jit(solution)/shard_map/all_to_all | solution.py:251
  68.4 0.0 copy-start
  68.4 1.7 %copy-done = bf16[8,128,1664]{2,1,0:T(8,128)(2,1)} copy-done((bf16[8,128,1664]{2,1,0:T(8,128)(2,1)}, bf16[8,128,1664]{2,1,0:T(8,128)(2,1)S(1)}, u32[]{:S(2)}) %copy-start) | copy-done | bytes 3407896
  70.1 25.7 %attend.1 = (bf16[1024,896]{1,0:T(8,128)(2,1)}, bf16[1024,256]{1,0:T(8,128)(2,1)}) custom-call(s32[1]{0:T(128)S(6)} %copy.13.len_ref, bf16[1024,1664]{1,0:T(8,128)(2,1)} %bitcast.20, bf16[1024,256]{1,0:T(8,128)(2,1)} %bitcast.21), custom_call_target="tpu_custom_call" | custom-call | tf_op jit(solution)/shard_map/attend/pallas_call | solution.py:206
  95.8 25.0 %all_to_all.25 = bf16[16,64,256]{2,1,0:T(8,128)(2,1)S(1)} all-to-all(bf16[16,64,256]{2,1,0:T(8,128)(2,1)} %bitcast.26), channel_id=1, replica_groups=mesh['prefix'=16,'resp'=8] {'prefix'}, dimensions={0} | all-to-all | bytes 1048576 | tf_op jit(solution)/shard_map/all_to_all | solution.py:255
  120.8 0.1 reduce_sum.12
  120.9 8.8 %all_to_all.26 = bf16[8,8,256]{2,1,0:T(8,128)(2,1)S(1)} all-to-all(bf16[8,8,256]{2,1,0:T(8,128)(2,1)S(1)} %bitcast.29), channel_id=1, replica_groups=mesh['prefix'=16,'resp'=8] {'resp'}, dimensions={0} | all-to-all | bytes 65536 | tf_op jit(solution)/shard_map/all_to_all | solution.py:259
  129.7 3.6 %all-to-all-start.2 = ((bf16[8,128,896]{2,1,0:T(8,128)(2,1)}), bf16[8,128,896]{2,1,0:T(8,128)(2,1)S(1)}, u32[]{:S(2)}, u32[]{:S(2)}) async-start(bf16[8,128,896]{2,1,0:T(8,128)(2,1)} %bitcast.22), calls=%async_computation.2 | async-start | bytes 3670016 | tf_op jit(solution)/shard_map/all_to_all | solution.py:256
  133.3 0.6 slice_bitcast_fusion
  133.9 21.9 %all-to-all-done.2.back_ref = bf16[8,128,896]{2,1,0:T(8,128)(2,1)S(1)} async-done(((bf16[8,128,896]{2,1,0:T(8,128)(2,1)}), bf16[8,128,896]{2,1,0:T(8,128)(2,1)S(1)}, u32[]{:S(2)}, u32[]{:S(2)}) %all-to-all-start.2) | async-done | bytes 1835040 | tf_op jit(solution)/shard_map/all_to_all | solution.py:256
  155.8 0.0 copy-start.1
  155.8 1.3 copy-done.1
  157.1 5.6 %unpack.1 = (bf16[128,5120]{1,0:T(8,128)(2,1)}, bf16[128,1024]{1,0:T(8,128)(2,1)}, bf16[128,1024]{1,0:T(8,128)(2,1)}) custom-call(bf16[8,128,896]{2,1,0:T(8,128)(2,1)} %copy-done.1), custom_call_target="tpu_custom_call" | custom-call | tf_op jit(solution)/shard_map/unpack/pallas_call | solution.py:78
  (1 shorter events, 0.0 us)
Async XLA Ops:
  2.2 20.3 %all-to-all-start.1 = ((bf16[16,64,256]{2,1,0:T(8,128)(2,1)}), bf16[16,64,256]{2,1,0:T(8,128)(2,1)S(1)}, u32[]{:S(2)}, u32[]{:S(2)}) async-start(bf16[16,64,256]{2,1,0:T(8,128)(2,1)} %broadcast_in_dim.15), calls=%async_computation.1 | async-start | bytes 1048576 | tf_op jit(solution)/shard_map/all_to_all | solution.py:253
  22.6 0.8 copy-start.2
  23.4 45.0 %all-to-all-start = ((bf16[8,128,1664]{2,1,0:T(8,128)(2,1)}), bf16[8,128,1664]{2,1,0:T(8,128)(2,1)S(1)}, u32[]{:S(2)}, u32[]{:S(2)}) async-start(bf16[8,128,1664]{2,1,0:T(8,128)(2,1)} %pack.1), calls=%async_computation | async-start | bytes 6815744 | tf_op jit(solution)/shard_map/all_to_all | solution.py:251
  68.4 1.7 %copy-start = (bf16[8,128,1664]{2,1,0:T(8,128)(2,1)}, bf16[8,128,1664]{2,1,0:T(8,128)(2,1)S(1)}, u32[]{:S(2)}) copy-start(bf16[8,128,1664]{2,1,0:T(8,128)(2,1)S(1)} %all-to-all-done) | copy-start | bytes 10223620
  129.7 26.1 %all-to-all-start.2 = ((bf16[8,128,896]{2,1,0:T(8,128)(2,1)}), bf16[8,128,896]{2,1,0:T(8,128)(2,1)S(1)}, u32[]{:S(2)}, u32[]{:S(2)}) async-start(bf16[8,128,896]{2,1,0:T(8,128)(2,1)} %bitcast.22), calls=%async_computation.2 | async-start | bytes 3670016 | tf_op jit(solution)/shard_map/all_to_all | solution.py:256
  155.8 1.3 copy-start.1

commit v2 on v1

v2 whole, which is shorter than its diff:
```python
import functools

import jax
import jax.numpy as jnp
from jax import lax
from jax.experimental import pallas as pl
from jax.experimental.pallas import tpu as pltpu
from jax.sharding import PartitionSpec as P

HEADS = 40
KV_HEADS = 8
GROUP = HEADS // KV_HEADS
HEAD_DIM = 128
SCALE = HEAD_DIM ** (-0.5)
EXP2_SCALE = SCALE * 1.4426950408889634
QW = GROUP * HEAD_DIM
KVD = 3 * HEAD_DIM
TILE = 256
WIDE_TILE = 512
PACK_ROWS = 32
CHUNKS = ((0, 1), (2, 3, 4))
GATHER_BITS = (1, 0, 2, 3)

NT = (((1,), (1,)), ((), ()))
NN = (((1,), (0,)), ((), ()))
BF16 = jnp.bfloat16
F32 = jnp.float32
ANY = pl.BlockSpec(memory_space=pl.ANY)
VMEM = pl.BlockSpec(memory_space=pltpu.VMEM)
SMEM = pl.BlockSpec(memory_space=pltpu.SMEM)


def dot(a, b, dims):
    return lax.dot_general(a, b, dims, preferred_element_type=F32)


def params(mib):
    return pltpu.CompilerParams(vmem_limit_bytes=mib * 1024 * 1024)


def times(index, size):
    return pl.multiple_of(index * size, size)


def send_width(chunk):
    return (KVD if chunk == 0 else 0) + 2 * HEAD_DIM * len(CHUNKS[chunk])


def back_width(chunk):
    return (2 * HEAD_DIM if chunk == len(CHUNKS) - 1 else 0) + HEAD_DIM * len(CHUNKS[chunk])


def gather_mask(index):
    return sum(((index >> step) & 1) << bit for step, bit in enumerate(GATHER_BITS))


def pack_kernel(place_ref, q_ref, g_ref, o_ref, k_ref, v_ref, *rest):
    outs, deltas_ref = rest[:-1], rest[-1]
    me = place_ref[1]
    rows = q_ref.shape[0]
    highs, lows = [], []
    for h in range(KV_HEADS):
        wide = slice(h * QW, (h + 1) * QW)
        product = g_ref[:, wide].astype(F32) * o_ref[:, wide].astype(F32)
        high = product.astype(BF16)
        highs.append(high)
        lows.append((product - high.astype(F32)).astype(BF16))
    row = lax.broadcasted_iota(jnp.int32, (QW, HEAD_DIM), 0) // HEAD_DIM
    lane = lax.broadcasted_iota(jnp.int32, (QW, HEAD_DIM), 1)
    ones = jnp.where((lane >= 3 * row) & (lane < 3 * row + 3), 1.0, 0.0).astype(BF16)
    left = dot(jnp.concatenate(highs), ones, NN) + dot(jnp.concatenate(lows), ones, NN)
    part = lax.broadcasted_iota(jnp.int32, left.shape, 1) % 3
    first = left.astype(BF16).astype(F32)
    second = (left - first).astype(BF16).astype(F32)
    third = left - first - second
    deltas = jnp.where(part == 0, first, jnp.where(part == 1, second, third))
    deltas_ref[...] = deltas.astype(BF16)
    for d in range(KV_HEADS):
        h = me ^ d
        for c, chunk in enumerate(CHUNKS):
            out = outs[c * KV_HEADS + d]
            at = 0
            if c == 0:
                thin = pl.ds(times(h, HEAD_DIM), HEAD_DIM)
                out[:, 0:HEAD_DIM] = k_ref[:, thin]
                out[:, HEAD_DIM : 2 * HEAD_DIM] = v_ref[:, thin]
                out[:, 2 * HEAD_DIM : KVD] = deltas_ref[pl.ds(times(h, rows), rows)]
                at = KVD
            size = len(chunk) * HEAD_DIM
            cols = pl.ds(pl.multiple_of(h * QW + chunk[0] * HEAD_DIM, HEAD_DIM), size)
            out[:, at : at + size] = q_ref[:, cols]
            out[:, at + size : at + 2 * size] = g_ref[:, cols]


def pack(place, q, g, o, k, v):
    rows = q.shape[0]
    block = min(PACK_ROWS, rows)
    wide = pl.BlockSpec((block, KV_HEADS * QW), lambda i: (i, 0))
    thin = pl.BlockSpec((block, KV_HEADS * HEAD_DIM), lambda i: (i, 0))
    widths = [send_width(c) for c in range(len(CHUNKS)) for d in range(KV_HEADS)]
    outs = pl.pallas_call(
        pack_kernel,
        grid=(rows // block,),
        in_specs=[SMEM, wide, wide, wide, thin, thin],
        out_specs=[pl.BlockSpec((block, w), lambda i: (i, 0)) for w in widths],
        out_shape=[jax.ShapeDtypeStruct((rows, w), BF16) for w in widths],
        scratch_shapes=[pltpu.VMEM((KV_HEADS * block, HEAD_DIM), BF16)],
        compiler_params=params(60),
        name="pack",
    )(place, q, g, o, k, v)
    return [outs[c * KV_HEADS : (c + 1) * KV_HEADS] for c in range(len(CHUNKS))]


def start_all(copies, sems):
    started = [pltpu.make_async_copy(src, dst, sems.at[n]) for n, (src, dst) in enumerate(copies)]
    for copy in started:
        copy.start()
    return started


def unpack_kernel(place_ref, *refs):
    count = len(CHUNKS) * KV_HEADS
    backs, (q_ref, k_ref, v_ref, sems) = refs[:count], refs[count:]
    me = place_ref[1]
    copies = []
    for c, chunk in enumerate(CHUNKS):
        size = len(chunk) * HEAD_DIM
        for d in range(KV_HEADS):
            back = backs[c * KV_HEADS + d]
            h = me ^ d
            cols = pl.ds(pl.multiple_of(h * QW + chunk[0] * HEAD_DIM, HEAD_DIM), size)
            copies.append((back.at[:, 0:size], q_ref.at[:, cols]))
            if c == len(CHUNKS) - 1:
                thin = pl.ds(times(h, HEAD_DIM), HEAD_DIM)
                copies.append((back.at[:, size : size + HEAD_DIM], k_ref.at[:, thin]))
                copies.append((back.at[:, size + HEAD_DIM :], v_ref.at[:, thin]))
    for copy in start_all(copies, sems):
        copy.wait()


def unpack(place, backs):
    flat = [a for chunk in backs for a in chunk]
    rows = flat[0].shape[0]
    return pl.pallas_call(
        unpack_kernel,
        in_specs=[SMEM] + [ANY] * len(flat),
        out_specs=[ANY] * 3,
        out_shape=[
            jax.ShapeDtypeStruct((rows, KV_HEADS * QW), BF16),
            jax.ShapeDtypeStruct((rows, KV_HEADS * HEAD_DIM), BF16),
            jax.ShapeDtypeStruct((rows, KV_HEADS * HEAD_DIM), BF16),
        ],
        scratch_shapes=[pltpu.SemaphoreType.DMA((len(flat) + 2 * KV_HEADS,))],
        compiler_params=params(4),
        name="unpack",
    )(place, *flat)


def attend_kernel(chunk, prompt, place_ref, *refs):
    refs = list(refs)
    take = lambda n: [refs.pop(0) for _ in range(n)]
    first, last = chunk == 0, chunk == len(CHUNKS) - 1
    heads = CHUNKS[chunk]
    wide = len(heads) * TILE
    size = len(heads) * HEAD_DIM
    x_in = take(KV_HEADS)
    if first:
        (pkv_in,) = take(1)
    else:
        dk_in, dv_in, k_all, v_all, k_t, d_all = take(6)
    back_out = take(KV_HEADS)
    if last:
        pg_out = take(lax.axis_size("prefix"))
    else:
        dk, dv = take(2)
        if first:
            k_all, v_all, k_t, d_all = take(4)
    x_ref, back_ref, in_sems, out_sems, qs, gs, e_all, m_all, l_all, p_s, l_s, dq_t = take(12)
    if last:
        pg_ref, dk, dv = take(3)
        if first:
            k_all, v_all, k_t, d_all = take(4)
    if first:
        (pkv_ref,) = take(1)

    parts = prompt // WIDE_TILE
    slots = x_ref.shape[0]
    length, me, me_prefix = place_ref[0], place_ref[1], place_ref[2]
    rows = slots // KV_HEADS
    at = KVD if first else 0
    copies = [
        (x_in[d], x_ref.at[pl.ds(times(me ^ d, rows), rows)]) for d in range(KV_HEADS)
    ]
    if first:
        sources = pkv_in.shape[0]
        share = prompt // sources
        copies += [
            (pkv_in.at[f], pkv_ref.at[pl.ds(times(me_prefix ^ gather_mask(f), share), share)])
            for f in range(sources)
        ]
    else:
        copies += [(dk_in, dk), (dv_in, dv)]
    copies = start_all(copies, in_sems)
    back_ref[...] = jnp.zeros_like(back_ref)
    if first:
        dk[...] = jnp.zeros_like(dk)
        dv[...] = jnp.zeros_like(dv)
    for copy in copies:
        copy.wait()
    if first:
        k_all[0:prompt] = pkv_ref[:, 0:HEAD_DIM]
        v_all[0:prompt] = pkv_ref[:, HEAD_DIM:]
        k_all[prompt:] = x_ref[:, 0:HEAD_DIM]
        v_all[prompt:] = x_ref[:, HEAD_DIM : 2 * HEAD_DIM]
        d_all[...] = x_ref[:, 2 * HEAD_DIM : KVD]
        for t in range((prompt + slots) // TILE):
            block = slice(t * TILE, (t + 1) * TILE)
            k_t[:, block] = k_all[block].astype(F32).T.astype(BF16)

    seen = lax.broadcasted_iota(jnp.int32, (TILE, TILE), 0) <= lax.broadcasted_iota(
        jnp.int32, (TILE, TILE), 1
    )

    def lanes(j):
        return slice(j * TILE, (j + 1) * TILE)

    def select(head, size):
        lane = lax.broadcasted_iota(jnp.int32, (size, HEAD_DIM), 1)
        return jnp.where((lane >= 3 * head) & (lane < 3 * head + 3), -1.0, 0.0).astype(BF16)

    def score_tile(block, index, diagonal):
        for j in range(len(heads)):
            s = dot(k_all[block], qs[lanes(j)], NT)
            if diagonal:
                s = jnp.where(seen, s, -jnp.inf)
            top = jnp.max(s, axis=0, keepdims=True)
            e = jnp.exp2((s - top) * EXP2_SCALE)
            m_all[pl.ds(index, 1), lanes(j)] = top
            l_all[pl.ds(index, 1), lanes(j)] = jnp.sum(e, axis=0, keepdims=True)
            e_all[block, lanes(j)] = e

    def grad_tile(block, keys, index, at):
        for j, head in enumerate(heads):
            shifted = dot(
                jnp.concatenate([v_all[block], select(head, keys)], axis=1), gs[lanes(j)], NT
            )
            p = e_all[block, lanes(j)] * m_all[pl.ds(index, 1), lanes(j)]
            p_s[at : at + keys, lanes(j)] = p.astype(BF16)
            l_s[at : at + keys, lanes(j)] = (p * shifted).astype(BF16)

    def grad_sums(block, keys):
        dv[block] += dot(p_s[0:keys], gs[:, 0:HEAD_DIM], NN)
        dk[block] += dot(l_s[0:keys], qs[...], NN)
        return dot(k_t[:, block], l_s[0:keys], NN)

    def slot_block(i, carry):
        here = pl.ds(times(i, TILE), TILE)
        for j in range(len(heads)):
            col = at + j * HEAD_DIM
            qs[lanes(j)] = x_ref[here, col : col + HEAD_DIM]
            gs[lanes(j), 0:HEAD_DIM] = x_ref[here, col + size : col + size + HEAD_DIM]
            gs[lanes(j), HEAD_DIM:] = d_all[here]

        def own(t):
            return pl.ds(pl.multiple_of(prompt + t * TILE, TILE), TILE)

        for t in range(parts):
            score_tile(slice(t * WIDE_TILE, (t + 1) * WIDE_TILE), t, False)
        score_tile(own(i), parts + i, True)

        def score_body(t, carry):
            score_tile(own(t), parts + t, False)
            return carry

        lax.fori_loop(0, i, score_body, 0)

        tile_index = lax.broadcasted_iota(jnp.int32, m_all.shape, 0)
        tops = jnp.where(tile_index <= parts + i, m_all[...], -jnp.inf)
        sums = jnp.where(tile_index <= parts + i, l_all[...], 0.0)
        weight = jnp.exp2((tops - jnp.max(tops, axis=0, keepdims=True)) * EXP2_SCALE)
        total = jnp.sum(weight * sums, axis=0, keepdims=True)
        slot = lax.broadcasted_iota(jnp.int32, (1, wide), 1) % TILE + i * TILE
        live = jnp.where(slot < length, 1.0, 0.0)
        m_all[...] = weight * (live / total)

        for t in range(parts):
            grad_tile(slice(t * WIDE_TILE, (t + 1) * WIDE_TILE), WIDE_TILE, t, t * WIDE_TILE)
        dq_t[...] = grad_sums(slice(0, prompt), prompt)

        def grad_body(t, carry):
            grad_tile(own(t), TILE, parts + t, 0)
            dq_t[...] += grad_sums(own(t), TILE)
            return carry

        lax.fori_loop(0, i + 1, grad_body, 0)
        for j in range(len(heads)):
            back_ref[here, j * HEAD_DIM : (j + 1) * HEAD_DIM] = (
                (dq_t[:, lanes(j)] * SCALE).T.astype(BF16)
            )
        return carry

    lax.fori_loop(0, lax.div(length + TILE - 1, TILE), slot_block, 0)
    copies = []
    if last:
        pg_ref[:, 0:HEAD_DIM] = (dk[0:prompt] * SCALE).astype(BF16)
        pg_ref[:, HEAD_DIM:] = dv[0:prompt].astype(BF16)
        share = prompt // len(pg_out)
        copies += [
            (pg_ref.at[pl.ds(times(me_prefix ^ d, share), share)], out)
            for d, out in enumerate(pg_out)
        ]
        back_ref[:, size : size + HEAD_DIM] = (dk[prompt:] * SCALE).astype(BF16)
        back_ref[:, size + HEAD_DIM :] = dv[prompt:].astype(BF16)
    copies += [
        (back_ref.at[pl.ds(times(me ^ d, rows), rows)], back_out[d]) for d in range(KV_HEADS)
    ]
    for copy in start_all(copies, out_sems):
        copy.wait()


def attend(chunk, prompt, place, x, carried):
    first, last = chunk == 0, chunk == len(CHUNKS) - 1
    rows = x[0].shape[0]
    slots = rows * KV_HEADS
    keys = slots + prompt
    wide = len(CHUNKS[chunk]) * TILE
    size = len(CHUNKS[chunk]) * HEAD_DIM
    responses = lax.axis_size("prefix")
    sums = [((keys, HEAD_DIM), F32)] * 2
    shared = [((keys, HEAD_DIM), BF16)] * 2 + [((HEAD_DIM, keys), BF16), ((slots, HEAD_DIM), BF16)]
    outs = [((rows, back_width(chunk)), BF16)] * KV_HEADS
    specs = [ANY] * KV_HEADS
    if last:
        outs += [((prompt // responses, 2 * HEAD_DIM), BF16)] * responses
        specs += [ANY] * responses
    else:
        outs += sums
        specs += [VMEM] * 2
        if first:
            outs += shared
            specs += [VMEM] * 4
    scratch = [
        pltpu.VMEM((slots, send_width(chunk)), BF16),
        pltpu.VMEM((slots, back_width(chunk)), BF16),
        pltpu.SemaphoreType.DMA((KV_HEADS + (responses if first else 2),)),
        pltpu.SemaphoreType.DMA((KV_HEADS + (responses if last else 0),)),
        pltpu.VMEM((wide, HEAD_DIM), BF16),
        pltpu.VMEM((wide, 2 * HEAD_DIM), BF16),
        pltpu.VMEM((keys, wide), F32),
        pltpu.VMEM((8, wide), F32),
        pltpu.VMEM((8, wide), F32),
        pltpu.VMEM((prompt, wide), BF16),
        pltpu.VMEM((prompt, wide), BF16),
        pltpu.VMEM((HEAD_DIM, wide), F32),
    ]
    if last:
        scratch += [pltpu.VMEM((prompt, 2 * HEAD_DIM), BF16)]
        scratch += [pltpu.VMEM(shape, dtype) for shape, dtype in sums]
        if first:
            scratch += [pltpu.VMEM(shape, dtype) for shape, dtype in shared]
    if first:
        scratch += [pltpu.VMEM((prompt, 2 * HEAD_DIM), BF16)]
    carried_specs = [ANY] if first else [ANY] * 2 + [VMEM] * 4
    return pl.pallas_call(
        functools.partial(attend_kernel, chunk, prompt),
        in_specs=[SMEM] + [ANY] * KV_HEADS + carried_specs,
        out_specs=specs,
        out_shape=[jax.ShapeDtypeStruct(shape, dtype) for shape, dtype in outs],
        scratch_shapes=scratch,
        compiler_params=params(40),
        cost_estimate=pl.CostEstimate(
            flops=10 * slots * (prompt + slots) * size, transcendentals=0, bytes_accessed=8 * slots * size
        ),
        name="attend%d" % chunk,
    )(place, *x, *carried)


def sum_kernel(place_ref, *refs):
    parts, outs, total = refs[:-KV_HEADS - 1], refs[-KV_HEADS - 1 : -1], refs[-1]
    value = parts[0][...].astype(F32)
    for part in parts[1:]:
        value = value + part[...].astype(F32)
    total[...] = value
    own = outs[0].shape[0]
    for d, out in enumerate(outs):
        out[...] = total[pl.ds(times(place_ref[1] ^ d, own), own)]


def sum_parts(place, parts):
    rows, width = parts[0].shape
    own = rows // KV_HEADS
    return pl.pallas_call(
        sum_kernel,
        in_specs=[SMEM] + [VMEM] * len(parts),
        out_specs=[VMEM] * KV_HEADS,
        out_shape=[jax.ShapeDtypeStruct((own, width), F32)] * KV_HEADS,
        scratch_shapes=[pltpu.VMEM((rows, width), F32)],
        compiler_params=params(4),
        name="sum_parts",
    )(place, *parts)


def spread_kernel(place_ref, *refs):
    parts, (k_ref, v_ref) = refs[:KV_HEADS], refs[KV_HEADS:]
    for d, part in enumerate(parts):
        cols = pl.ds(times(place_ref[1] ^ d, HEAD_DIM), HEAD_DIM)
        k_ref[:, cols] = part[:, 0:HEAD_DIM]
        v_ref[:, cols] = part[:, HEAD_DIM:]


def spread_heads(place, parts):
    shape = jax.ShapeDtypeStruct((parts[0].shape[0], KV_HEADS * HEAD_DIM), F32)
    return pl.pallas_call(
        spread_kernel,
        in_specs=[SMEM] + [VMEM] * KV_HEADS,
        out_specs=[VMEM] * 2,
        out_shape=[shape] * 2,
        compiler_params=params(4),
        name="spread_heads",
    )(place, *parts)


def swap(value, axis, d):
    return lax.ppermute(value, axis, [(i, i ^ d) for i in range(lax.axis_size(axis))])


def swap_all(values, axis):
    return [values[0]] + [swap(values[d], axis, d) for d in range(1, len(values))]


def gather_prompt(value):
    value = value[None]
    for bit in GATHER_BITS:
        value = jnp.concatenate([value, swap(value, "prefix", 1 << bit)])
    return value


def local(
    resp_query,
    resp_keys,
    resp_values,
    resp_out,
    resp_grad,
    prompt_keys,
    prompt_values,
    resp_lengths,
):
    head = lax.axis_index("resp")
    prompt = prompt_keys.shape[0] * lax.axis_size("prefix")
    place = jnp.stack([resp_lengths[0], head, lax.axis_index("prefix")])
    cut = lambda a: lax.dynamic_slice_in_dim(a, head * HEAD_DIM, HEAD_DIM, 1)
    pkv = gather_prompt(jnp.concatenate([cut(prompt_keys), cut(prompt_values)], axis=1))
    sends = pack(place, resp_query[0], resp_grad[0], resp_out[0], resp_keys[0], resp_values[0])
    arrived = [swap_all(send, "resp") for send in sends]
    carried = [pkv]
    shared = []
    backs = []
    for chunk, x in enumerate(arrived):
        outs = attend(chunk, prompt, place, x, carried)
        back, outs = outs[:KV_HEADS], outs[KV_HEADS:]
        if chunk == len(CHUNKS) - 1:
            pg = swap_all(outs, "prefix")
        else:
            shared = shared or outs[2:]
            carried = outs[:2] + shared
        backs.append(swap_all(back, "resp"))
    pg = spread_heads(place, swap_all(sum_parts(place, pg), "resp"))
    grad_query, grad_keys, grad_values = unpack(place, backs)
    return (
        grad_query[None],
        grad_keys[None],
        grad_values[None],
        pg[0].astype(BF16),
        pg[1].astype(BF16),
    )


def solution(mesh):
    return jax.shard_map(
        local,
        mesh=mesh,
        in_specs=(
            P("prefix", "resp", None),
            P("prefix", "resp", None),
            P("prefix", "resp", None),
            P("prefix", "resp", None),
            P("prefix", "resp", None),
            P("prefix", None),
            P("prefix", None),
            P("prefix"),
        ),
        out_specs=(
            P("prefix", "resp", None),
            P("prefix", "resp", None),
            P("prefix", "resp", None),
            P(("prefix", "resp"), None),
            P(("prefix", "resp"), None),
        ),
        check_vma=False,
    )
```

time: 164 us -> 202 us (1.23)
  starting transfers between devices: 16.1 us -> 111 us
  blocking collectives: 33.8 us -> 0 us
  waiting for transfers between devices: 66.5 us -> 50.8 us
  local copies, waits for them, and re-layouts: 5.97 us -> 0.83 us
  Pallas kernels: 38.9 us -> 35.6 us
    ppermute x0 -> x54, starting transfers between devices: none -> 111 us  [swap(): lax.ppermute(value, axis, [(i, i ^ d) for i in range(lax.axis_size(axis))])]
    all_to_all x3 -> x0, waiting for transfers between devices: 66.5 us -> none  [the longest x1 39.9 us: local(): x = lax.all_to_all(send, 'resp', 0, 0, tiled=True)]
    ppermute x0 -> x54, waiting for transfers between devices: none -> 50.8 us  [swap(): lax.ppermute(value, axis, [(i, i ^ d) for i in range(lax.axis_size(axis))])]
    all_to_all x2 -> x0, blocking collectives: 33.8 us -> none  [the longest x1 25 us: local(): lax.all_to_all(pg.reshape(responses, part, width), 'prefix', 0, 0, tiled=...]
    all_to_all x3 -> x0, starting transfers between devices: 16.1 us -> none  [the longest x1 7.96 us: local(): lax.all_to_all(copies, 'prefix', 0, 0, tiled=True)]
    unnamed x6 -> x19, local copies, waits for them, and re-layouts: 3.76 us -> 0.05 us
    pallas_call x3 -> x6, Pallas kernels: 38.9 us -> 35.6 us  [the longest x2 27.2 us: attend(): pl.pallas_call(functools.partial(attend_kernel, chunk, prompt), in_specs=...]
  transfers between devices with their start and end apart: 3 -> 54, of which waited for: 3 -> 19; matrix products, arithmetic and copies ran while one was open for 0% -> 1% of each run, Pallas kernels for 5% -> 9%
where the time goes in v2:
time: 202 us
  starting transfers between devices  111 us (55%)
  waiting for transfers between devices  50.8 us (25%)
  Pallas kernels  35.6 us (18%)
    ppermute x54, starting transfers between devices, swap(): lax.ppermute(value, axis, [(i, i ^ d) for i in range(lax.axis_size(axis))])  111 us
    ppermute x54, waiting for transfers between devices, swap(): lax.ppermute(value, axis, [(i, i ^ d) for i in range(lax.axis_size(axis))])  50.8 us
    pallas_call x2, Pallas kernels, attend(): pl.pallas_call(functools.partial(attend_kernel, chunk, prompt), in_specs=...  27.2 us
    pallas_call x1, Pallas kernels, pack(): pl.pallas_call(pack_kernel, grid=(rows // block,), in_specs=[SMEM, wide,...  5.21 us
  transfers between devices with their start and end apart: 54, of which 19 were waited for; matrix products, arithmetic and copies ran while one was open for 1% of the time, Pallas kernels for 9%

profile of v2, /device:TPU:0, one launch (start us, length us, event | category | flops | bytes accessed | tf_op | source)
XLA Modules:
  0.0 201.9 jit_solution(7921201558423901562)
XLA Ops:
  1.4 3.2 %collective-permute-start.7 = (bf16[1,64,256]{2,1,0:T(8,128)(2,1)S(1)}, bf16[1,64,256]{2,1,0:T(8,128)(2,1)S(1)}, u32[]{:S(2)}, u32[]{:S(2)}) collective-permute-start(bf16[1,64,256]{2,1,0:T(8,128)(2,1)S(1)} %maximum_bitcast_fusion), channel_id=1, source_target_pairs={{0,16},{8,24},{16,0},{24,8},{32,48},{40,56},{48,32},{56,40},{64,80... | collective-permute-start | bytes 98312 | tf_op jit(solution)/shard_map/ppermute | solution.py:424
  11.6 5.2 %pack.1 = (bf16[128,896]{1,0:T(8,128)(2,1)}, bf16[128,896]{1,0:T(8,128)(2,1)}, bf16[128,896]{1,0:T(8,128)(2,1)}, bf16[128,896]{1,0:T(8,128)(2,1)}, bf16[128,896]...) custom-call(s32[3]{0:T(128)} %pad_add_fusion.place_ref, ...), custom_call_target="tpu_custom_call" | custom-call | tf_op jit(solution)/shard_map/pack/pallas_call | solution.py:101
  21.0 3.7 %collective-permute-start.10 = (bf16[8,64,256]{2,1,0:T(8,128)(2,1)S(1)}, bf16[8,64,256]{2,1,0:T(8,128)(2,1)S(1)}, u32[]{:S(2)}, u32[]{:S(2)}) collective-permute-start(bf16[8,64,256]{2,1,0:T(8,128)(2,1)S(1)} %pad_maximum_fusion), channel_id=1, source_target_pairs={{0,64},{8,72},{16,80},{24,88},{32,96},{40,104},{48,112},{56,120},{... | collective-permute-start | bytes 786440 | tf_op jit(solution)/shard_map/ppermute | solution.py:424
  24.9 2.5 %collective-permute-start.2 = (bf16[128,896]{1,0:T(8,128)(2,1)}, bf16[128,896]{1,0:T(8,128)(2,1)S(1)}, u32[]{:S(2)}, u32[]{:S(2)}) collective-permute-start(bf16[128,896]{1,0:T(8,128)(2,1)} %get-tuple-element.75), channel_id=1, source_target_pairs={{0,3},{1,2},{2,1},{3,0},{4,7},{5,6},{6,5},{7,4},{8,11},{9,10},{10,... | collective-permute-start | bytes 688136 | tf_op jit(solution)/shard_map/ppermute | solution.py:424
  27.5 2.9 %collective-permute-start.3 = (bf16[128,896]{1,0:T(8,128)(2,1)}, bf16[128,896]{1,0:T(8,128)(2,1)S(1)}, u32[]{:S(2)}, u32[]{:S(2)}) collective-permute-start(bf16[128,896]{1,0:T(8,128)(2,1)} %get-tuple-element.76), channel_id=1, source_target_pairs={{0,4},{1,5},{2,6},{3,7},{4,0},{5,1},{6,2},{7,3},{8,12},{9,13},{10,... | collective-permute-start | bytes 688136 | tf_op jit(solution)/shard_map/ppermute | solution.py:424
  30.4 3.6 %collective-permute-start.4 = (bf16[128,896]{1,0:T(8,128)(2,1)}, bf16[128,896]{1,0:T(8,128)(2,1)S(1)}, u32[]{:S(2)}, u32[]{:S(2)}) collective-permute-start(bf16[128,896]{1,0:T(8,128)(2,1)} %get-tuple-element.77), channel_id=1, source_target_pairs={{0,5},{1,4},{2,7},{3,6},{4,1},{5,0},{6,3},{7,2},{8,13},{9,12},{10,... | collective-permute-start | bytes 688136 | tf_op jit(solution)/shard_map/ppermute | solution.py:424
  34.0 8.0 %collective-permute-done.1.refs_2_ = bf16[128,896]{1,0:T(8,128)(2,1)S(1)} collective-permute-done((bf16[128,896]{1,0:T(8,128)(2,1)}, bf16[128,896]{1,0:T(8,128)(2,1)S(1)}, u32[]{:S(2)}, u32[]{:S(2)}) %collective-permute-start.1) | collective-permute-done | bytes 229408 | tf_op jit(solution)/shard_map/ppermute | solution.py:424
  46.1 3.8 %collective-permute-done.3.refs_4_ = bf16[128,896]{1,0:T(8,128)(2,1)S(1)} collective-permute-done((bf16[128,896]{1,0:T(8,128)(2,1)}, bf16[128,896]{1,0:T(8,128)(2,1)S(1)}, u32[]{:S(2)}, u32[]{:S(2)}) %collective-permute-start.3) | collective-permute-done | bytes 229408 | tf_op jit(solution)/shard_map/ppermute | solution.py:424
  50.8 3.2 %collective-permute-start.22 = (bf16[128,768]{1,0:T(8,128)(2,1)S(1)}, bf16[128,768]{1,0:T(8,128)(2,1)S(1)}, u32[]{:S(2)}, u32[]{:S(2)}) collective-permute-start(bf16[128,768]{1,0:T(8,128)(2,1)S(1)} %copy-done.5), channel_id=1, source_target_pairs={{0,5},{1,4},{2,7},{3,6},{4,1},{5,0},{6,3},{7,2},{8,13},{9,12},{10,... | collective-permute-start | bytes 589832 | tf_op jit(solution)/shard_map/ppermute | solution.py:424
  54.0 11.7 %collective-permute-done.5.refs_6_ = bf16[128,896]{1,0:T(8,128)(2,1)S(1)} collective-permute-done((bf16[128,896]{1,0:T(8,128)(2,1)}, bf16[128,896]{1,0:T(8,128)(2,1)S(1)}, u32[]{:S(2)}, u32[]{:S(2)}) %collective-permute-start.5) | collective-permute-done | bytes 229408 | tf_op jit(solution)/shard_map/ppermute | solution.py:424
  68.0 12.2 %attend0.1 = (bf16[128,256]{1,0:T(8,128)(2,1)S(1)}, bf16[128,256]{1,0:T(8,128)(2,1)S(1)}, bf16[128,256]{1,0:T(8,128)(2,1)S(1)}, bf16[128,256]{1,0:T(8,128)(2,1)S...) custom-call(s32[3]{0:T(128)S(1)} %copy-done, ...), custom_call_target="tpu_custom_call" | custom-call | flops 5368709120 | bytes 2097152 | tf_op jit(solution)/shard_map/attend0/pallas_call | solution.py:364
  80.3 15.0 %attend1.1 = (bf16[128,640]{1,0:T(8,128)(2,1)S(1)}, bf16[128,640]{1,0:T(8,128)(2,1)S(1)}, bf16[128,640]{1,0:T(8,128)(2,1)S(1)}, bf16[128,640]{1,0:T(8,128)(2,1)S...) custom-call(s32[3]{0:T(128)S(1)} %copy-done, ...), custom_call_target="tpu_custom_call" | custom-call | flops 8053063680 | bytes 3145728 | tf_op jit(solution)/shard_map/attend1/pallas_call | solution.py:364
  95.4 13.0 %collective-permute-start.33 = (bf16[64,256]{1,0:T(8,128)(2,1)S(1)}, bf16[64,256]{1,0:T(8,128)(2,1)S(1)}, u32[]{:S(2)}, u32[]{:S(2)}) collective-permute-start(bf16[64,256]{1,0:T(8,128)(2,1)S(1)} %get-tuple-element.115), channel_id=1, source_target_pairs={{0,16},{8,24},{16,0},{24,8},{32,48},{40,56},{48,32},{56,40},{64,80... | collective-permute-start | bytes 98312 | tf_op jit(solution)/shard_map/ppermute | solution.py:424
  108.5 12.4 %collective-permute-start.35 = (bf16[64,256]{1,0:T(8,128)(2,1)S(1)}, bf16[64,256]{1,0:T(8,128)(2,1)S(1)}, u32[]{:S(2)}, u32[]{:S(2)}) collective-permute-start(bf16[64,256]{1,0:T(8,128)(2,1)S(1)} %get-tuple-element.117), channel_id=1, source_target_pairs={{0,32},{8,40},{16,48},{24,56},{32,0},{40,8},{48,16},{56,24},{64,96... | collective-permute-start | bytes 98312 | tf_op jit(solution)/shard_map/ppermute | solution.py:424
  120.9 4.4 %collective-permute-start.37 = (bf16[64,256]{1,0:T(8,128)(2,1)S(1)}, bf16[64,256]{1,0:T(8,128)(2,1)S(1)}, u32[]{:S(2)}, u32[]{:S(2)}) collective-permute-start(bf16[64,256]{1,0:T(8,128)(2,1)S(1)} %get-tuple-element.119), channel_id=1, source_target_pairs={{0,48},{8,56},{16,32},{24,40},{32,16},{40,24},{48,0},{56,8},{64,11... | collective-permute-start | bytes 98312 | tf_op jit(solution)/shard_map/ppermute | solution.py:424
  125.4 5.6 %collective-permute-start.39 = (bf16[64,256]{1,0:T(8,128)(2,1)S(1)}, bf16[64,256]{1,0:T(8,128)(2,1)S(1)}, u32[]{:S(2)}, u32[]{:S(2)}) collective-permute-start(bf16[64,256]{1,0:T(8,128)(2,1)S(1)} %get-tuple-element.121), channel_id=1, source_target_pairs={{0,64},{8,72},{16,80},{24,88},{32,96},{40,104},{48,112},{56,120},{... | collective-permute-start | bytes 98312 | tf_op jit(solution)/shard_map/ppermute | solution.py:424
  131.0 5.9 %collective-permute-start.41 = (bf16[64,256]{1,0:T(8,128)(2,1)S(1)}, bf16[64,256]{1,0:T(8,128)(2,1)S(1)}, u32[]{:S(2)}, u32[]{:S(2)}) collective-permute-start(bf16[64,256]{1,0:T(8,128)(2,1)S(1)} %get-tuple-element.123), channel_id=1, source_target_pairs={{0,80},{8,88},{16,64},{24,72},{32,112},{40,120},{48,96},{56,104},{... | collective-permute-start | bytes 98312 | tf_op jit(solution)/shard_map/ppermute | solution.py:424
  139.7 4.7 %collective-permute-start.45 = (bf16[64,256]{1,0:T(8,128)(2,1)S(1)}, bf16[64,256]{1,0:T(8,128)(2,1)S(1)}, u32[]{:S(2)}, u32[]{:S(2)}) collective-permute-start(bf16[64,256]{1,0:T(8,128)(2,1)S(1)} %get-tuple-element.127), channel_id=1, source_target_pairs={{0,112},{8,120},{16,96},{24,104},{32,80},{40,88},{48,64},{56,72},{... | collective-permute-start | bytes 98312 | tf_op jit(solution)/shard_map/ppermute | solution.py:424
  147.3 4.3 %collective-permute-done.46.refs_15_ = bf16[64,256]{1,0:T(8,128)(2,1)S(1)} collective-permute-done((bf16[64,256]{1,0:T(8,128)(2,1)S(1)}, bf16[64,256]{1,0:T(8,128)(2,1)S(1)}, u32[]{:S(2)}, u32[]{:S(2)}) %collective-permute-start.46) | collective-permute-done | bytes 32800 | tf_op jit(solution)/shard_map/ppermute | solution.py:424
  156.4 3.8 %collective-permute-done.48.refs_2_ = f32[8,256]{1,0:T(8,128)S(1)} collective-permute-done((f32[8,256]{1,0:T(8,128)S(1)}, f32[8,256]{1,0:T(8,128)S(1)}, u32[]{:S(2)}, u32[]{:S(2)}) %collective-permute-start.48) | collective-permute-done | bytes 8224 | tf_op jit(solution)/shard_map/ppermute | solution.py:424
  170.3 3.7 %collective-permute-done.53.refs_7_ = f32[8,256]{1,0:T(8,128)S(1)} collective-permute-done((f32[8,256]{1,0:T(8,128)S(1)}, f32[8,256]{1,0:T(8,128)S(1)}, u32[]{:S(2)}, u32[]{:S(2)}) %collective-permute-start.53) | collective-permute-done | bytes 8224 | tf_op jit(solution)/shard_map/ppermute | solution.py:424
  174.0 2.6 %collective-permute-start.14 = (bf16[128,256]{1,0:T(8,128)(2,1)S(1)}, bf16[128,256]{1,0:T(8,128)(2,1)S(1)}, u32[]{:S(2)}, u32[]{:S(2)}) collective-permute-start(bf16[128,256]{1,0:T(8,128)(2,1)S(1)} %get-tuple-element.84), channel_id=1, source_target_pairs={{0,4},{1,5},{2,6},{3,7},{4,0},{5,1},{6,2},{7,3},{8,12},{9,13},{10,... | collective-permute-start | bytes 196616 | tf_op jit(solution)/shard_map/ppermute | solution.py:424
  184.7 3.8 %collective-permute-start.28 = (bf16[128,640]{1,0:T(8,128)(2,1)S(1)}, bf16[128,640]{1,0:T(8,128)(2,1)S(1)}, u32[]{:S(2)}, u32[]{:S(2)}) collective-permute-start(bf16[128,640]{1,0:T(8,128)(2,1)S(1)} %get-tuple-element.106), channel_id=1, source_target_pairs={{0,4},{1,5},{2,6},{3,7},{4,0},{5,1},{6,2},{7,3},{8,12},{9,13},{10,... | collective-permute-start | bytes 491528 | tf_op jit(solution)/shard_map/ppermute | solution.py:424
  196.2 3.5 %collective-permute-done.30.refs_14_ = bf16[128,640]{1,0:T(8,128)(2,1)S(1)} collective-permute-done((bf16[128,640]{1,0:T(8,128)(2,1)S(1)}, bf16[128,640]{1,0:T(8,128)(2,1)S(1)}, u32[]{:S(2)}, u32[]{:S(2)}) %collective-permute-start.30) | collective-permute-done | bytes 163872 | tf_op jit(solution)/shard_map/ppermute | solution.py:424
  (119 shorter events, 57.7 us)
Async XLA Ops:
  8.3 12.7 %collective-permute-start.9 = (bf16[4,64,256]{2,1,0:T(8,128)(2,1)S(1)}, bf16[4,64,256]{2,1,0:T(8,128)(2,1)S(1)}, u32[]{:S(2)}, u32[]{:S(2)}) collective-permute-start(bf16[4,64,256]{2,1,0:T(8,128)(2,1)S(1)} %pad_maximum_fusion.1), channel_id=1, source_target_pairs={{0,32},{8,40},{16,48},{24,56},{32,0},{40,8},{48,16},{56,24},{64,96... | collective-permute-start | bytes 393224 | tf_op jit(solution)/shard_map/ppermute | solution.py:424
  20.6 21.4 %collective-permute-start.1 = (bf16[128,896]{1,0:T(8,128)(2,1)}, bf16[128,896]{1,0:T(8,128)(2,1)S(1)}, u32[]{:S(2)}, u32[]{:S(2)}) collective-permute-start(bf16[128,896]{1,0:T(8,128)(2,1)} %get-tuple-element.74), channel_id=1, source_target_pairs={{0,2},{1,3},{2,0},{3,1},{4,6},{5,7},{6,4},{7,5},{8,10},{9,11},{10,... | collective-permute-start | bytes 688136 | tf_op jit(solution)/shard_map/ppermute | solution.py:424
  21.0 23.3 %collective-permute-start.10 = (bf16[8,64,256]{2,1,0:T(8,128)(2,1)S(1)}, bf16[8,64,256]{2,1,0:T(8,128)(2,1)S(1)}, u32[]{:S(2)}, u32[]{:S(2)}) collective-permute-start(bf16[8,64,256]{2,1,0:T(8,128)(2,1)S(1)} %pad_maximum_fusion), channel_id=1, source_target_pairs={{0,64},{8,72},{16,80},{24,88},{32,96},{40,104},{48,112},{56,120},{... | collective-permute-start | bytes 786440 | tf_op jit(solution)/shard_map/ppermute | solution.py:424
  24.9 19.4 %collective-permute-start.2 = (bf16[128,896]{1,0:T(8,128)(2,1)}, bf16[128,896]{1,0:T(8,128)(2,1)S(1)}, u32[]{:S(2)}, u32[]{:S(2)}) collective-permute-start(bf16[128,896]{1,0:T(8,128)(2,1)} %get-tuple-element.75), channel_id=1, source_target_pairs={{0,3},{1,2},{2,1},{3,0},{4,7},{5,6},{6,5},{7,4},{8,11},{9,10},{10,... | collective-permute-start | bytes 688136 | tf_op jit(solution)/shard_map/ppermute | solution.py:424
  27.5 22.4 %collective-permute-start.3 = (bf16[128,896]{1,0:T(8,128)(2,1)}, bf16[128,896]{1,0:T(8,128)(2,1)S(1)}, u32[]{:S(2)}, u32[]{:S(2)}) collective-permute-start(bf16[128,896]{1,0:T(8,128)(2,1)} %get-tuple-element.76), channel_id=1, source_target_pairs={{0,4},{1,5},{2,6},{3,7},{4,0},{5,1},{6,2},{7,3},{8,12},{9,13},{10,... | collective-permute-start | bytes 688136 | tf_op jit(solution)/shard_map/ppermute | solution.py:424
  30.4 20.5 %collective-permute-start.4 = (bf16[128,896]{1,0:T(8,128)(2,1)}, bf16[128,896]{1,0:T(8,128)(2,1)S(1)}, u32[]{:S(2)}, u32[]{:S(2)}) collective-permute-start(bf16[128,896]{1,0:T(8,128)(2,1)} %get-tuple-element.77), channel_id=1, source_target_pairs={{0,5},{1,4},{2,7},{3,6},{4,1},{5,0},{6,3},{7,2},{8,13},{9,12},{10,... | collective-permute-start | bytes 688136 | tf_op jit(solution)/shard_map/ppermute | solution.py:424
  42.0 23.7 %collective-permute-start.5 = (bf16[128,896]{1,0:T(8,128)(2,1)}, bf16[128,896]{1,0:T(8,128)(2,1)S(1)}, u32[]{:S(2)}, u32[]{:S(2)}) collective-permute-start(bf16[128,896]{1,0:T(8,128)(2,1)} %get-tuple-element.78), channel_id=1, source_target_pairs={{0,6},{1,7},{2,4},{3,5},{4,2},{5,3},{6,0},{7,1},{8,14},{9,15},{10,... | collective-permute-start | bytes 688136 | tf_op jit(solution)/shard_map/ppermute | solution.py:424
  44.3 22.7 %collective-permute-start.6 = (bf16[128,896]{1,0:T(8,128)(2,1)}, bf16[128,896]{1,0:T(8,128)(2,1)S(1)}, u32[]{:S(2)}, u32[]{:S(2)}) collective-permute-start(bf16[128,896]{1,0:T(8,128)(2,1)} %get-tuple-element.79), channel_id=1, source_target_pairs={{0,7},{1,6},{2,5},{3,4},{4,3},{5,2},{6,1},{7,0},{8,15},{9,14},{10,... | collective-permute-start | bytes 688136 | tf_op jit(solution)/shard_map/ppermute | solution.py:424
  44.4 35.8 %collective-permute-start.20 = (bf16[128,768]{1,0:T(8,128)(2,1)S(1)}, bf16[128,768]{1,0:T(8,128)(2,1)S(1)}, u32[]{:S(2)}, u32[]{:S(2)}) collective-permute-start(bf16[128,768]{1,0:T(8,128)(2,1)S(1)} %copy-done.7), channel_id=1, source_target_pairs={{0,3},{1,2},{2,1},{3,0},{4,7},{5,6},{6,5},{7,4},{8,11},{9,10},{10,... | collective-permute-start | bytes 589832 | tf_op jit(solution)/shard_map/ppermute | solution.py:424
  49.9 30.3 %collective-permute-start.21 = (bf16[128,768]{1,0:T(8,128)(2,1)S(1)}, bf16[128,768]{1,0:T(8,128)(2,1)S(1)}, u32[]{:S(2)}, u32[]{:S(2)}) collective-permute-start(bf16[128,768]{1,0:T(8,128)(2,1)S(1)} %copy-done.6), channel_id=1, source_target_pairs={{0,4},{1,5},{2,6},{3,7},{4,0},{5,1},{6,2},{7,3},{8,12},{9,13},{10,... | collective-permute-start | bytes 589832 | tf_op jit(solution)/shard_map/ppermute | solution.py:424
  50.8 29.4 %collective-permute-start.22 = (bf16[128,768]{1,0:T(8,128)(2,1)S(1)}, bf16[128,768]{1,0:T(8,128)(2,1)S(1)}, u32[]{:S(2)}, u32[]{:S(2)}) collective-permute-start(bf16[128,768]{1,0:T(8,128)(2,1)S(1)} %copy-done.5), channel_id=1, source_target_pairs={{0,5},{1,4},{2,7},{3,6},{4,1},{5,0},{6,3},{7,2},{8,13},{9,12},{10,... | collective-permute-start | bytes 589832 | tf_op jit(solution)/shard_map/ppermute | solution.py:424
  65.7 14.5 %collective-permute-start.23 = (bf16[128,768]{1,0:T(8,128)(2,1)S(1)}, bf16[128,768]{1,0:T(8,128)(2,1)S(1)}, u32[]{:S(2)}, u32[]{:S(2)}) collective-permute-start(bf16[128,768]{1,0:T(8,128)(2,1)S(1)} %copy-done.4), channel_id=1, source_target_pairs={{0,6},{1,7},{2,4},{3,5},{4,2},{5,3},{6,0},{7,1},{8,14},{9,15},{10,... | collective-permute-start | bytes 589832 | tf_op jit(solution)/shard_map/ppermute | solution.py:424
  67.0 13.3 %collective-permute-start.24 = (bf16[128,768]{1,0:T(8,128)(2,1)S(1)}, bf16[128,768]{1,0:T(8,128)(2,1)S(1)}, u32[]{:S(2)}, u32[]{:S(2)}) collective-permute-start(bf16[128,768]{1,0:T(8,128)(2,1)S(1)} %copy-done.3), channel_id=1, source_target_pairs={{0,7},{1,6},{2,5},{3,4},{4,3},{5,2},{6,1},{7,0},{8,15},{9,14},{10,... | collective-permute-start | bytes 589832 | tf_op jit(solution)/shard_map/ppermute | solution.py:424
  95.3 25.6 %collective-permute-start.32 = (bf16[64,256]{1,0:T(8,128)(2,1)S(1)}, bf16[64,256]{1,0:T(8,128)(2,1)S(1)}, u32[]{:S(2)}, u32[]{:S(2)}) collective-permute-start(bf16[64,256]{1,0:T(8,128)(2,1)S(1)} %get-tuple-element.114), channel_id=1, source_target_pairs={{0,8},{8,0},{16,24},{24,16},{32,40},{40,32},{48,56},{56,48},{64,72... | collective-permute-start | bytes 98312 | tf_op jit(solution)/shard_map/ppermute | solution.py:424
  95.4 29.8 %collective-permute-start.33 = (bf16[64,256]{1,0:T(8,128)(2,1)S(1)}, bf16[64,256]{1,0:T(8,128)(2,1)S(1)}, u32[]{:S(2)}, u32[]{:S(2)}) collective-permute-start(bf16[64,256]{1,0:T(8,128)(2,1)S(1)} %get-tuple-element.115), channel_id=1, source_target_pairs={{0,16},{8,24},{16,0},{24,8},{32,48},{40,56},{48,32},{56,40},{64,80... | collective-permute-start | bytes 98312 | tf_op jit(solution)/shard_map/ppermute | solution.py:424
  108.4 17.0 %collective-permute-start.34 = (bf16[64,256]{1,0:T(8,128)(2,1)S(1)}, bf16[64,256]{1,0:T(8,128)(2,1)S(1)}, u32[]{:S(2)}, u32[]{:S(2)}) collective-permute-start(bf16[64,256]{1,0:T(8,128)(2,1)S(1)} %get-tuple-element.116), channel_id=1, source_target_pairs={{0,24},{8,16},{16,8},{24,0},{32,56},{40,48},{48,40},{56,32},{64,88... | collective-permute-start | bytes 98312 | tf_op jit(solution)/shard_map/ppermute | solution.py:424
  108.5 22.5 %collective-permute-start.35 = (bf16[64,256]{1,0:T(8,128)(2,1)S(1)}, bf16[64,256]{1,0:T(8,128)(2,1)S(1)}, u32[]{:S(2)}, u32[]{:S(2)}) collective-permute-start(bf16[64,256]{1,0:T(8,128)(2,1)S(1)} %get-tuple-element.117), channel_id=1, source_target_pairs={{0,32},{8,40},{16,48},{24,56},{32,0},{40,8},{48,16},{56,24},{64,96... | collective-permute-start | bytes 98312 | tf_op jit(solution)/shard_map/ppermute | solution.py:424
  120.9 16.0 %collective-permute-start.37 = (bf16[64,256]{1,0:T(8,128)(2,1)S(1)}, bf16[64,256]{1,0:T(8,128)(2,1)S(1)}, u32[]{:S(2)}, u32[]{:S(2)}) collective-permute-start(bf16[64,256]{1,0:T(8,128)(2,1)S(1)} %get-tuple-element.119), channel_id=1, source_target_pairs={{0,48},{8,56},{16,32},{24,40},{32,16},{40,24},{48,0},{56,8},{64,11... | collective-permute-start | bytes 98312 | tf_op jit(solution)/shard_map/ppermute | solution.py:424
  125.3 11.8 %collective-permute-start.38 = (bf16[64,256]{1,0:T(8,128)(2,1)S(1)}, bf16[64,256]{1,0:T(8,128)(2,1)S(1)}, u32[]{:S(2)}, u32[]{:S(2)}) collective-permute-start(bf16[64,256]{1,0:T(8,128)(2,1)S(1)} %get-tuple-element.120), channel_id=1, source_target_pairs={{0,56},{8,48},{16,40},{24,32},{32,24},{40,16},{48,8},{56,0},{64,12... | collective-permute-start | bytes 98312 | tf_op jit(solution)/shard_map/ppermute | solution.py:424
  125.4 13.7 %collective-permute-start.39 = (bf16[64,256]{1,0:T(8,128)(2,1)S(1)}, bf16[64,256]{1,0:T(8,128)(2,1)S(1)}, u32[]{:S(2)}, u32[]{:S(2)}) collective-permute-start(bf16[64,256]{1,0:T(8,128)(2,1)S(1)} %get-tuple-element.121), channel_id=1, source_target_pairs={{0,64},{8,72},{16,80},{24,88},{32,96},{40,104},{48,112},{56,120},{... | collective-permute-start | bytes 98312 | tf_op jit(solution)/shard_map/ppermute | solution.py:424
  131.0 13.4 %collective-permute-start.41 = (bf16[64,256]{1,0:T(8,128)(2,1)S(1)}, bf16[64,256]{1,0:T(8,128)(2,1)S(1)}, u32[]{:S(2)}, u32[]{:S(2)}) collective-permute-start(bf16[64,256]{1,0:T(8,128)(2,1)S(1)} %get-tuple-element.123), channel_id=1, source_target_pairs={{0,80},{8,88},{16,64},{24,72},{32,112},{40,120},{48,96},{56,104},{... | collective-permute-start | bytes 98312 | tf_op jit(solution)/shard_map/ppermute | solution.py:424
  145.4 28.6 %collective-permute-start.11 = (bf16[128,256]{1,0:T(8,128)(2,1)S(1)}, bf16[128,256]{1,0:T(8,128)(2,1)S(1)}, u32[]{:S(2)}, u32[]{:S(2)}) collective-permute-start(bf16[128,256]{1,0:T(8,128)(2,1)S(1)} %get-tuple-element.81), channel_id=1, source_target_pairs={{0,1},{1,0},{2,3},{3,2},{4,5},{5,4},{6,7},{7,6},{8,9},{9,8},{10,11... | collective-permute-start | bytes 196616 | tf_op jit(solution)/shard_map/ppermute | solution.py:424
  152.9 36.7 %collective-permute-start.25 = (bf16[128,640]{1,0:T(8,128)(2,1)S(1)}, bf16[128,640]{1,0:T(8,128)(2,1)S(1)}, u32[]{:S(2)}, u32[]{:S(2)}) collective-permute-start(bf16[128,640]{1,0:T(8,128)(2,1)S(1)} %get-tuple-element.103), channel_id=1, source_target_pairs={{0,1},{1,0},{2,3},{3,2},{4,5},{5,4},{6,7},{7,6},{8,9},{9,8},{10,11... | collective-permute-start | bytes 491528 | tf_op jit(solution)/shard_map/ppermute | solution.py:424
  154.4 37.4 %collective-permute-start.26 = (bf16[128,640]{1,0:T(8,128)(2,1)S(1)}, bf16[128,640]{1,0:T(8,128)(2,1)S(1)}, u32[]{:S(2)}, u32[]{:S(2)}) collective-permute-start(bf16[128,640]{1,0:T(8,128)(2,1)S(1)} %get-tuple-element.104), channel_id=1, source_target_pairs={{0,2},{1,3},{2,0},{3,1},{4,6},{5,7},{6,4},{7,5},{8,10},{9,11},{10,... | collective-permute-start | bytes 491528 | tf_op jit(solution)/shard_map/ppermute | solution.py:424
  (38 other events, 524.3 us)

commit v3 on v1

v3 whole, which is shorter than its diff:
```python
import jax
import jax.numpy as jnp
from jax import lax
from jax.experimental import pallas as pl
from jax.experimental.pallas import tpu as pltpu
from jax.sharding import PartitionSpec as P

HEADS = 40
KV_HEADS = 8
GROUP = HEADS // KV_HEADS
HEAD_DIM = 128
SCALE = HEAD_DIM ** (-0.5)
EXP2_SCALE = SCALE * 1.4426950408889634
QW = GROUP * HEAD_DIM
KVD = 3 * HEAD_DIM
TILE = 256
WIDE_TILE = 512
PACK_ROWS = 32
GATHER_BITS = (1, 0, 2, 3)
SEND_W = KVD + 2 * QW
BACK_W = QW + 2 * HEAD_DIM
NEAR = 4

NT = (((1,), (1,)), ((), ()))
NN = (((1,), (0,)), ((), ()))
BF16 = jnp.bfloat16
F32 = jnp.float32
ANY = pl.BlockSpec(memory_space=pl.ANY)
VMEM = pl.BlockSpec(memory_space=pltpu.VMEM)
SMEM = pl.BlockSpec(memory_space=pltpu.SMEM)


def dot(a, b, dims):
    return lax.dot_general(a, b, dims, preferred_element_type=F32)


def params(mib):
    return pltpu.CompilerParams(vmem_limit_bytes=mib * 1024 * 1024)


def times(index, size):
    return pl.multiple_of(index * size, size)


def gather_mask(index):
    return sum(((index >> step) & 1) << bit for step, bit in enumerate(GATHER_BITS))


def pack_kernel(q_ref, g_ref, o_ref, k_ref, v_ref, send_ref):
    rows = q_ref.shape[0]
    highs, lows = [], []
    for h in range(KV_HEADS):
        thin = slice(h * HEAD_DIM, (h + 1) * HEAD_DIM)
        wide = slice(h * QW, (h + 1) * QW)
        send_ref[h, :, 0:HEAD_DIM] = k_ref[:, thin]
        send_ref[h, :, HEAD_DIM : 2 * HEAD_DIM] = v_ref[:, thin]
        send_ref[h, :, KVD : KVD + QW] = q_ref[:, wide]
        send_ref[h, :, KVD + QW :] = g_ref[:, wide]
        product = g_ref[:, wide].astype(F32) * o_ref[:, wide].astype(F32)
        high = product.astype(BF16)
        highs.append(high)
        lows.append((product - high.astype(F32)).astype(BF16))
    row = lax.broadcasted_iota(jnp.int32, (QW, HEAD_DIM), 0) // HEAD_DIM
    lane = lax.broadcasted_iota(jnp.int32, (QW, HEAD_DIM), 1)
    ones = jnp.where((lane >= 3 * row) & (lane < 3 * row + 3), 1.0, 0.0).astype(BF16)
    left = dot(jnp.concatenate(highs), ones, NN) + dot(jnp.concatenate(lows), ones, NN)
    part = lax.broadcasted_iota(jnp.int32, left.shape, 1) % 3
    first = left.astype(BF16).astype(F32)
    second = (left - first).astype(BF16).astype(F32)
    third = left - first - second
    deltas = jnp.where(part == 0, first, jnp.where(part == 1, second, third)).astype(BF16)
    for h in range(KV_HEADS):
        send_ref[h, :, 2 * HEAD_DIM : KVD] = deltas[h * rows : (h + 1) * rows]


def pack(q, g, o, k, v):
    rows = q.shape[0]
    block = min(PACK_ROWS, rows)
    wide = pl.BlockSpec((block, KV_HEADS * QW), lambda i: (i, 0))
    thin = pl.BlockSpec((block, KV_HEADS * HEAD_DIM), lambda i: (i, 0))
    return pl.pallas_call(
        pack_kernel,
        grid=(rows // block,),
        in_specs=[wide, wide, wide, thin, thin],
        out_specs=pl.BlockSpec((KV_HEADS, block, SEND_W), lambda i: (0, i, 0)),
        out_shape=jax.ShapeDtypeStruct((KV_HEADS, rows, SEND_W), BF16),
        compiler_params=params(60),
        name="pack",
    )(q, g, o, k, v)


def start_all(copies, sems):
    started = [pltpu.make_async_copy(src, dst, sems.at[n]) for n, (src, dst) in enumerate(copies)]
    for copy in started:
        copy.start()
    return started


def unpack_kernel(back_ref, q_ref, k_ref, v_ref, sems):
    copies = []
    for h in range(KV_HEADS):
        thin = slice(h * HEAD_DIM, (h + 1) * HEAD_DIM)
        wide = slice(h * QW, (h + 1) * QW)
        copies.append((back_ref.at[h, :, 0:QW], q_ref.at[:, wide]))
        copies.append((back_ref.at[h, :, QW : QW + HEAD_DIM], k_ref.at[:, thin]))
        copies.append((back_ref.at[h, :, QW + HEAD_DIM :], v_ref.at[:, thin]))
    for copy in start_all(copies, sems):
        copy.wait()


def unpack(back):
    rows = back.shape[1]
    return pl.pallas_call(
        unpack_kernel,
        in_specs=[ANY],
        out_specs=[ANY] * 3,
        out_shape=[
            jax.ShapeDtypeStruct((rows, KV_HEADS * QW), BF16),
            jax.ShapeDtypeStruct((rows, KV_HEADS * HEAD_DIM), BF16),
            jax.ShapeDtypeStruct((rows, KV_HEADS * HEAD_DIM), BF16),
        ],
        scratch_shapes=[pltpu.SemaphoreType.DMA((3 * KV_HEADS,))],
        compiler_params=params(4),
        name="unpack",
    )(back)


def attend_kernel(place_ref, x_in, pkv_in, back_out, *refs):
    pg_out, refs = refs[:NEAR], refs[NEAR:]
    x_ref, pkv_ref, back_ref, pg_ref, sems, k_all, v_all, k_t, d_all, qs, gs = refs[:11]
    e_all, m_all, l_all, p_s, l_s, dq_t, dk, dv = refs[11:]
    prompt = pkv_ref.shape[0]
    slots = x_ref.shape[0]
    wide = GROUP * TILE
    heads, size, at = range(GROUP), QW, KVD
    parts = prompt // WIDE_TILE
    length, me_prefix = place_ref[0], place_ref[1]
    sources = pkv_in.shape[0]
    share = prompt // sources
    copies = [(x_in, x_ref)] + [
        (pkv_in.at[f], pkv_ref.at[pl.ds(times(me_prefix ^ gather_mask(f), share), share)])
        for f in range(sources)
    ]
    copies = start_all(copies, sems)
    back_ref[...] = jnp.zeros_like(back_ref)
    dk[...] = jnp.zeros_like(dk)
    dv[...] = jnp.zeros_like(dv)
    for copy in copies:
        copy.wait()
    k_all[0:prompt] = pkv_ref[:, 0:HEAD_DIM]
    v_all[0:prompt] = pkv_ref[:, HEAD_DIM:]
    k_all[prompt:] = x_ref[:, 0:HEAD_DIM]
    v_all[prompt:] = x_ref[:, HEAD_DIM : 2 * HEAD_DIM]
    d_all[...] = x_ref[:, 2 * HEAD_DIM : KVD]
    for t in range((prompt + slots) // TILE):
        block = slice(t * TILE, (t + 1) * TILE)
        k_t[:, block] = k_all[block].astype(F32).T.astype(BF16)

    seen = lax.broadcasted_iota(jnp.int32, (TILE, TILE), 0) <= lax.broadcasted_iota(
        jnp.int32, (TILE, TILE), 1
    )

    def lanes(j):
        return slice(j * TILE, (j + 1) * TILE)

    def select(j, size):
        lane = lax.broadcasted_iota(jnp.int32, (size, HEAD_DIM), 1)
        return jnp.where((lane >= 3 * j) & (lane < 3 * j + 3), -1.0, 0.0).astype(BF16)

    def score_tile(block, index, diagonal):
        for j in heads:
            s = dot(k_all[block], qs[lanes(j)], NT)
            if diagonal:
                s = jnp.where(seen, s, -jnp.inf)
            top = jnp.max(s, axis=0, keepdims=True)
            e = jnp.exp2((s - top) * EXP2_SCALE)
            m_all[pl.ds(index, 1), lanes(j)] = top
            l_all[pl.ds(index, 1), lanes(j)] = jnp.sum(e, axis=0, keepdims=True)
            e_all[block, lanes(j)] = e

    def grad_tile(block, keys, index, at):
        for j in heads:
            shifted = dot(
                jnp.concatenate([v_all[block], select(j, keys)], axis=1), gs[lanes(j)], NT
            )
            p = e_all[block, lanes(j)] * m_all[pl.ds(index, 1), lanes(j)]
            p_s[at : at + keys, lanes(j)] = p.astype(BF16)
            l_s[at : at + keys, lanes(j)] = (p * shifted).astype(BF16)

    def grad_sums(block, keys):
        dv[block] += dot(p_s[0:keys], gs[:, 0:HEAD_DIM], NN)
        dk[block] += dot(l_s[0:keys], qs[...], NN)
        return dot(k_t[:, block], l_s[0:keys], NN)

    def slot_block(i, carry):
        here = pl.ds(times(i, TILE), TILE)
        for j in heads:
            col = at + j * HEAD_DIM
            qs[lanes(j)] = x_ref[here, col : col + HEAD_DIM]
            gs[lanes(j), 0:HEAD_DIM] = x_ref[here, col + size : col + size + HEAD_DIM]
            gs[lanes(j), HEAD_DIM:] = d_all[here]

        def own(t):
            return pl.ds(pl.multiple_of(prompt + t * TILE, TILE), TILE)

        for t in range(parts):
            score_tile(slice(t * WIDE_TILE, (t + 1) * WIDE_TILE), t, False)
        score_tile(own(i), parts + i, True)

        def score_body(t, carry):
            score_tile(own(t), parts + t, False)
            return carry

        lax.fori_loop(0, i, score_body, 0)

        tile_index = lax.broadcasted_iota(jnp.int32, m_all.shape, 0)
        tops = jnp.where(tile_index <= parts + i, m_all[...], -jnp.inf)
        sums = jnp.where(tile_index <= parts + i, l_all[...], 0.0)
        weight = jnp.exp2((tops - jnp.max(tops, axis=0, keepdims=True)) * EXP2_SCALE)
        total = jnp.sum(weight * sums, axis=0, keepdims=True)
        slot = lax.broadcasted_iota(jnp.int32, (1, wide), 1) % TILE + i * TILE
        live = jnp.where(slot < length, 1.0, 0.0)
        m_all[...] = weight * (live / total)

        for t in range(parts):
            grad_tile(slice(t * WIDE_TILE, (t + 1) * WIDE_TILE), WIDE_TILE, t, t * WIDE_TILE)
        dq_t[...] = grad_sums(slice(0, prompt), prompt)

        def grad_body(t, carry):
            grad_tile(own(t), TILE, parts + t, 0)
            dq_t[...] += grad_sums(own(t), TILE)
            return carry

        lax.fori_loop(0, i + 1, grad_body, 0)
        for j in heads:
            back_ref[here, j * HEAD_DIM : (j + 1) * HEAD_DIM] = (
                (dq_t[:, lanes(j)] * SCALE).T.astype(BF16)
            )
        return carry

    lax.fori_loop(0, lax.div(length + TILE - 1, TILE), slot_block, 0)
    pg_ref[:, 0:HEAD_DIM] = (dk[0:prompt] * SCALE).astype(BF16)
    pg_ref[:, HEAD_DIM:] = dv[0:prompt].astype(BF16)
    back_ref[:, size : size + HEAD_DIM] = (dk[prompt:] * SCALE).astype(BF16)
    back_ref[:, size + HEAD_DIM :] = dv[prompt:].astype(BF16)
    near = me_prefix % NEAR
    copies = [
        (pg_ref.at[pl.ds(times(far * NEAR + (near ^ d), share), share)], out.at[far])
        for d, out in enumerate(pg_out)
        for far in range(sources // NEAR)
    ]
    for copy in start_all([(back_ref, back_out)] + copies, sems):
        copy.wait()


def attend(place, x, pkv):
    slots, width = x.shape
    responses, share, prompt_width = pkv.shape
    prompt = responses * share
    keys = slots + prompt
    wide = GROUP * TILE
    part = ((responses // NEAR, share, prompt_width), BF16)
    outs = [((slots, BACK_W), BF16)] + [part] * NEAR
    return pl.pallas_call(
        attend_kernel,
        in_specs=[SMEM, ANY, ANY],
        out_specs=[ANY] * len(outs),
        out_shape=[jax.ShapeDtypeStruct(shape, dtype) for shape, dtype in outs],
        scratch_shapes=[
            pltpu.VMEM((slots, width), BF16),
            pltpu.VMEM((prompt, prompt_width), BF16),
            pltpu.VMEM((slots, BACK_W), BF16),
            pltpu.VMEM((prompt, prompt_width), BF16),
            pltpu.SemaphoreType.DMA((1 + responses,)),
            pltpu.VMEM((keys, HEAD_DIM), BF16),
            pltpu.VMEM((keys, HEAD_DIM), BF16),
            pltpu.VMEM((HEAD_DIM, keys), BF16),
            pltpu.VMEM((slots, HEAD_DIM), BF16),
            pltpu.VMEM((wide, HEAD_DIM), BF16),
            pltpu.VMEM((wide, 2 * HEAD_DIM), BF16),
            pltpu.VMEM((keys, wide), F32),
            pltpu.VMEM((8, wide), F32),
            pltpu.VMEM((8, wide), F32),
            pltpu.VMEM((prompt, wide), BF16),
            pltpu.VMEM((prompt, wide), BF16),
            pltpu.VMEM((HEAD_DIM, wide), F32),
            pltpu.VMEM((keys, HEAD_DIM), F32),
            pltpu.VMEM((keys, HEAD_DIM), F32),
        ],
        compiler_params=params(44),
        cost_estimate=pl.CostEstimate(
            flops=10 * slots * keys * QW, transcendentals=0, bytes_accessed=8 * slots * QW
        ),
        name="attend",
    )(place, x, pkv)


def near_kernel(place_ref, *refs):
    parts, outs, total = refs[:NEAR], refs[NEAR:-1], refs[-1]
    value = parts[0][...].astype(F32)
    for part in parts[1:]:
        value = value + part[...].astype(F32)
    total[...] = value
    for d, out in enumerate(outs):
        out[...] = total[(place_ref[1] // NEAR) ^ d]


def sum_near(place, parts):
    far, share, width = parts[0].shape
    return pl.pallas_call(
        near_kernel,
        in_specs=[SMEM] + [VMEM] * NEAR,
        out_specs=[VMEM] * far,
        out_shape=[jax.ShapeDtypeStruct((share, width), F32)] * far,
        scratch_shapes=[pltpu.VMEM((far, share, width), F32)],
        compiler_params=params(4),
        cost_estimate=pl.CostEstimate(flops=5 * 10**10, transcendentals=0, bytes_accessed=2**20),
        name="sum_near",
    )(place, *parts)


def swap(value, axis, d):
    return lax.ppermute(value, axis, [(i, i ^ d) for i in range(lax.axis_size(axis))])


def local(
    resp_query,
    resp_keys,
    resp_values,
    resp_out,
    resp_grad,
    prompt_keys,
    prompt_values,
    resp_lengths,
):
    head = lax.axis_index("resp")
    responses = lax.axis_size("prefix")
    rows = resp_query.shape[1]
    place = jnp.stack([resp_lengths[0], lax.axis_index("prefix")])
    cut = lambda a: lax.dynamic_slice_in_dim(a, head * HEAD_DIM, HEAD_DIM, 1)
    pkv = jnp.concatenate([cut(prompt_keys), cut(prompt_values)], axis=1)[None]
    first = swap(pkv, "prefix", 1 << GATHER_BITS[0])
    send = pack(resp_query[0], resp_grad[0], resp_out[0], resp_keys[0], resp_values[0])
    x = lax.all_to_all(send, "resp", 0, 0, tiled=True)
    pkv, first, _ = lax.optimization_barrier((pkv, first, send))
    pkv = jnp.concatenate([pkv, first])
    for bit in GATHER_BITS[1:]:
        pkv = jnp.concatenate([pkv, swap(pkv, "prefix", 1 << bit)])
    outs = attend(place, x.reshape(KV_HEADS * rows, SEND_W), pkv)
    back, parts = outs[0], outs[1:]
    back = lax.all_to_all(back.reshape(KV_HEADS, rows, BACK_W), "resp", 0, 0, tiled=True)
    parts = [parts[0]] + [swap(parts[d], "prefix", d) for d in range(1, NEAR)]
    parts = sum_near(place, parts)
    parts = [parts[0]] + [swap(parts[d], "prefix", NEAR * d) for d in range(1, len(parts))]
    share, width = parts[0].shape
    total = sum(parts[1:], parts[0]).astype(BF16).reshape(KV_HEADS, share // KV_HEADS, width)
    back, total = lax.optimization_barrier((back, total))
    total = lax.all_to_all(total, "resp", 0, 0, tiled=True)
    total = total.reshape(KV_HEADS, share // KV_HEADS, 2, HEAD_DIM).transpose(2, 1, 0, 3)
    total = total.reshape(2, share // KV_HEADS, KV_HEADS * HEAD_DIM)
    grad_query, grad_keys, grad_values = unpack(back)
    return (grad_query[None], grad_keys[None], grad_values[None], total[0], total[1])


def solution(mesh):
    return jax.shard_map(
        local,
        mesh=mesh,
        in_specs=(
            P("prefix", "resp", None),
            P("prefix", "resp", None),
            P("prefix", "resp", None),
            P("prefix", "resp", None),
            P("prefix", "resp", None),
            P("prefix", None),
            P("prefix", None),
            P("prefix"),
        ),
        out_specs=(
            P("prefix", "resp", None),
            P("prefix", "resp", None),
            P("prefix", "resp", None),
            P(("prefix", "resp"), None),
            P(("prefix", "resp"), None),
        ),
        check_vma=False,
    )
```

time: 164 us -> 152 us (0.927)
  blocking collectives: 33.8 us -> 0 us
  starting transfers between devices: 16.1 us -> 30.5 us
  waiting for transfers between devices: 66.5 us -> 71.3 us
  Pallas kernels: 38.9 us -> 42.3 us
    ppermute x0 -> x10, waiting for transfers between devices: none -> 54.2 us  [swap(): lax.ppermute(value, axis, [(i, i ^ d) for i in range(lax.axis_size(axis))])]
    all_to_all x1, waiting for transfers between devices: 39.9 us -> 0.01 us  [local(): x = lax.all_to_all(send, 'resp', 0, 0, tiled=True)]
    all_to_all x2 -> x0, blocking collectives: 33.8 us -> none  [the longest x1 25 us: local(): lax.all_to_all(pg.reshape(responses, part, width), 'prefix', 0, 0, tiled=...]
    ppermute x0 -> x10, starting transfers between devices: none -> 16.4 us  [swap(): lax.ppermute(value, axis, [(i, i ^ d) for i in range(lax.axis_size(axis))])]
    all_to_all x1, waiting for transfers between devices: 21.9 us -> 12.3 us  [local(): lax.all_to_all(back.reshape(KV_HEADS, rows, BACK_W), 'resp', 0, 0, tiled=...]
    all_to_all x1, starting transfers between devices: 7.96 us -> 3.33 us  [local(): total = lax.all_to_all(total, 'resp', 0, 0, tiled=True)]
    pallas_call x3 -> x4, Pallas kernels: 38.9 us -> 42.3 us  [the longest x1 34.8 us: attend(): pl.pallas_call(attend_kernel, in_specs=[SMEM, ANY, ANY], out_specs=[ANY]...]
    all_to_all x1, starting transfers between devices: 3.59 us -> 5.3 us  [local(): lax.all_to_all(back.reshape(KV_HEADS, rows, BACK_W), 'resp', 0, 0, tiled=...]
  transfers between devices with their start and end apart: 3 -> 13, of which waited for: 3 -> 9; matrix products, arithmetic and copies ran while one was open for 0% -> 1% of each run, Pallas kernels for 5% -> 1%
where the time goes in v3:
time: 152 us
  waiting for transfers between devices  71.3 us (47%)
  Pallas kernels  42.3 us (28%)
  starting transfers between devices  30.5 us (20%)
  local copies, waits for them, and re-layouts  5.14 us (3%)
    ppermute x10, waiting for transfers between devices, swap(): lax.ppermute(value, axis, [(i, i ^ d) for i in range(lax.axis_size(axis))])  54.2 us
    pallas_call x1, Pallas kernels, attend(): pl.pallas_call(attend_kernel, in_specs=[SMEM, ANY, ANY], out_specs=[ANY]...  34.8 us
    ppermute x10, starting transfers between devices, swap(): lax.ppermute(value, axis, [(i, i ^ d) for i in range(lax.axis_size(axis))])  16.4 us
    all_to_all x1, waiting for transfers between devices, local(): lax.all_to_all(back.reshape(KV_HEADS, rows, BACK_W), 'resp', 0, 0, tiled=...  12.3 us
    all_to_all x1, starting transfers between devices, local(): x = lax.all_to_all(send, 'resp', 0, 0, tiled=True)  5.48 us
    pallas_call x1, Pallas kernels, pack(): pl.pallas_call(pack_kernel, grid=(rows // block,), in_specs=[wide, wide,...  5.43 us
    all_to_all x1, starting transfers between devices, local(): lax.all_to_all(back.reshape(KV_HEADS, rows, BACK_W), 'resp', 0, 0, tiled=...  5.3 us
    all_to_all x1, waiting for transfers between devices, local(): total = lax.all_to_all(total, 'resp', 0, 0, tiled=True)  4.76 us
  transfers between devices with their start and end apart: 13, of which 9 were waited for; matrix products, arithmetic and copies ran while one was open for 1% of the time, Pallas kernels for 1%

profile of v3, /device:TPU:0, one launch (start us, length us, event | category | flops | bytes accessed | tf_op | source)
XLA Modules:
  0.0 151.9 jit_solution(5365051582718472791)
XLA Ops:
  0.6 5.4 %pack.1 = bf16[8,128,1664]{2,1,0:T(8,128)(2,1)} custom-call(bf16[128,5120]{1,0:T(8,128)(2,1)} %bitcast.26, bf16[128,5120]{1,0:T(8,128)(2,1)} %bitcast.27, bf16[128,5120]{1,0:T(8,128)(2,1)} %bitcast.28, bf16[128,1024]{1,0:T(8,128)(2,1)} %bitcast.29, bf16[128,1024]{1,0:T(8,128)(2,1)} %bitcast.30), custom_call_target="tpu_custom_call" | custom-call | tf_op jit(solution)/shard_map/pack/pallas_call | solution.py:81
  6.1 5.5 %all-to-all-start = ((bf16[8,128,1664]{2,1,0:T(8,128)(2,1)}), bf16[8,128,1664]{2,1,0:T(8,128)(2,1)S(1)}, u32[]{:S(2)}, u32[]{:S(2)}) async-start(bf16[8,128,1664]{2,1,0:T(8,128)(2,1)} %pack.1), calls=%async_computation | async-start | bytes 6815744 | tf_op jit(solution)/shard_map/all_to_all | solution.py:344
  12.3 2.8 %collective-permute-start = (bf16[1,64,256]{2,1,0:T(8,128)(2,1)S(1)}, bf16[1,64,256]{2,1,0:T(8,128)(2,1)S(1)}, u32[]{:S(2)}, u32[]{:S(2)}) collective-permute-start(bf16[1,64,256]{2,1,0:T(8,128)(2,1)S(1)} %maximum_bitcast_fusion), channel_id=1, source_target_pairs={{0,16},{8,24},{16,0},{24,8},{32,48},{40,56},{48,32},{56,40},{64,80... | collective-permute-start | bytes 98312 | tf_op jit(solution)/shard_map/ppermute | solution.py:323
  15.1 37.3 %collective-permute-done = bf16[1,64,256]{2,1,0:T(8,128)(2,1)S(1)} collective-permute-done((bf16[1,64,256]{2,1,0:T(8,128)(2,1)S(1)}, bf16[1,64,256]{2,1,0:T(8,128)(2,1)S(1)}, u32[]{:S(2)}, u32[]{:S(2)}) %collective-permute-start) | collective-permute-done | bytes 32800 | tf_op jit(solution)/shard_map/ppermute | solution.py:323
  53.7 0.8 collective-permute-done.1
  54.6 2.0 %collective-permute-start.2 = (bf16[4,64,256]{2,1,0:T(8,128)(2,1)S(1)}, bf16[4,64,256]{2,1,0:T(8,128)(2,1)S(1)}, u32[]{:S(2)}, u32[]{:S(2)}) collective-permute-start(bf16[4,64,256]{2,1,0:T(8,128)(2,1)S(1)} %pad_maximum_fusion.1), channel_id=1, source_target_pairs={{0,32},{8,40},{16,48},{24,56},{32,0},{40,8},{48,16},{56,24},{64,96... | collective-permute-start | bytes 393224 | tf_op jit(solution)/shard_map/ppermute | solution.py:323
  56.6 3.7 %collective-permute-done.2 = bf16[4,64,256]{2,1,0:T(8,128)(2,1)S(1)} collective-permute-done((bf16[4,64,256]{2,1,0:T(8,128)(2,1)S(1)}, bf16[4,64,256]{2,1,0:T(8,128)(2,1)S(1)}, u32[]{:S(2)}, u32[]{:S(2)}) %collective-permute-start.2) | collective-permute-done | bytes 131104 | tf_op jit(solution)/shard_map/ppermute | solution.py:323
  60.4 3.8 %collective-permute-start.3 = (bf16[8,64,256]{2,1,0:T(8,128)(2,1)S(1)}, bf16[8,64,256]{2,1,0:T(8,128)(2,1)S(1)}, u32[]{:S(2)}, u32[]{:S(2)}) collective-permute-start(bf16[8,64,256]{2,1,0:T(8,128)(2,1)S(1)} %pad_maximum_fusion), channel_id=1, source_target_pairs={{0,64},{8,72},{16,80},{24,88},{32,96},{40,104},{48,112},{56,120},{... | collective-permute-start | bytes 786440 | tf_op jit(solution)/shard_map/ppermute | solution.py:323
  64.2 5.8 %collective-permute-done.3 = bf16[8,64,256]{2,1,0:T(8,128)(2,1)S(1)} collective-permute-done((bf16[8,64,256]{2,1,0:T(8,128)(2,1)S(1)}, bf16[8,64,256]{2,1,0:T(8,128)(2,1)S(1)}, u32[]{:S(2)}, u32[]{:S(2)}) %collective-permute-start.3) | collective-permute-done | bytes 262176 | tf_op jit(solution)/shard_map/ppermute | solution.py:323
  70.0 0.8 copy-done.1
  70.8 1.0 copy-done.2
  71.8 34.8 %attend.1 = (bf16[1024,896]{1,0:T(8,128)(2,1)S(1)}, bf16[4,64,256]{2,1,0:T(8,128)(2,1)S(1)}, bf16[4,64,256]{2,1,0:T(8,128)(2,1)}, bf16[4,64,256]{2,1,0:T(8,128)(2,1)}, bf16[4,64,256]{2,1,0:T(8,128)(2,1)S(1)}) custom-call(s32[2]{0:T(128)S(1)} %pad_add_fusion.place_ref, bf16[1024,1664]{1,0:T(8,128)(2,1)S(1)} %bitcast.24, bf16[16,64,256]{2,1,0:T(8,128)(2,1)S(1)} %copy-done.2), custom_call_target="tpu_custom_call" | custom-call | flops 13421772800 | bytes 5242880 | tf_op jit(solution)/shard_map/attend/pallas_call | solution.py:264
  106.6 1.3 copy-done
  108.6 3.4 %collective-permute-start.6 = (bf16[4,64,256]{2,1,0:T(8,128)(2,1)S(1)}, bf16[4,64,256]{2,1,0:T(8,128)(2,1)S(1)}, u32[]{:S(2)}, u32[]{:S(2)}) collective-permute-start(bf16[4,64,256]{2,1,0:T(8,128)(2,1)S(1)} %get-tuple-element.27), channel_id=1, source_target_pairs={{0,24},{8,16},{16,8},{24,0},{32,56},{40,48},{48,40},{56,32},{64,88... | collective-permute-start | bytes 393224 | tf_op jit(solution)/shard_map/ppermute | solution.py:323
  111.9 5.3 %all-to-all-start.1 = ((bf16[8,128,896]{2,1,0:T(8,128)(2,1)}), bf16[8,128,896]{2,1,0:T(8,128)(2,1)S(1)}, u32[]{:S(2)}, u32[]{:S(2)}) async-start(bf16[8,128,896]{2,1,0:T(8,128)(2,1)} %bitcast.25), calls=%async_computation.1 | async-start | bytes 3670016 | tf_op jit(solution)/shard_map/all_to_all | solution.py:351
  117.2 1.4 collective-permute-done.6.refs_3_
  119.2 3.5 %collective-permute-start.9 = (f32[64,256]{1,0:T(8,128)S(1)}, f32[64,256]{1,0:T(8,128)S(1)}, u32[]{:S(2)}, u32[]{:S(2)}) collective-permute-start(f32[64,256]{1,0:T(8,128)S(1)} %get-tuple-element.31), channel_id=1, source_target_pairs={{0,96},{8,104},{16,112},{24,120},{32,64},{40,72},{48,80},{56,88},{... | collective-permute-start | bytes 196616 | tf_op jit(solution)/shard_map/ppermute | solution.py:323
  122.7 0.9 collective-permute-start.7
  123.7 2.2 %collective-permute-done.9 = f32[64,256]{1,0:T(8,128)S(1)} collective-permute-done((f32[64,256]{1,0:T(8,128)S(1)}, f32[64,256]{1,0:T(8,128)S(1)}, u32[]{:S(2)}, u32[]{:S(2)}) %collective-permute-start.9) | collective-permute-done | bytes 65568 | tf_op jit(solution)/shard_map/ppermute | solution.py:323
  125.9 3.0 %collective-permute-done.8 = f32[64,256]{1,0:T(8,128)S(1)} collective-permute-done((f32[64,256]{1,0:T(8,128)S(1)}, f32[64,256]{1,0:T(8,128)S(1)}, u32[]{:S(2)}, u32[]{:S(2)}) %collective-permute-start.8) | collective-permute-done | bytes 65568 | tf_op jit(solution)/shard_map/ppermute | solution.py:323
  129.5 12.3 %all-to-all-done.1.back_ref = bf16[8,128,896]{2,1,0:T(8,128)(2,1)S(1)} async-done(((bf16[8,128,896]{2,1,0:T(8,128)(2,1)}), bf16[8,128,896]{2,1,0:T(8,128)(2,1)S(1)}, u32[]{:S(2)}, u32[]{:S(2)}) %all-to-all-start.1) | async-done | bytes 1835040 | tf_op jit(solution)/shard_map/all_to_all | solution.py:351
  141.8 3.3 %all-to-all-start.2 = ((bf16[8,8,256]{2,1,0:T(8,128)(2,1)}), bf16[8,8,256]{2,1,0:T(8,128)(2,1)S(1)}, u32[]{:S(2)}, u32[]{:S(2)}) async-start(bf16[8,8,256]{2,1,0:T(8,128)(2,1)} %fusion), calls=%async_computation.2 | async-start | bytes 65536 | tf_op jit(solution)/shard_map/all_to_all | solution.py:358
  145.1 1.4 unpack.1
  146.6 4.8 %all-to-all-done.2 = bf16[8,8,256]{2,1,0:T(8,128)(2,1)S(1)} async-done(((bf16[8,8,256]{2,1,0:T(8,128)(2,1)}), bf16[8,8,256]{2,1,0:T(8,128)(2,1)S(1)}, u32[]{:S(2)}, u32[]{:S(2)}) %all-to-all-start.2) | async-done | bytes 32800 | tf_op jit(solution)/shard_map/all_to_all | solution.py:358
  (30 shorter events, 4.1 us)
Async XLA Ops:
  6.1 64.7 %all-to-all-start = ((bf16[8,128,1664]{2,1,0:T(8,128)(2,1)}), bf16[8,128,1664]{2,1,0:T(8,128)(2,1)S(1)}, u32[]{:S(2)}, u32[]{:S(2)}) async-start(bf16[8,128,1664]{2,1,0:T(8,128)(2,1)} %pack.1), calls=%async_computation | async-start | bytes 6815744 | tf_op jit(solution)/shard_map/all_to_all | solution.py:344
  12.3 40.1 %collective-permute-start = (bf16[1,64,256]{2,1,0:T(8,128)(2,1)S(1)}, bf16[1,64,256]{2,1,0:T(8,128)(2,1)S(1)}, u32[]{:S(2)}, u32[]{:S(2)}) collective-permute-start(bf16[1,64,256]{2,1,0:T(8,128)(2,1)S(1)} %maximum_bitcast_fusion), channel_id=1, source_target_pairs={{0,16},{8,24},{16,0},{24,8},{32,48},{40,56},{48,32},{56,40},{64,80... | collective-permute-start | bytes 98312 | tf_op jit(solution)/shard_map/ppermute | solution.py:323
  53.1 1.5 collective-permute-start.1
  54.6 5.8 %collective-permute-start.2 = (bf16[4,64,256]{2,1,0:T(8,128)(2,1)S(1)}, bf16[4,64,256]{2,1,0:T(8,128)(2,1)S(1)}, u32[]{:S(2)}, u32[]{:S(2)}) collective-permute-start(bf16[4,64,256]{2,1,0:T(8,128)(2,1)S(1)} %pad_maximum_fusion.1), channel_id=1, source_target_pairs={{0,32},{8,40},{16,48},{24,56},{32,0},{40,8},{48,16},{56,24},{64,96... | collective-permute-start | bytes 393224 | tf_op jit(solution)/shard_map/ppermute | solution.py:323
  60.4 9.6 %collective-permute-start.3 = (bf16[8,64,256]{2,1,0:T(8,128)(2,1)S(1)}, bf16[8,64,256]{2,1,0:T(8,128)(2,1)S(1)}, u32[]{:S(2)}, u32[]{:S(2)}) collective-permute-start(bf16[8,64,256]{2,1,0:T(8,128)(2,1)S(1)} %pad_maximum_fusion), channel_id=1, source_target_pairs={{0,64},{8,72},{16,80},{24,88},{32,96},{40,104},{48,112},{56,120},{... | collective-permute-start | bytes 786440 | tf_op jit(solution)/shard_map/ppermute | solution.py:323
  70.0 0.8 copy-start.1
  70.8 1.0 copy-start.2
  106.6 1.3 copy-start
  107.9 0.7 copy-start.3
  108.5 8.7 %collective-permute-start.4 = (bf16[4,64,256]{2,1,0:T(8,128)(2,1)}, bf16[4,64,256]{2,1,0:T(8,128)(2,1)S(1)}, u32[]{:S(2)}, u32[]{:S(2)}) collective-permute-start(bf16[4,64,256]{2,1,0:T(8,128)(2,1)} %get-tuple-element.25), channel_id=1, source_target_pairs={{0,8},{8,0},{16,24},{24,16},{32,40},{40,32},{48,56},{56,48},{64,72... | collective-permute-start | bytes 393224 | tf_op jit(solution)/shard_map/ppermute | solution.py:323
  108.5 8.7 %collective-permute-start.5 = (bf16[4,64,256]{2,1,0:T(8,128)(2,1)}, bf16[4,64,256]{2,1,0:T(8,128)(2,1)S(1)}, u32[]{:S(2)}, u32[]{:S(2)}) collective-permute-start(bf16[4,64,256]{2,1,0:T(8,128)(2,1)} %get-tuple-element.26), channel_id=1, source_target_pairs={{0,16},{8,24},{16,0},{24,8},{32,48},{40,56},{48,32},{56,40},{64,80... | collective-permute-start | bytes 393224 | tf_op jit(solution)/shard_map/ppermute | solution.py:323
  108.6 10.0 %collective-permute-start.6 = (bf16[4,64,256]{2,1,0:T(8,128)(2,1)S(1)}, bf16[4,64,256]{2,1,0:T(8,128)(2,1)S(1)}, u32[]{:S(2)}, u32[]{:S(2)}) collective-permute-start(bf16[4,64,256]{2,1,0:T(8,128)(2,1)S(1)} %get-tuple-element.27), channel_id=1, source_target_pairs={{0,24},{8,16},{16,8},{24,0},{32,56},{40,48},{48,40},{56,32},{64,88... | collective-permute-start | bytes 393224 | tf_op jit(solution)/shard_map/ppermute | solution.py:323
  111.9 6.7 %copy-start.4 = (bf16[4,64,256]{2,1,0:T(8,128)(2,1)S(1)}, bf16[4,64,256]{2,1,0:T(8,128)(2,1)}, u32[]{:S(2)}) copy-start(bf16[4,64,256]{2,1,0:T(8,128)(2,1)} %copy-done.3) | copy-start | bytes 393220
  111.9 29.9 %all-to-all-start.1 = ((bf16[8,128,896]{2,1,0:T(8,128)(2,1)}), bf16[8,128,896]{2,1,0:T(8,128)(2,1)S(1)}, u32[]{:S(2)}, u32[]{:S(2)}) async-start(bf16[8,128,896]{2,1,0:T(8,128)(2,1)} %bitcast.25), calls=%async_computation.1 | async-start | bytes 3670016 | tf_op jit(solution)/shard_map/all_to_all | solution.py:351
  119.2 6.6 %collective-permute-start.9 = (f32[64,256]{1,0:T(8,128)S(1)}, f32[64,256]{1,0:T(8,128)S(1)}, u32[]{:S(2)}, u32[]{:S(2)}) collective-permute-start(f32[64,256]{1,0:T(8,128)S(1)} %get-tuple-element.31), channel_id=1, source_target_pairs={{0,96},{8,104},{16,112},{24,120},{32,64},{40,72},{48,80},{56,88},{... | collective-permute-start | bytes 196616 | tf_op jit(solution)/shard_map/ppermute | solution.py:323
  122.7 6.1 %collective-permute-start.8 = (f32[64,256]{1,0:T(8,128)S(1)}, f32[64,256]{1,0:T(8,128)S(1)}, u32[]{:S(2)}, u32[]{:S(2)}) collective-permute-start(f32[64,256]{1,0:T(8,128)S(1)} %get-tuple-element.30), channel_id=1, source_target_pairs={{0,64},{8,72},{16,80},{24,88},{32,96},{40,104},{48,112},{56,120},{... | collective-permute-start | bytes 196616 | tf_op jit(solution)/shard_map/ppermute | solution.py:323
  122.7 6.1 %collective-permute-start.7 = (f32[64,256]{1,0:T(8,128)S(1)}, f32[64,256]{1,0:T(8,128)S(1)}, u32[]{:S(2)}, u32[]{:S(2)}) collective-permute-start(f32[64,256]{1,0:T(8,128)S(1)} %get-tuple-element.29), channel_id=1, source_target_pairs={{0,32},{8,40},{16,48},{24,56},{32,0},{40,8},{48,16},{56,24},{64,96... | collective-permute-start | bytes 196616 | tf_op jit(solution)/shard_map/ppermute | solution.py:323
  141.8 9.5 %all-to-all-start.2 = ((bf16[8,8,256]{2,1,0:T(8,128)(2,1)}), bf16[8,8,256]{2,1,0:T(8,128)(2,1)S(1)}, u32[]{:S(2)}, u32[]{:S(2)}) async-start(bf16[8,8,256]{2,1,0:T(8,128)(2,1)} %fusion), calls=%async_computation.2 | async-start | bytes 65536 | tf_op jit(solution)/shard_map/all_to_all | solution.py:358

commit v4 on v3

--- a/solution.py
+++ b/solution.py
@@ -21,11 +21,11 @@
 BACK_W = QW + 2 * HEAD_DIM
 NEAR = 4
 
-NT = (((1,), (1,)), ((), ()))
 NN = (((1,), (0,)), ((), ()))
 BF16 = jnp.bfloat16
 F32 = jnp.float32
 ANY = pl.BlockSpec(memory_space=pl.ANY)
+HBM = pl.BlockSpec(memory_space=pltpu.HBM)
 VMEM = pl.BlockSpec(memory_space=pltpu.VMEM)
 SMEM = pl.BlockSpec(memory_space=pltpu.SMEM)
 
@@ -85,6 +85,7 @@
         out_specs=pl.BlockSpec((KV_HEADS, block, SEND_W), lambda i: (0, i, 0)),
         out_shape=jax.ShapeDtypeStruct((KV_HEADS, rows, SEND_W), BF16),
         compiler_params=params(60),
+        cost_estimate=pl.CostEstimate(flops=10**10, transcendentals=0, bytes_accessed=2**23),
         name="pack",
     )(q, g, o, k, v)
 
@@ -125,20 +126,21 @@
     )(back)
 
 
-def attend_kernel(place_ref, x_in, pkv_in, back_out, *refs):
+def attend_kernel(place_ref, x_in, pkv_low, pkv_high, back_out, *refs):
     pg_out, refs = refs[:NEAR], refs[NEAR:]
-    x_ref, pkv_ref, back_ref, pg_ref, sems, k_all, v_all, k_t, d_all, qs, gs = refs[:11]
-    e_all, m_all, l_all, p_s, l_s, dq_t, dk, dv = refs[11:]
+    x_ref, pkv_ref, back_ref, pg_ref, sems, k_all, v_all, k_t, d_all, qs, gs, qs_t, gs_t = refs[:13]
+    e_all, m_all, l_all, p_s, l_s, dq_t, dk, dv = refs[13:]
     prompt = pkv_ref.shape[0]
     slots = x_ref.shape[0]
     wide = GROUP * TILE
     heads, size, at = range(GROUP), QW, KVD
     parts = prompt // WIDE_TILE
     length, me_prefix = place_ref[0], place_ref[1]
-    sources = pkv_in.shape[0]
+    half = pkv_low.shape[0]
+    sources = 2 * half
     share = prompt // sources
     copies = [(x_in, x_ref)] + [
-        (pkv_in.at[f], pkv_ref.at[pl.ds(times(me_prefix ^ gather_mask(f), share), share)])
+        ((pkv_low, pkv_high)[f // half].at[f % half], pkv_ref.at[pl.ds(times(me_prefix ^ gather_mask(f), share), share)])
         for f in range(sources)
     ]
     copies = start_all(copies, sems)
@@ -160,6 +162,9 @@
         jnp.int32, (TILE, TILE), 1
     )
 
+    def flip(a):
+        return a.astype(F32).T.astype(BF16)
+
     def lanes(j):
         return slice(j * TILE, (j + 1) * TILE)
 
@@ -169,7 +174,7 @@
 
     def score_tile(block, index, diagonal):
         for j in heads:
-            s = dot(k_all[block], qs[lanes(j)], NT)
+            s = dot(k_all[block], qs_t[:, lanes(j)], NN)
             if diagonal:
                 s = jnp.where(seen, s, -jnp.inf)
             top = jnp.max(s, axis=0, keepdims=True)
@@ -181,24 +186,29 @@
     def grad_tile(block, keys, index, at):
         for j in heads:
             shifted = dot(
-                jnp.concatenate([v_all[block], select(j, keys)], axis=1), gs[lanes(j)], NT
+                jnp.concatenate([v_all[block], select(j, keys)], axis=1), gs_t[:, lanes(j)], NN
             )
             p = e_all[block, lanes(j)] * m_all[pl.ds(index, 1), lanes(j)]
             p_s[at : at + keys, lanes(j)] = p.astype(BF16)
             l_s[at : at + keys, lanes(j)] = (p * shifted).astype(BF16)
 
     def grad_sums(block, keys):
-        dv[block] += dot(p_s[0:keys], gs[:, 0:HEAD_DIM], NN)
+        dv[block] += dot(p_s[0:keys], gs[...], NN)
         dk[block] += dot(l_s[0:keys], qs[...], NN)
         return dot(k_t[:, block], l_s[0:keys], NN)
 
     def slot_block(i, carry):
         here = pl.ds(times(i, TILE), TILE)
+        delta_t = flip(d_all[here])
         for j in heads:
             col = at + j * HEAD_DIM
-            qs[lanes(j)] = x_ref[here, col : col + HEAD_DIM]
-            gs[lanes(j), 0:HEAD_DIM] = x_ref[here, col + size : col + size + HEAD_DIM]
-            gs[lanes(j), HEAD_DIM:] = d_all[here]
+            q = x_ref[here, col : col + HEAD_DIM]
+            g = x_ref[here, col + size : col + size + HEAD_DIM]
+            qs[lanes(j)] = q
+            gs[lanes(j)] = g
+            qs_t[:, lanes(j)] = flip(q)
+            gs_t[0:HEAD_DIM, lanes(j)] = flip(g)
+            gs_t[HEAD_DIM:, lanes(j)] = delta_t
 
         def own(t):
             return pl.ds(pl.multiple_of(prompt + t * TILE, TILE), TILE)
@@ -255,7 +265,8 @@
 
 def attend(place, x, pkv):
     slots, width = x.shape
-    responses, share, prompt_width = pkv.shape
+    half, share, prompt_width = pkv[0].shape
+    responses = 2 * half
     prompt = responses * share
     keys = slots + prompt
     wide = GROUP * TILE
@@ -263,8 +274,8 @@
     outs = [((slots, BACK_W), BF16)] + [part] * NEAR
     return pl.pallas_call(
         attend_kernel,
-        in_specs=[SMEM, ANY, ANY],
-        out_specs=[ANY] * len(outs),
+        in_specs=[SMEM, ANY, ANY, ANY],
+        out_specs=[HBM] * len(outs),
         out_shape=[jax.ShapeDtypeStruct(shape, dtype) for shape, dtype in outs],
         scratch_shapes=[
             pltpu.VMEM((slots, width), BF16),
@@ -277,7 +288,9 @@
             pltpu.VMEM((HEAD_DIM, keys), BF16),
             pltpu.VMEM((slots, HEAD_DIM), BF16),
             pltpu.VMEM((wide, HEAD_DIM), BF16),
-            pltpu.VMEM((wide, 2 * HEAD_DIM), BF16),
+            pltpu.VMEM((wide, HEAD_DIM), BF16),
+            pltpu.VMEM((HEAD_DIM, wide), BF16),
+            pltpu.VMEM((2 * HEAD_DIM, wide), BF16),
             pltpu.VMEM((keys, wide), F32),
             pltpu.VMEM((8, wide), F32),
             pltpu.VMEM((8, wide), F32),
@@ -292,7 +305,7 @@
             flops=10 * slots * keys * QW, transcendentals=0, bytes_accessed=8 * slots * QW
         ),
         name="attend",
-    )(place, x, pkv)
+    )(place, x, *pkv)
 
 
 def near_kernel(place_ref, *refs):
@@ -341,11 +354,12 @@
     pkv = jnp.concatenate([cut(prompt_keys), cut(prompt_values)], axis=1)[None]
     first = swap(pkv, "prefix", 1 << GATHER_BITS[0])
     send = pack(resp_query[0], resp_grad[0], resp_out[0], resp_keys[0], resp_values[0])
+    pkv, first, send = lax.optimization_barrier((pkv, first, send))
     x = lax.all_to_all(send, "resp", 0, 0, tiled=True)
-    pkv, first, _ = lax.optimization_barrier((pkv, first, send))
     pkv = jnp.concatenate([pkv, first])
-    for bit in GATHER_BITS[1:]:
+    for bit in GATHER_BITS[1:-1]:
         pkv = jnp.concatenate([pkv, swap(pkv, "prefix", 1 << bit)])
+    pkv = [pkv, swap(pkv, "prefix", 1 << GATHER_BITS[-1])]
     outs = attend(place, x.reshape(KV_HEADS * rows, SEND_W), pkv)
     back, parts = outs[0], outs[1:]
     back = lax.all_to_all(back.reshape(KV_HEADS, rows, BACK_W), "resp", 0, 0, tiled=True)

time: 152 us -> 134 us (0.88)
  the two profiles are of different devices: /device:TPU:0 before, /device:TPU:100 now
where the time goes in v4:
time: 134 us; the launch traced here: 133 us
  waiting for transfers between devices  59.9 us (45%)
  Pallas kernels  42 us (31%)
  starting transfers between devices  22.9 us (17%)
  local copies, waits for them, and re-layouts  5.82 us (4%)
  between operations  1.38 us (1%)
    pallas_call x1, Pallas kernels, attend(): pl.pallas_call(attend_kernel, in_specs=[SMEM, ANY, ANY, ANY], out_specs=[...  34.5 us
    all_to_all x1, waiting for transfers between devices, local(): x = lax.all_to_all(send, 'resp', 0, 0, tiled=True)  23.7 us
    ppermute x10, waiting for transfers between devices, swap(): lax.ppermute(value, axis, [(i, i ^ d) for i in range(lax.axis_size(axis))])  18.4 us
    all_to_all x1, waiting for transfers between devices, local(): lax.all_to_all(back.reshape(KV_HEADS, rows, BACK_W), 'resp', 0, 0, tiled=...  12.9 us
    ppermute x10, starting transfers between devices, swap(): lax.ppermute(value, axis, [(i, i ^ d) for i in range(lax.axis_size(axis))])  9.84 us
    all_to_all x1, starting transfers between devices, local(): x = lax.all_to_all(send, 'resp', 0, 0, tiled=True)  6.01 us
    pallas_call x1, Pallas kernels, pack(): pl.pallas_call(pack_kernel, grid=(rows // block,), in_specs=[wide, wide,...  5.43 us
    all_to_all x1, waiting for transfers between devices, local(): total = lax.all_to_all(total, 'resp', 0, 0, tiled=True)  4.76 us
  transfers between devices with their start and end apart: 13, of which 11 were waited for; matrix products, arithmetic and copies ran while one was open for 2% of the time, Pallas kernels for 6%

profile of v4, /device:TPU:100, one launch (start us, length us, event | category | flops | bytes accessed | tf_op | source)
XLA Modules:
  0.0 132.7 jit_solution(13570084471078867216)
XLA Ops:
  0.6 0.7 constant_dynamic-slice_fusion
  2.0 5.4 %pack.1 = bf16[8,128,1664]{2,1,0:T(8,128)(2,1)} custom-call(bf16[128,5120]{1,0:T(8,128)(2,1)} %bitcast.26, bf16[128,5120]{1,0:T(8,128)(2,1)} %bitcast.27, bf16[128,5120]{1,0:T(8,128)(2,1)} %bitcast.28, bf16[128,1024]{1,0:T(8,128)(2,1)} %bitcast.30, bf16[128,1024]{1,0:T(8,128)(2,1)} %bitcast.31), custom_call_target="tpu_custom_call" | custom-call | flops 10000000000 | bytes 8388608 | tf_op jit(solution)/shard_map/pack/pallas_call | solution.py:81
  7.4 6.0 %all-to-all-start = ((bf16[8,128,1664]{2,1,0:T(8,128)(2,1)}), bf16[8,128,1664]{2,1,0:T(8,128)(2,1)S(1)}, u32[]{:S(2)}, u32[]{:S(2)}) async-start(bf16[8,128,1664]{2,1,0:T(8,128)(2,1)} %pack.1), calls=%async_computation | async-start | bytes 6815744 | tf_op jit(solution)/shard_map/all_to_all | solution.py:358
  15.9 0.6 constant_dynamic-update-slice_fusion.1
  16.5 3.9 %collective-permute-done.2 = bf16[4,64,256]{2,1,0:T(8,128)(2,1)S(1)} collective-permute-done((bf16[4,64,256]{2,1,0:T(8,128)(2,1)S(1)}, bf16[4,64,256]{2,1,0:T(8,128)(2,1)S(1)}, u32[]{:S(2)}, u32[]{:S(2)}) %collective-permute-start.2) | collective-permute-done | bytes 131104 | tf_op jit(solution)/shard_map/ppermute | solution.py:336
  20.4 0.7 constant_dynamic-update-slice_fusion.pkv_low
  22.4 8.1 %collective-permute-done.3.pkv_high = bf16[8,64,256]{2,1,0:T(8,128)(2,1)} collective-permute-done((bf16[8,64,256]{2,1,0:T(8,128)(2,1)}, bf16[8,64,256]{2,1,0:T(8,128)(2,1)}, u32[]{:S(2)}, u32[]{:S(2)}) %collective-permute-start.3) | collective-permute-done | bytes 262176 | tf_op jit(solution)/shard_map/ppermute | solution.py:336
  30.4 23.7 %all-to-all-done = bf16[8,128,1664]{2,1,0:T(8,128)(2,1)S(1)} async-done(((bf16[8,128,1664]{2,1,0:T(8,128)(2,1)}), bf16[8,128,1664]{2,1,0:T(8,128)(2,1)S(1)}, u32[]{:S(2)}, u32[]{:S(2)}) %all-to-all-start) | async-done | bytes 3407904 | tf_op jit(solution)/shard_map/all_to_all | solution.py:358
  54.2 34.5 %attend.1 = (bf16[1024,896]{1,0:T(8,128)(2,1)S(1)}, bf16[4,64,256]{2,1,0:T(8,128)(2,1)S(1)}, bf16[4,64,256]{2,1,0:T(8,128)(2,1)}, bf16[4,64,256]{2,1,0:T(8,128)(2,1)}, bf16[4,64,256]{2,1,0:T(8,128)(2,1)S(1)}) custom-call(s32[2]{0:T(128)S(1)} %pad_add_fusion.place_ref, bf16[1024,1664]{1,0:T(8,128)(2,1)S(1)} %bitcast.24, ...), custom_call_target="tpu_custom_call" | custom-call | flops 13421772800 | bytes 5242880 | tf_op jit(solution)/shard_map/attend/pallas_call | solution.py:275
  88.7 1.3 copy-done
  89.9 0.7 copy-done.1
  90.6 3.4 %collective-permute-start.6 = (bf16[4,64,256]{2,1,0:T(8,128)(2,1)S(1)}, bf16[4,64,256]{2,1,0:T(8,128)(2,1)S(1)}, u32[]{:S(2)}, u32[]{:S(2)}) collective-permute-start(bf16[4,64,256]{2,1,0:T(8,128)(2,1)S(1)} %get-tuple-element.29), channel_id=1, source_target_pairs={{0,24},{8,16},{16,8},{24,0},{32,56},{40,48},{48,40},{56,32},{64,88... | collective-permute-start | bytes 393224 | tf_op jit(solution)/shard_map/ppermute | solution.py:336
  94.0 3.7 %all-to-all-start.1 = ((bf16[8,128,896]{2,1,0:T(8,128)(2,1)}), bf16[8,128,896]{2,1,0:T(8,128)(2,1)S(1)}, u32[]{:S(2)}, u32[]{:S(2)}) async-start(bf16[8,128,896]{2,1,0:T(8,128)(2,1)} %bitcast.25), calls=%async_computation.1 | async-start | bytes 3670016 | tf_op jit(solution)/shard_map/all_to_all | solution.py:365
  97.7 0.9 collective-permute-done.5.refs_2_
  98.6 2.0 %collective-permute-done.6.refs_3_ = bf16[4,64,256]{2,1,0:T(8,128)(2,1)S(1)} collective-permute-done((bf16[4,64,256]{2,1,0:T(8,128)(2,1)S(1)}, bf16[4,64,256]{2,1,0:T(8,128)(2,1)S(1)}, u32[]{:S(2)}, u32[]{:S(2)}) %collective-permute-start.6) | collective-permute-done | bytes 131104 | tf_op jit(solution)/shard_map/ppermute | solution.py:336
  100.6 0.6 sum_near.1
  101.4 0.7 collective-permute-start.8
  102.0 4.0 %collective-permute-start.9 = (f32[64,256]{1,0:T(8,128)S(1)}, f32[64,256]{1,0:T(8,128)S(1)}, u32[]{:S(2)}, u32[]{:S(2)}) collective-permute-start(f32[64,256]{1,0:T(8,128)S(1)} %get-tuple-element.33), channel_id=1, source_target_pairs={{0,96},{8,104},{16,112},{24,120},{32,64},{40,72},{48,80},{56,88},{... | collective-permute-start | bytes 196616 | tf_op jit(solution)/shard_map/ppermute | solution.py:336
  106.2 1.4 %collective-permute-done.8 = f32[64,256]{1,0:T(8,128)S(1)} collective-permute-done((f32[64,256]{1,0:T(8,128)S(1)}, f32[64,256]{1,0:T(8,128)S(1)}, u32[]{:S(2)}, u32[]{:S(2)}) %collective-permute-start.8) | collective-permute-done | bytes 65568 | tf_op jit(solution)/shard_map/ppermute | solution.py:336
  107.6 1.3 %collective-permute-done.9 = f32[64,256]{1,0:T(8,128)S(1)} collective-permute-done((f32[64,256]{1,0:T(8,128)S(1)}, f32[64,256]{1,0:T(8,128)S(1)}, u32[]{:S(2)}, u32[]{:S(2)}) %collective-permute-start.9) | collective-permute-done | bytes 65568 | tf_op jit(solution)/shard_map/ppermute | solution.py:336
  109.6 12.9 %all-to-all-done.1.back_ref = bf16[8,128,896]{2,1,0:T(8,128)(2,1)S(1)} async-done(((bf16[8,128,896]{2,1,0:T(8,128)(2,1)}), bf16[8,128,896]{2,1,0:T(8,128)(2,1)S(1)}, u32[]{:S(2)}, u32[]{:S(2)}) %all-to-all-start.1) | async-done | bytes 1835040 | tf_op jit(solution)/shard_map/all_to_all | solution.py:365
  122.5 3.3 %all-to-all-start.2 = ((bf16[8,8,256]{2,1,0:T(8,128)(2,1)}), bf16[8,8,256]{2,1,0:T(8,128)(2,1)S(1)}, u32[]{:S(2)}, u32[]{:S(2)}) async-start(bf16[8,8,256]{2,1,0:T(8,128)(2,1)} %fusion), calls=%async_computation.2 | async-start | bytes 65536 | tf_op jit(solution)/shard_map/all_to_all | solution.py:372
  125.9 1.4 %unpack.1 = (bf16[128,5120]{1,0:T(8,128)(2,1)}, bf16[128,1024]{1,0:T(8,128)(2,1)}, bf16[128,1024]{1,0:T(8,128)(2,1)}) custom-call(bf16[8,128,896]{2,1,0:T(8,128)(2,1)S(1)} %all-to-all-done.1.back_ref), custom_call_target="tpu_custom_call" | custom-call | tf_op jit(solution)/shard_map/unpack/pallas_call | solution.py:114
  127.3 4.8 %all-to-all-done.2 = bf16[8,8,256]{2,1,0:T(8,128)(2,1)S(1)} async-done(((bf16[8,8,256]{2,1,0:T(8,128)(2,1)}), bf16[8,8,256]{2,1,0:T(8,128)(2,1)S(1)}, u32[]{:S(2)}, u32[]{:S(2)}) %all-to-all-start.2) | async-done | bytes 32800 | tf_op jit(solution)/shard_map/all_to_all | solution.py:372
  (24 shorter events, 5.2 us)
Async XLA Ops:
  1.4 6.0 %collective-permute-start = (bf16[1,64,256]{2,1,0:T(8,128)(2,1)S(1)}, bf16[1,64,256]{2,1,0:T(8,128)(2,1)S(1)}, u32[]{:S(2)}, u32[]{:S(2)}) collective-permute-start(bf16[1,64,256]{2,1,0:T(8,128)(2,1)S(1)} %maximum_bitcast_fusion), channel_id=1, source_target_pairs={{0,16},{8,24},{16,0},{24,8},{32,48},{40,56},{48,32},{56,40},{64,80... | collective-permute-start | bytes 98312 | tf_op jit(solution)/shard_map/ppermute | solution.py:336
  7.4 46.7 %all-to-all-start = ((bf16[8,128,1664]{2,1,0:T(8,128)(2,1)}), bf16[8,128,1664]{2,1,0:T(8,128)(2,1)S(1)}, u32[]{:S(2)}, u32[]{:S(2)}) async-start(bf16[8,128,1664]{2,1,0:T(8,128)(2,1)} %pack.1), calls=%async_computation | async-start | bytes 6815744 | tf_op jit(solution)/shard_map/all_to_all | solution.py:358
  13.4 1.3 %collective-permute-start.1 = (bf16[2,64,256]{2,1,0:T(8,128)(2,1)S(1)}, bf16[2,64,256]{2,1,0:T(8,128)(2,1)S(1)}, u32[]{:S(2)}, u32[]{:S(2)}) collective-permute-start(bf16[2,64,256]{2,1,0:T(8,128)(2,1)S(1)} %pad_maximum_fusion.1), channel_id=1, source_target_pairs={{0,8},{8,0},{16,24},{24,16},{32,40},{40,32},{48,56},{56,48},{64,72... | collective-permute-start | bytes 196616 | tf_op jit(solution)/shard_map/ppermute | solution.py:336
  14.8 5.6 %collective-permute-start.2 = (bf16[4,64,256]{2,1,0:T(8,128)(2,1)S(1)}, bf16[4,64,256]{2,1,0:T(8,128)(2,1)S(1)}, u32[]{:S(2)}, u32[]{:S(2)}) collective-permute-start(bf16[4,64,256]{2,1,0:T(8,128)(2,1)S(1)} %pad_maximum_fusion), channel_id=1, source_target_pairs={{0,32},{8,40},{16,48},{24,56},{32,0},{40,8},{48,16},{56,24},{64,96... | collective-permute-start | bytes 393224 | tf_op jit(solution)/shard_map/ppermute | solution.py:336
  21.1 9.4 %collective-permute-start.3 = (bf16[8,64,256]{2,1,0:T(8,128)(2,1)}, bf16[8,64,256]{2,1,0:T(8,128)(2,1)}, u32[]{:S(2)}, u32[]{:S(2)}) collective-permute-start(bf16[8,64,256]{2,1,0:T(8,128)(2,1)} %constant_dynamic-update-slice_fusion.pkv_low), channel_id=1, source_target_pairs={{0,64},{8,72},{16,80},{24,88},{32,96},{40,104},{48,112},{56,120},{... | collective-permute-start | bytes 786440 | tf_op jit(solution)/shard_map/ppermute | solution.py:336
  88.7 1.3 copy-start
  89.9 0.7 copy-start.1
  90.6 7.1 %collective-permute-start.4 = (bf16[4,64,256]{2,1,0:T(8,128)(2,1)}, bf16[4,64,256]{2,1,0:T(8,128)(2,1)S(1)}, u32[]{:S(2)}, u32[]{:S(2)}) collective-permute-start(bf16[4,64,256]{2,1,0:T(8,128)(2,1)} %get-tuple-element.27), channel_id=1, source_target_pairs={{0,8},{8,0},{16,24},{24,16},{32,40},{40,32},{48,56},{56,48},{64,72... | collective-permute-start | bytes 393224 | tf_op jit(solution)/shard_map/ppermute | solution.py:336
  90.6 8.0 %collective-permute-start.5 = (bf16[4,64,256]{2,1,0:T(8,128)(2,1)}, bf16[4,64,256]{2,1,0:T(8,128)(2,1)S(1)}, u32[]{:S(2)}, u32[]{:S(2)}) collective-permute-start(bf16[4,64,256]{2,1,0:T(8,128)(2,1)} %get-tuple-element.28), channel_id=1, source_target_pairs={{0,16},{8,24},{16,0},{24,8},{32,48},{40,56},{48,32},{56,40},{64,80... | collective-permute-start | bytes 393224 | tf_op jit(solution)/shard_map/ppermute | solution.py:336
  90.6 10.0 %collective-permute-start.6 = (bf16[4,64,256]{2,1,0:T(8,128)(2,1)S(1)}, bf16[4,64,256]{2,1,0:T(8,128)(2,1)S(1)}, u32[]{:S(2)}, u32[]{:S(2)}) collective-permute-start(bf16[4,64,256]{2,1,0:T(8,128)(2,1)S(1)} %get-tuple-element.29), channel_id=1, source_target_pairs={{0,24},{8,16},{16,8},{24,0},{32,56},{40,48},{48,40},{56,32},{64,88... | collective-permute-start | bytes 393224 | tf_op jit(solution)/shard_map/ppermute | solution.py:336
  94.0 6.7 %copy-start.2 = (bf16[4,64,256]{2,1,0:T(8,128)(2,1)S(1)}, bf16[4,64,256]{2,1,0:T(8,128)(2,1)}, u32[]{:S(2)}) copy-start(bf16[4,64,256]{2,1,0:T(8,128)(2,1)} %copy-done.1) | copy-start | bytes 393220
  94.0 28.6 %all-to-all-start.1 = ((bf16[8,128,896]{2,1,0:T(8,128)(2,1)}), bf16[8,128,896]{2,1,0:T(8,128)(2,1)S(1)}, u32[]{:S(2)}, u32[]{:S(2)}) async-start(bf16[8,128,896]{2,1,0:T(8,128)(2,1)} %bitcast.25), calls=%async_computation.1 | async-start | bytes 3670016 | tf_op jit(solution)/shard_map/all_to_all | solution.py:365
  101.3 5.0 %collective-permute-start.7 = (f32[64,256]{1,0:T(8,128)S(1)}, f32[64,256]{1,0:T(8,128)S(1)}, u32[]{:S(2)}, u32[]{:S(2)}) collective-permute-start(f32[64,256]{1,0:T(8,128)S(1)} %get-tuple-element.31), channel_id=1, source_target_pairs={{0,32},{8,40},{16,48},{24,56},{32,0},{40,8},{48,16},{56,24},{64,96... | collective-permute-start | bytes 196616 | tf_op jit(solution)/shard_map/ppermute | solution.py:336
  101.4 6.2 %collective-permute-start.8 = (f32[64,256]{1,0:T(8,128)S(1)}, f32[64,256]{1,0:T(8,128)S(1)}, u32[]{:S(2)}, u32[]{:S(2)}) collective-permute-start(f32[64,256]{1,0:T(8,128)S(1)} %get-tuple-element.32), channel_id=1, source_target_pairs={{0,64},{8,72},{16,80},{24,88},{32,96},{40,104},{48,112},{56,120},{... | collective-permute-start | bytes 196616 | tf_op jit(solution)/shard_map/ppermute | solution.py:336
  102.0 6.9 %collective-permute-start.9 = (f32[64,256]{1,0:T(8,128)S(1)}, f32[64,256]{1,0:T(8,128)S(1)}, u32[]{:S(2)}, u32[]{:S(2)}) collective-permute-start(f32[64,256]{1,0:T(8,128)S(1)} %get-tuple-element.33), channel_id=1, source_target_pairs={{0,96},{8,104},{16,112},{24,120},{32,64},{40,72},{48,80},{56,88},{... | collective-permute-start | bytes 196616 | tf_op jit(solution)/shard_map/ppermute | solution.py:336
  122.5 9.5 %all-to-all-start.2 = ((bf16[8,8,256]{2,1,0:T(8,128)(2,1)}), bf16[8,8,256]{2,1,0:T(8,128)(2,1)S(1)}, u32[]{:S(2)}, u32[]{:S(2)}) async-start(bf16[8,8,256]{2,1,0:T(8,128)(2,1)} %fusion), calls=%async_computation.2 | async-start | bytes 65536 | tf_op jit(solution)/shard_map/all_to_all | solution.py:372

commit v5 on v4

v5 whole, which is shorter than its diff:
```python
import jax
import jax.numpy as jnp
from jax import lax
from jax.experimental import pallas as pl
from jax.experimental.pallas import tpu as pltpu
from jax.sharding import PartitionSpec as P

HEADS = 40
KV_HEADS = 8
GROUP = HEADS // KV_HEADS
HEAD_DIM = 128
SCALE = HEAD_DIM ** (-0.5)
EXP2_SCALE = SCALE * 1.4426950408889634
QW = GROUP * HEAD_DIM
KVD = 3 * HEAD_DIM
TILE = 256
STATS = 16
UNSEEN = -1e30
PACK_ROWS = 32
GATHER_BITS = (1, 0, 2, 3)
SEND_W = KVD + 2 * QW
BACK_W = QW + 2 * HEAD_DIM
X_BIT, CORE_BIT = 2, 1

NN = (((1,), (0,)), ((), ()))
BF16 = jnp.bfloat16
F32 = jnp.float32
ANY = pl.BlockSpec(memory_space=pl.ANY)
HBM = pl.BlockSpec(memory_space=pltpu.HBM)
VMEM = pl.BlockSpec(memory_space=pltpu.VMEM)
SMEM = pl.BlockSpec(memory_space=pltpu.SMEM)


def dot(a, b, dims):
    return lax.dot_general(a, b, dims, preferred_element_type=F32)


def params(mib):
    return pltpu.CompilerParams(vmem_limit_bytes=mib * 1024 * 1024)


def times(index, size):
    return pl.multiple_of(index * size, size)


def gather_mask(index):
    return sum(((index >> step) & 1) << bit for step, bit in enumerate(GATHER_BITS))


def pack_kernel(q_ref, g_ref, o_ref, k_ref, v_ref, send_ref):
    rows = q_ref.shape[0]
    highs, lows = [], []
    for h in range(KV_HEADS):
        thin = slice(h * HEAD_DIM, (h + 1) * HEAD_DIM)
        wide = slice(h * QW, (h + 1) * QW)
        send_ref[h, :, 0:HEAD_DIM] = k_ref[:, thin]
        send_ref[h, :, HEAD_DIM : 2 * HEAD_DIM] = v_ref[:, thin]
        send_ref[h, :, KVD : KVD + QW] = q_ref[:, wide]
        send_ref[h, :, KVD + QW :] = g_ref[:, wide]
        product = g_ref[:, wide].astype(F32) * o_ref[:, wide].astype(F32)
        high = product.astype(BF16)
        highs.append(high)
        lows.append((product - high.astype(F32)).astype(BF16))
    row = lax.broadcasted_iota(jnp.int32, (QW, HEAD_DIM), 0) // HEAD_DIM
    lane = lax.broadcasted_iota(jnp.int32, (QW, HEAD_DIM), 1)
    ones = jnp.where((lane >= 3 * row) & (lane < 3 * row + 3), 1.0, 0.0).astype(BF16)
    left = dot(jnp.concatenate(highs), ones, NN) + dot(jnp.concatenate(lows), ones, NN)
    part = lax.broadcasted_iota(jnp.int32, left.shape, 1) % 3
    first = left.astype(BF16).astype(F32)
    second = (left - first).astype(BF16).astype(F32)
    third = left - first - second
    deltas = jnp.where(part == 0, first, jnp.where(part == 1, second, third)).astype(BF16)
    for h in range(KV_HEADS):
        send_ref[h, :, 2 * HEAD_DIM : KVD] = deltas[h * rows : (h + 1) * rows]


def pack(q, g, o, k, v):
    rows = q.shape[0]
    block = min(PACK_ROWS, rows)
    wide = pl.BlockSpec((block, KV_HEADS * QW), lambda i: (i, 0))
    thin = pl.BlockSpec((block, KV_HEADS * HEAD_DIM), lambda i: (i, 0))
    return pl.pallas_call(
        pack_kernel,
        grid=(rows // block,),
        in_specs=[wide, wide, wide, thin, thin],
        out_specs=pl.BlockSpec((KV_HEADS, block, SEND_W), lambda i: (0, i, 0)),
        out_shape=jax.ShapeDtypeStruct((KV_HEADS, rows, SEND_W), BF16),
        compiler_params=params(60),
        cost_estimate=pl.CostEstimate(flops=10**10, transcendentals=0, bytes_accessed=2**23),
        name="pack",
    )(q, g, o, k, v)


def start_all(copies, sems):
    started = [pltpu.make_async_copy(src, dst, sems.at[n]) for n, (src, dst) in enumerate(copies)]
    for copy in started:
        copy.start()
    return started


def unpack_kernel(back_ref, q_ref, k_ref, v_ref, sems):
    copies = []
    for h in range(KV_HEADS):
        thin = slice(h * HEAD_DIM, (h + 1) * HEAD_DIM)
        wide = slice(h * QW, (h + 1) * QW)
        copies.append((back_ref.at[h, :, 0:QW], q_ref.at[:, wide]))
        copies.append((back_ref.at[h, :, QW : QW + HEAD_DIM], k_ref.at[:, thin]))
        copies.append((back_ref.at[h, :, QW + HEAD_DIM :], v_ref.at[:, thin]))
    for copy in start_all(copies, sems):
        copy.wait()


def unpack(back):
    rows = back.shape[1]
    return pl.pallas_call(
        unpack_kernel,
        in_specs=[ANY],
        out_specs=[ANY] * 3,
        out_shape=[
            jax.ShapeDtypeStruct((rows, KV_HEADS * QW), BF16),
            jax.ShapeDtypeStruct((rows, KV_HEADS * HEAD_DIM), BF16),
            jax.ShapeDtypeStruct((rows, KV_HEADS * HEAD_DIM), BF16),
        ],
        scratch_shapes=[pltpu.SemaphoreType.DMA((3 * KV_HEADS,))],
        compiler_params=params(4),
        name="unpack",
    )(back)


def attend_kernel(place_ref, x_ref, pkv_low, pkv_high, back_out, pg_keep, pg_give, *refs):
    pkv_ref, back_ref, pg_ref, sems, k_all, v_all, k_t, d_all = refs[:8]
    p_s, l_s, dq_t, dk, dv = refs[8:13]
    sets = [refs[13:20], refs[20:27]]
    prompt = pkv_ref.shape[0]
    slots = x_ref.shape[0]
    wide = GROUP * TILE
    prompt_tiles = prompt // TILE
    length, me_prefix = place_ref[0], place_ref[1]
    half = pkv_low.shape[0]
    sources = 2 * half
    share = prompt // sources
    copies = [
        ((pkv_low, pkv_high)[f // half].at[f % half], pkv_ref.at[pl.ds(times(me_prefix ^ gather_mask(f), share), share)])
        for f in range(sources)
    ]
    copies = start_all(copies, sems)
    back_ref[...] = jnp.zeros_like(back_ref)
    dk[...] = jnp.zeros_like(dk)
    dv[...] = jnp.zeros_like(dv)
    for copy in copies:
        copy.wait()

    def flip(a):
        return a.astype(F32).T.astype(BF16)

    k_all[0:prompt] = pkv_ref[:, 0:HEAD_DIM]
    v_all[0:prompt] = pkv_ref[:, HEAD_DIM:]
    k_all[prompt:] = x_ref[:, 0:HEAD_DIM]
    v_all[prompt:] = x_ref[:, HEAD_DIM : 2 * HEAD_DIM]
    d_all[...] = x_ref[:, 2 * HEAD_DIM : KVD]
    for t in range((prompt + slots) // TILE):
        block = slice(t * TILE, (t + 1) * TILE)
        k_t[:, block] = flip(k_all[block])

    def lanes(j):
        return slice(j * TILE, (j + 1) * TILE)

    def tile_rows(t, count):
        return pl.ds(times(t, TILE), count * TILE)

    def stat_rows(t, count):
        return pl.ds(times(t, STATS), count * STATS)

    def sweep(body, tiles):
        def pair(n, carry):
            body(2 * n, 2)
            return carry

        lax.fori_loop(0, tiles // 2, pair, 0)
        if tiles % 2:
            body(tiles - 1, 1)

    def load_block(i, block):
        qs, gs, qs_t, gs_t = block[:4]
        here = slice(i * TILE, (i + 1) * TILE)
        delta_t = flip(d_all[here])
        for j in range(GROUP):
            col = KVD + j * HEAD_DIM
            q = x_ref[here, col : col + HEAD_DIM]
            g = x_ref[here, col + QW : col + QW + HEAD_DIM]
            qs[lanes(j)] = q
            gs[lanes(j)] = g
            qs_t[:, lanes(j)] = flip(q)
            gs_t[0:HEAD_DIM, lanes(j)] = flip(g)
            gs_t[HEAD_DIM:, lanes(j)] = delta_t

    def score_head(t, count, j, block, diagonal=False):
        qs_t, e_all, tops, sums = block[2], block[4], block[5], block[6]
        s = dot(k_all[tile_rows(t, count)], qs_t[:, lanes(j)], NN)
        if diagonal:
            seen = lax.broadcasted_iota(jnp.int32, s.shape, 0) <= lax.broadcasted_iota(
                jnp.int32, s.shape, 1
            )
            s = jnp.where(seen, s, UNSEEN)
        groups = count * STATS // 8
        s = s.reshape(groups, -1, 8, TILE)
        top = jnp.max(s, axis=1, keepdims=True)
        e = jnp.exp2((s - top) * EXP2_SCALE)
        tops[stat_rows(t, count), lanes(j)] = top.reshape(groups * 8, TILE)
        sums[stat_rows(t, count), lanes(j)] = jnp.sum(e, axis=1).reshape(groups * 8, TILE)
        e_all[tile_rows(t, count), lanes(j)] = e.reshape(count * TILE, TILE)

    def normalise(i, block):
        tops, sums = block[5], block[6]
        rows = STATS * (prompt_tiles + i + 1)
        top = tops[0:rows]
        weight = jnp.exp2((top - jnp.max(top, axis=0, keepdims=True)) * EXP2_SCALE)
        total = jnp.sum(weight * sums[0:rows], axis=0, keepdims=True)
        slot = lax.broadcasted_iota(jnp.int32, (1, wide), 1) % TILE + i * TILE
        tops[0:rows] = weight * (jnp.where(slot < length, 1.0, 0.0) / total)

    def grad_head(t, count, j, block):
        gs_t, e_all, factors = block[3], block[4], block[5]
        lane = lax.broadcasted_iota(jnp.int32, (count * TILE, HEAD_DIM), 1)
        select = jnp.where((lane >= 3 * j) & (lane < 3 * j + 3), -1.0, 0.0).astype(BF16)
        values = jnp.concatenate([v_all[tile_rows(t, count)], select], axis=1)
        shifted = dot(values, gs_t[:, lanes(j)], NN)
        groups = count * STATS // 8
        e = e_all[tile_rows(t, count), lanes(j)].reshape(groups, -1, 8, TILE)
        factor = factors[stat_rows(t, count), lanes(j)].reshape(groups, 1, 8, TILE)
        p = (e * factor).reshape(count * TILE, TILE)
        p_s[0 : count * TILE, lanes(j)] = p.astype(BF16)
        l_s[0 : count * TILE, lanes(j)] = (p * shifted).astype(BF16)

    def grad_sums(t, count, block):
        qs, gs = block[:2]
        rows, held = tile_rows(t, count), slice(0, count * TILE)
        dv[rows] += dot(p_s[held], gs[...], NN)
        dk[rows] += dot(l_s[held], qs[...], NN)
        dq_t[...] += dot(k_t[:, rows], l_s[held], NN)

    def finish(i):
        here = slice(i * TILE, (i + 1) * TILE)
        for j in range(GROUP):
            back_ref[here, j * HEAD_DIM : (j + 1) * HEAD_DIM] = (
                (dq_t[:, lanes(j)] * SCALE).T.astype(BF16)
            )

    def scores(t, count):
        for j in range(GROUP):
            score_head(t, count, j, sets[0])

    load_block(0, sets[0])
    sweep(scores, prompt_tiles)
    for j in range(GROUP):
        score_head(prompt_tiles, 1, j, sets[0], diagonal=True)
    normalise(0, sets[0])

    blocks = slots // TILE
    live = lax.div(length + TILE - 1, TILE)
    for i in range(blocks):
        now, later = sets[i % 2], sets[(i + 1) % 2]
        tiles = prompt_tiles + i + 1
        dq_t[...] = jnp.zeros_like(dq_t)

        def grads(t, count):
            for j in range(GROUP):
                grad_head(t, count, j, now)
            grad_sums(t, count, now)

        def both(t, count):
            for j in range(GROUP):
                grad_head(t, count, j, now)
                score_head(t, count, j, later)
            grad_sums(t, count, now)

        if i + 1 < blocks:

            @pl.when(live > i + 1)
            def _():
                load_block(i + 1, later)
                sweep(both, tiles)
                finish(i)
                for j in range(GROUP):
                    score_head(tiles, 1, j, later, diagonal=True)
                normalise(i + 1, later)

        @pl.when(live == i + 1)
        def _():
            sweep(grads, tiles)
            finish(i)

    pg_ref[:, 0:HEAD_DIM] = (dk[0:prompt] * SCALE).astype(BF16)
    pg_ref[:, HEAD_DIM:] = dv[0:prompt].astype(BF16)
    back_ref[:, QW : QW + HEAD_DIM] = (dk[prompt:] * SCALE).astype(BF16)
    back_ref[:, QW + HEAD_DIM :] = dv[prompt:].astype(BF16)
    mine = me_prefix & X_BIT
    copies = [
        (pg_ref.at[pl.ds(times(f + (f & -X_BIT) + (mine ^ bit), share), share)], out.at[f])
        for bit, out in ((0, pg_keep), (X_BIT, pg_give))
        for f in range(half)
    ]
    for copy in start_all([(back_ref, back_out)] + copies, sems):
        copy.wait()


def attend(place, x, pkv):
    slots = x.shape[0]
    half, share, prompt_width = pkv[0].shape
    responses = 2 * half
    prompt = responses * share
    keys = slots + prompt
    wide = GROUP * TILE
    outs = [((slots, BACK_W), BF16)] + [((half, share, prompt_width), BF16)] * 2
    stats = pltpu.VMEM((keys // TILE * STATS, wide), F32)
    one_set = [
        pltpu.VMEM((wide, HEAD_DIM), BF16),
        pltpu.VMEM((wide, HEAD_DIM), BF16),
        pltpu.VMEM((HEAD_DIM, wide), BF16),
        pltpu.VMEM((2 * HEAD_DIM, wide), BF16),
        pltpu.VMEM((keys, wide), F32),
        stats,
        stats,
    ]
    return pl.pallas_call(
        attend_kernel,
        in_specs=[SMEM, VMEM, ANY, ANY],
        out_specs=[HBM] * len(outs),
        out_shape=[pltpu.HBM(shape, dtype) for shape, dtype in outs],
        scratch_shapes=[
            pltpu.VMEM((prompt, prompt_width), BF16),
            pltpu.VMEM((slots, BACK_W), BF16),
            pltpu.VMEM((prompt, prompt_width), BF16),
            pltpu.SemaphoreType.DMA((1 + responses,)),
            pltpu.VMEM((keys, HEAD_DIM), BF16),
            pltpu.VMEM((keys, HEAD_DIM), BF16),
            pltpu.VMEM((HEAD_DIM, keys), BF16),
            pltpu.VMEM((slots, HEAD_DIM), BF16),
            pltpu.VMEM((2 * TILE, wide), BF16),
            pltpu.VMEM((2 * TILE, wide), BF16),
            pltpu.VMEM((HEAD_DIM, wide), F32),
            pltpu.VMEM((keys, HEAD_DIM), F32),
            pltpu.VMEM((keys, HEAD_DIM), F32),
        ]
        + one_set * 2,
        compiler_params=params(50),
        cost_estimate=pl.CostEstimate(
            flops=10 * slots * keys * QW, transcendentals=0, bytes_accessed=8 * slots * QW
        ),
        name="attend",
    )(place, pltpu.with_memory_space_constraint(x, pltpu.VMEM), *pkv)


def core_kernel(place_ref, mine_ref, got_ref, keep_ref, give_ref, total):
    total[...] = mine_ref[...].astype(F32) + got_ref[...].astype(F32)
    core = place_ref[1] & CORE_BIT
    for f in range(keep_ref.shape[0]):
        keep_ref[f] = total[2 * f + core]
        give_ref[f] = total[2 * f + 1 - core]


def sum_over_x(place, mine, got):
    count, share, width = mine.shape
    part = jax.ShapeDtypeStruct((count // 2, share, width), F32)
    return pl.pallas_call(
        core_kernel,
        in_specs=[SMEM, VMEM, VMEM],
        out_specs=[VMEM] * 2,
        out_shape=[part] * 2,
        scratch_shapes=[pltpu.VMEM(mine.shape, F32)],
        compiler_params=params(8),
        cost_estimate=pl.CostEstimate(flops=5 * 10**10, transcendentals=0, bytes_accessed=2**20),
        name="sum_over_x",
    )(place, mine, got)


def z_kernel(place_ref, mine_ref, got_ref, *refs):
    outs, total = refs[:-1], refs[-1]
    total[...] = mine_ref[...] + got_ref[...]
    z = place_ref[1] // (2 * X_BIT)
    for d, out in enumerate(outs):
        out[...] = total[z ^ d]


def sum_over_cores(place, mine, got):
    count, share, width = mine.shape
    return pl.pallas_call(
        z_kernel,
        in_specs=[SMEM, VMEM, VMEM],
        out_specs=[VMEM] * count,
        out_shape=[jax.ShapeDtypeStruct((share, width), F32)] * count,
        scratch_shapes=[pltpu.VMEM(mine.shape, F32)],
        compiler_params=params(8),
        name="sum_over_cores",
    )(place, mine, got)


def swap(value, axis, d):
    return lax.ppermute(value, axis, [(i, i ^ d) for i in range(lax.axis_size(axis))])


def local(
    resp_query,
    resp_keys,
    resp_values,
    resp_out,
    resp_grad,
    prompt_keys,
    prompt_values,
    resp_lengths,
):
    head = lax.axis_index("resp")
    rows = resp_query.shape[1]
    place = jnp.stack([resp_lengths[0], lax.axis_index("prefix")])
    cut = lambda a: lax.dynamic_slice_in_dim(a, head * HEAD_DIM, HEAD_DIM, 1)
    pkv = jnp.concatenate([cut(prompt_keys), cut(prompt_values)], axis=1)[None]
    first = swap(pkv, "prefix", 1 << GATHER_BITS[0])
    send = pack(resp_query[0], resp_grad[0], resp_out[0], resp_keys[0], resp_values[0])
    pkv, first, send = lax.optimization_barrier((pkv, first, send))
    x = lax.all_to_all(send, "resp", 0, 0, tiled=True)
    pkv = jnp.concatenate([pkv, first])
    for bit in GATHER_BITS[1:-1]:
        pkv = jnp.concatenate([pkv, swap(pkv, "prefix", 1 << bit)])
    pkv = [pkv, swap(pkv, "prefix", 1 << GATHER_BITS[-1])]
    back, keep, give = attend(place, x.reshape(KV_HEADS * rows, SEND_W), pkv)
    back = lax.all_to_all(back.reshape(KV_HEADS, rows, BACK_W), "resp", 0, 0, tiled=True)
    keep, give = sum_over_x(place, keep, swap(give, "prefix", X_BIT))
    parts = sum_over_cores(place, keep, swap(give, "prefix", CORE_BIT))
    parts = [parts[0]] + [swap(parts[d], "prefix", 2 * X_BIT * d) for d in range(1, len(parts))]
    share, width = parts[0].shape
    total = sum(parts[1:], parts[0]).astype(BF16).reshape(KV_HEADS, share // KV_HEADS, width)
    back, total = lax.optimization_barrier((back, total))
    total = lax.all_to_all(total, "resp", 0, 0, tiled=True)
    total = total.reshape(KV_HEADS, share // KV_HEADS, 2, HEAD_DIM).transpose(2, 1, 0, 3)
    total = total.reshape(2, share // KV_HEADS, KV_HEADS * HEAD_DIM)
    grad_query, grad_keys, grad_values = unpack(back)
    return (grad_query[None], grad_keys[None], grad_values[None], total[0], total[1])


def solution(mesh):
    return jax.shard_map(
        local,
        mesh=mesh,
        in_specs=(
            P("prefix", "resp", None),
            P("prefix", "resp", None),
            P("prefix", "resp", None),
            P("prefix", "resp", None),
            P("prefix", "resp", None),
            P("prefix", None),
            P("prefix", None),
            P("prefix"),
        ),
        out_specs=(
            P("prefix", "resp", None),
            P("prefix", "resp", None),
            P("prefix", "resp", None),
            P(("prefix", "resp"), None),
            P(("prefix", "resp"), None),
        ),
        check_vma=False,
    )
```

time: 134 us -> 125 us (0.933)
  the two profiles are of different devices: /device:TPU:100 before, /device:TPU:32 now
where the time goes in v5:
time: 125 us
  waiting for transfers between devices  56.6 us (45%)
  starting transfers between devices  38.3 us (31%)
  Pallas kernels  23.6 us (19%)
  local copies, waits for them, and re-layouts  3.91 us (3%)
  between operations  1.38 us (1%)
    ppermute x9, starting transfers between devices, swap(): lax.ppermute(value, axis, [(i, i ^ d) for i in range(lax.axis_size(axis))])  26.8 us
    all_to_all x1, waiting for transfers between devices, local(): x = lax.all_to_all(send, 'resp', 0, 0, tiled=True)  23.7 us
    ppermute x9, waiting for transfers between devices, swap(): lax.ppermute(value, axis, [(i, i ^ d) for i in range(lax.axis_size(axis))])  19.3 us
    pallas_call x1, Pallas kernels, attend(): pl.pallas_call(attend_kernel, in_specs=[SMEM, VMEM, ANY, ANY], out_specs=...  15.5 us
    all_to_all x1, waiting for transfers between devices, local(): lax.all_to_all(back.reshape(KV_HEADS, rows, BACK_W), 'resp', 0, 0, tiled=...  8.83 us
    pallas_call x1, Pallas kernels, pack(): pl.pallas_call(pack_kernel, grid=(rows // block,), in_specs=[wide, wide,...  5.45 us
    all_to_all x1, waiting for transfers between devices, local(): total = lax.all_to_all(total, 'resp', 0, 0, tiled=True)  4.76 us
    all_to_all x1, starting transfers between devices, local(): x = lax.all_to_all(send, 'resp', 0, 0, tiled=True)  4.49 us
  transfers between devices with their start and end apart: 12, of which 11 were waited for; matrix products, arithmetic and copies ran while one was open for 3% of the time, Pallas kernels for 7%

profile of v5, /device:TPU:32, one launch (start us, length us, event | category | flops | bytes accessed | tf_op | source)
XLA Modules:
  0.0 124.5 jit_solution(11224348463749348995)
XLA Ops:
  0.6 0.8 constant_dynamic-slice_fusion
  1.4 3.1 %collective-permute-start = (bf16[1,64,256]{2,1,0:T(8,128)(2,1)S(1)}, bf16[1,64,256]{2,1,0:T(8,128)(2,1)S(1)}, u32[]{:S(2)}, u32[]{:S(2)}) collective-permute-start(bf16[1,64,256]{2,1,0:T(8,128)(2,1)S(1)} %maximum_bitcast_fusion), channel_id=1, source_target_pairs={{0,16},{8,24},{16,0},{24,8},{32,48},{40,56},{48,32},{56,40},{64,80... | collective-permute-start | bytes 98312 | tf_op jit(solution)/shard_map/ppermute | solution.py:399
  4.5 5.4 %pack.1 = bf16[8,128,1664]{2,1,0:T(8,128)(2,1)} custom-call(bf16[128,5120]{1,0:T(8,128)(2,1)} %bitcast.26, bf16[128,5120]{1,0:T(8,128)(2,1)} %bitcast.27, bf16[128,5120]{1,0:T(8,128)(2,1)} %bitcast.28, bf16[128,1024]{1,0:T(8,128)(2,1)} %bitcast.30, bf16[128,1024]{1,0:T(8,128)(2,1)} %bitcast.31), custom_call_target="tpu_custom_call" | custom-call | flops 10000000000 | bytes 8388608 | tf_op jit(solution)/shard_map/pack/pallas_call | solution.py:82
  10.0 4.5 %all-to-all-start = ((bf16[8,128,1664]{2,1,0:T(8,128)(2,1)}), bf16[8,128,1664]{2,1,0:T(8,128)(2,1)S(1)}, u32[]{:S(2)}, u32[]{:S(2)}) async-start(bf16[8,128,1664]{2,1,0:T(8,128)(2,1)} %pack.1), calls=%async_computation | async-start | bytes 6815744 | tf_op jit(solution)/shard_map/all_to_all | solution.py:420
  17.2 4.2 %collective-permute-done.2 = bf16[4,64,256]{2,1,0:T(8,128)(2,1)S(1)} collective-permute-done((bf16[4,64,256]{2,1,0:T(8,128)(2,1)S(1)}, bf16[4,64,256]{2,1,0:T(8,128)(2,1)S(1)}, u32[]{:S(2)}, u32[]{:S(2)}) %collective-permute-start.2) | collective-permute-done | bytes 131104 | tf_op jit(solution)/shard_map/ppermute | solution.py:399
  21.4 0.7 constant_dynamic-update-slice_fusion.pkv_low
  22.1 3.0 %collective-permute-start.3 = (bf16[8,64,256]{2,1,0:T(8,128)(2,1)}, bf16[8,64,256]{2,1,0:T(8,128)(2,1)}, u32[]{:S(2)}, u32[]{:S(2)}) collective-permute-start(bf16[8,64,256]{2,1,0:T(8,128)(2,1)} %constant_dynamic-update-slice_fusion.pkv_low), channel_id=1, source_target_pairs={{0,64},{8,72},{16,80},{24,88},{32,96},{40,104},{48,112},{56,120},{... | collective-permute-start | bytes 786440 | tf_op jit(solution)/shard_map/ppermute | solution.py:399
  25.8 5.7 %collective-permute-done.3.pkv_high = bf16[8,64,256]{2,1,0:T(8,128)(2,1)} collective-permute-done((bf16[8,64,256]{2,1,0:T(8,128)(2,1)}, bf16[8,64,256]{2,1,0:T(8,128)(2,1)}, u32[]{:S(2)}, u32[]{:S(2)}) %collective-permute-start.3) | collective-permute-done | bytes 262176 | tf_op jit(solution)/shard_map/ppermute | solution.py:399
  31.5 23.7 %all-to-all-done = bf16[8,128,1664]{2,1,0:T(8,128)(2,1)S(1)} async-done(((bf16[8,128,1664]{2,1,0:T(8,128)(2,1)}), bf16[8,128,1664]{2,1,0:T(8,128)(2,1)S(1)}, u32[]{:S(2)}, u32[]{:S(2)}) %all-to-all-start) | async-done | bytes 3407904 | tf_op jit(solution)/shard_map/all_to_all | solution.py:420
  55.2 15.5 %attend.1 = (bf16[1024,896]{1,0:T(8,128)(2,1)}, bf16[8,64,256]{2,1,0:T(8,128)(2,1)}, bf16[8,64,256]{2,1,0:T(8,128)(2,1)}) custom-call(s32[2]{0:T(128)S(1)} %pad_add_fusion.place_ref, bf16[1024,1664]{1,0:T(8,128)(2,1)S(1)} %bitcast.24, bf16[8,64,256]{2,1,0:T(8,128)(2,1)} %constant_dynamic-update-slice_fusion.pkv_low, ...), custom_call_target="tpu_custom_call" | custom-call | flops 13421772800 | bytes 5242880 | tf_op jit(solution)/shard_map/attend/pallas_call | solution.py:325
  70.7 16.8 %collective-permute-start.4 = (bf16[8,64,256]{2,1,0:T(8,128)(2,1)}, bf16[8,64,256]{2,1,0:T(8,128)(2,1)S(1)}, u32[]{:S(2)}, u32[]{:S(2)}) collective-permute-start(bf16[8,64,256]{2,1,0:T(8,128)(2,1)} %get-tuple-element.27), channel_id=1, source_target_pairs={{0,16},{8,24},{16,0},{24,8},{32,48},{40,56},{48,32},{56,40},{64,80... | collective-permute-start | bytes 786440 | tf_op jit(solution)/shard_map/ppermute | solution.py:399
  87.5 3.7 %all-to-all-start.1 = ((bf16[8,128,896]{2,1,0:T(8,128)(2,1)}), bf16[8,128,896]{2,1,0:T(8,128)(2,1)S(1)}, u32[]{:S(2)}, u32[]{:S(2)}) async-start(bf16[8,128,896]{2,1,0:T(8,128)(2,1)} %bitcast.25), calls=%async_computation.1 | async-start | bytes 3670016 | tf_op jit(solution)/shard_map/all_to_all | solution.py:426
  91.2 3.3 %collective-permute-done.4.got_ref = bf16[8,64,256]{2,1,0:T(8,128)(2,1)S(1)} collective-permute-done((bf16[8,64,256]{2,1,0:T(8,128)(2,1)}, bf16[8,64,256]{2,1,0:T(8,128)(2,1)S(1)}, u32[]{:S(2)}, u32[]{:S(2)}) %collective-permute-start.4) | collective-permute-done | bytes 262176 | tf_op jit(solution)/shard_map/ppermute | solution.py:399
  94.5 0.7 sum_over_x.1
  95.2 1.5 %collective-permute-done.5.got_ref = f32[4,64,256]{2,1,0:T(8,128)S(1)} collective-permute-done((f32[4,64,256]{2,1,0:T(8,128)S(1)}, f32[4,64,256]{2,1,0:T(8,128)S(1)}, u32[]{:S(2)}, u32[]{:S(2)}) %collective-permute-start.5) | collective-permute-done | bytes 262176 | tf_op jit(solution)/shard_map/ppermute | solution.py:399
  98.0 2.2 %collective-permute-start.7 = (f32[64,256]{1,0:T(8,128)S(1)}, f32[64,256]{1,0:T(8,128)S(1)}, u32[]{:S(2)}, u32[]{:S(2)}) collective-permute-start(f32[64,256]{1,0:T(8,128)S(1)} %get-tuple-element.32), channel_id=1, source_target_pairs={{0,64},{8,72},{16,80},{24,88},{32,96},{40,104},{48,112},{56,120},{... | collective-permute-start | bytes 196616 | tf_op jit(solution)/shard_map/ppermute | solution.py:399
  100.2 0.7 collective-permute-start.8
  100.9 1.0 collective-permute-done.6
  101.9 2.0 %collective-permute-done.7 = f32[64,256]{1,0:T(8,128)S(1)} collective-permute-done((f32[64,256]{1,0:T(8,128)S(1)}, f32[64,256]{1,0:T(8,128)S(1)}, u32[]{:S(2)}, u32[]{:S(2)}) %collective-permute-start.7) | collective-permute-done | bytes 65568 | tf_op jit(solution)/shard_map/ppermute | solution.py:399
  103.9 1.0 collective-permute-done.8
  105.6 8.8 %all-to-all-done.1.back_ref = bf16[8,128,896]{2,1,0:T(8,128)(2,1)S(1)} async-done(((bf16[8,128,896]{2,1,0:T(8,128)(2,1)}), bf16[8,128,896]{2,1,0:T(8,128)(2,1)S(1)}, u32[]{:S(2)}, u32[]{:S(2)}) %all-to-all-start.1) | async-done | bytes 1835040 | tf_op jit(solution)/shard_map/all_to_all | solution.py:426
  114.4 3.3 %all-to-all-start.2 = ((bf16[8,8,256]{2,1,0:T(8,128)(2,1)}), bf16[8,8,256]{2,1,0:T(8,128)(2,1)S(1)}, u32[]{:S(2)}, u32[]{:S(2)}) async-start(bf16[8,8,256]{2,1,0:T(8,128)(2,1)} %fusion), calls=%async_computation.2 | async-start | bytes 65536 | tf_op jit(solution)/shard_map/all_to_all | solution.py:433
  117.7 1.4 %unpack.1 = (bf16[128,5120]{1,0:T(8,128)(2,1)}, bf16[128,1024]{1,0:T(8,128)(2,1)}, bf16[128,1024]{1,0:T(8,128)(2,1)}) custom-call(bf16[8,128,896]{2,1,0:T(8,128)(2,1)S(1)} %all-to-all-done.1.back_ref), custom_call_target="tpu_custom_call" | custom-call | tf_op jit(solution)/shard_map/unpack/pallas_call | solution.py:115
  119.2 4.8 %all-to-all-done.2 = bf16[8,8,256]{2,1,0:T(8,128)(2,1)S(1)} async-done(((bf16[8,8,256]{2,1,0:T(8,128)(2,1)}), bf16[8,8,256]{2,1,0:T(8,128)(2,1)S(1)}, u32[]{:S(2)}, u32[]{:S(2)}) %all-to-all-start.2) | async-done | bytes 32800 | tf_op jit(solution)/shard_map/all_to_all | solution.py:433
  (19 shorter events, 5.4 us)
Async XLA Ops:
  1.4 8.6 %collective-permute-start = (bf16[1,64,256]{2,1,0:T(8,128)(2,1)S(1)}, bf16[1,64,256]{2,1,0:T(8,128)(2,1)S(1)}, u32[]{:S(2)}, u32[]{:S(2)}) collective-permute-start(bf16[1,64,256]{2,1,0:T(8,128)(2,1)S(1)} %maximum_bitcast_fusion), channel_id=1, source_target_pairs={{0,16},{8,24},{16,0},{24,8},{32,48},{40,56},{48,32},{56,40},{64,80... | collective-permute-start | bytes 98312 | tf_op jit(solution)/shard_map/ppermute | solution.py:399
  10.0 45.2 %all-to-all-start = ((bf16[8,128,1664]{2,1,0:T(8,128)(2,1)}), bf16[8,128,1664]{2,1,0:T(8,128)(2,1)S(1)}, u32[]{:S(2)}, u32[]{:S(2)}) async-start(bf16[8,128,1664]{2,1,0:T(8,128)(2,1)} %pack.1), calls=%async_computation | async-start | bytes 6815744 | tf_op jit(solution)/shard_map/all_to_all | solution.py:420
  14.5 1.3 %collective-permute-start.1 = (bf16[2,64,256]{2,1,0:T(8,128)(2,1)S(1)}, bf16[2,64,256]{2,1,0:T(8,128)(2,1)S(1)}, u32[]{:S(2)}, u32[]{:S(2)}) collective-permute-start(bf16[2,64,256]{2,1,0:T(8,128)(2,1)S(1)} %pad_maximum_fusion.1), channel_id=1, source_target_pairs={{0,8},{8,0},{16,24},{24,16},{32,40},{40,32},{48,56},{56,48},{64,72... | collective-permute-start | bytes 196616 | tf_op jit(solution)/shard_map/ppermute | solution.py:399
  15.8 5.6 %collective-permute-start.2 = (bf16[4,64,256]{2,1,0:T(8,128)(2,1)S(1)}, bf16[4,64,256]{2,1,0:T(8,128)(2,1)S(1)}, u32[]{:S(2)}, u32[]{:S(2)}) collective-permute-start(bf16[4,64,256]{2,1,0:T(8,128)(2,1)S(1)} %pad_maximum_fusion), channel_id=1, source_target_pairs={{0,32},{8,40},{16,48},{24,56},{32,0},{40,8},{48,16},{56,24},{64,96... | collective-permute-start | bytes 393224 | tf_op jit(solution)/shard_map/ppermute | solution.py:399
  22.1 9.4 %collective-permute-start.3 = (bf16[8,64,256]{2,1,0:T(8,128)(2,1)}, bf16[8,64,256]{2,1,0:T(8,128)(2,1)}, u32[]{:S(2)}, u32[]{:S(2)}) collective-permute-start(bf16[8,64,256]{2,1,0:T(8,128)(2,1)} %constant_dynamic-update-slice_fusion.pkv_low), channel_id=1, source_target_pairs={{0,64},{8,72},{16,80},{24,88},{32,96},{40,104},{48,112},{56,120},{... | collective-permute-start | bytes 786440 | tf_op jit(solution)/shard_map/ppermute | solution.py:399
  70.7 23.7 %collective-permute-start.4 = (bf16[8,64,256]{2,1,0:T(8,128)(2,1)}, bf16[8,64,256]{2,1,0:T(8,128)(2,1)S(1)}, u32[]{:S(2)}, u32[]{:S(2)}) collective-permute-start(bf16[8,64,256]{2,1,0:T(8,128)(2,1)} %get-tuple-element.27), channel_id=1, source_target_pairs={{0,16},{8,24},{16,0},{24,8},{32,48},{40,56},{48,32},{56,40},{64,80... | collective-permute-start | bytes 786440 | tf_op jit(solution)/shard_map/ppermute | solution.py:399
  87.5 7.0 %copy-start = (bf16[8,64,256]{2,1,0:T(8,128)(2,1)S(1)}, bf16[8,64,256]{2,1,0:T(8,128)(2,1)}, u32[]{:S(2)}) copy-start(bf16[8,64,256]{2,1,0:T(8,128)(2,1)} %get-tuple-element.26.mine_ref) | copy-start | bytes 786436
  87.5 26.9 %all-to-all-start.1 = ((bf16[8,128,896]{2,1,0:T(8,128)(2,1)}), bf16[8,128,896]{2,1,0:T(8,128)(2,1)S(1)}, u32[]{:S(2)}, u32[]{:S(2)}) async-start(bf16[8,128,896]{2,1,0:T(8,128)(2,1)} %bitcast.25), calls=%async_computation.1 | async-start | bytes 3670016 | tf_op jit(solution)/shard_map/all_to_all | solution.py:426
  95.1 1.6 %collective-permute-start.5 = (f32[4,64,256]{2,1,0:T(8,128)S(1)}, f32[4,64,256]{2,1,0:T(8,128)S(1)}, u32[]{:S(2)}, u32[]{:S(2)}) collective-permute-start(f32[4,64,256]{2,1,0:T(8,128)S(1)} %get-tuple-element.29), channel_id=1, source_target_pairs={{0,8},{8,0},{16,24},{24,16},{32,40},{40,32},{48,56},{56,48},{64,72... | collective-permute-start | bytes 786440 | tf_op jit(solution)/shard_map/ppermute | solution.py:399
  97.4 4.5 %collective-permute-start.6 = (f32[64,256]{1,0:T(8,128)S(1)}, f32[64,256]{1,0:T(8,128)S(1)}, u32[]{:S(2)}, u32[]{:S(2)}) collective-permute-start(f32[64,256]{1,0:T(8,128)S(1)} %get-tuple-element.31), channel_id=1, source_target_pairs={{0,32},{8,40},{16,48},{24,56},{32,0},{40,8},{48,16},{56,24},{64,96... | collective-permute-start | bytes 196616 | tf_op jit(solution)/shard_map/ppermute | solution.py:399
  98.0 5.9 %collective-permute-start.7 = (f32[64,256]{1,0:T(8,128)S(1)}, f32[64,256]{1,0:T(8,128)S(1)}, u32[]{:S(2)}, u32[]{:S(2)}) collective-permute-start(f32[64,256]{1,0:T(8,128)S(1)} %get-tuple-element.32), channel_id=1, source_target_pairs={{0,64},{8,72},{16,80},{24,88},{32,96},{40,104},{48,112},{56,120},{... | collective-permute-start | bytes 196616 | tf_op jit(solution)/shard_map/ppermute | solution.py:399
  100.2 4.8 %collective-permute-start.8 = (f32[64,256]{1,0:T(8,128)S(1)}, f32[64,256]{1,0:T(8,128)S(1)}, u32[]{:S(2)}, u32[]{:S(2)}) collective-permute-start(f32[64,256]{1,0:T(8,128)S(1)} %get-tuple-element.33), channel_id=1, source_target_pairs={{0,96},{8,104},{16,112},{24,120},{32,64},{40,72},{48,80},{56,88},{... | collective-permute-start | bytes 196616 | tf_op jit(solution)/shard_map/ppermute | solution.py:399
  114.4 9.5 %all-to-all-start.2 = ((bf16[8,8,256]{2,1,0:T(8,128)(2,1)}), bf16[8,8,256]{2,1,0:T(8,128)(2,1)S(1)}, u32[]{:S(2)}, u32[]{:S(2)}) async-start(bf16[8,8,256]{2,1,0:T(8,128)(2,1)} %fusion), calls=%async_computation.2 | async-start | bytes 65536 | tf_op jit(solution)/shard_map/all_to_all | solution.py:433
